TPU v7x, 512 devices: a whole 4x8x8 slice. The times are simulated.
512 devices in a mesh: seq: 64 (over x, z, core), exp: 8 (over y).
Axes of the slice: x: 4, y: 8, z: 8, core: 2. Of those that a mesh axis runs over, the one named last changes fastest.
Arguments:
- residual: bfloat16 [8, 2048, 2048], P('exp', 'seq'), may hold values from -6 to 6
- queries: bfloat16 [8, 2048, 1024], P('exp', 'seq'), may hold values from -8 to 8
- keys: bfloat16 [8, 2048, 1024], P('exp', 'seq'), may hold values from -6 to 6
- values: bfloat16 [8, 2048, 1024], P('exp', 'seq'), may hold values from -6 to 6
- block_mask: int32 [8, 16, 16], P('exp'), may hold values 0 or 1
- out_weight: bfloat16 [1024, 2048], P(None, 'exp'), may hold values from -0.1875 to 0.1875
- norm_gain: float32 [2048], replicated, may hold values from 0.1 to 1.9
- router: bfloat16 [2048, 64], replicated, may hold values from -0.125 to 0.125
- route_ids: int32 [8, 2048, 2], P('exp', 'seq'), may hold values from 0 to 63, all different within a row; in each aligned block of 32 rows (0 to 31, 32 to 63, ..., all dimensions but the last counted through in order) at most 2 rows name the same one
- w_gate: bfloat16 [64, 2048, 1408], P('seq', None, 'exp'), may hold values from -0.125 to 0.125
- w_up: bfloat16 [64, 2048, 1408], P('seq', None, 'exp'), may hold values from -0.125 to 0.125
- w_down: bfloat16 [64, 1408, 2048], P('seq', 'exp'), may hold values from -0.15625 to 0.15625
Outputs:
- attended: bfloat16 [8, 2048, 1024], P('exp', 'seq')
- mixed: bfloat16 [8, 2048, 2048], P('exp', 'seq')
Inputs may be any that keep to these rules, and one draw needn't show every extreme that they name: `route_ids`: each event names two different experts; among the events of one device block no expert is named more than 2 times, a bound that some block reaches.
All inputs are finite; a program needn't handle non-finite values. No bound on the sum of `block_mask` on one device may be relied on, other than what follows from the above.
Results may differ from a plain program's by a relative error of at most 0.013.
Values may be sent and summed in bfloat16 or wider, within the bound.
No kernel may reach another device: no remote copies, remote signals or barrier semaphores. Data moves between devices by JAX's collectives and lax.ppermute only.
A program may use at most 64 MiB of HBM per device.

v0:
```python
import jax
import jax.numpy as jnp
from jax import lax
from jax.sharding import PartitionSpec as P

HEAD = 128
CAP = 2
BLOCK = 128


def activate(tokens, gate_part, up_part):
    flat = tokens.reshape(-1, tokens.shape[-1])
    gate_p = jnp.dot(flat, gate_part, preferred_element_type=jnp.float32)
    up_p = jnp.dot(flat, up_part, preferred_element_type=jnp.float32)
    active = (jax.nn.silu(gate_p) * up_p).astype(jnp.bfloat16)
    return active.reshape(tokens.shape[:-1] + (gate_part.shape[1],))


def shards(
    residual,
    queries,
    keys,
    values,
    block_mask,
    out_weight,
    norm_gain,
    router,
    route_ids,
    w_gate,
    w_up,
    w_down,
):
    query_rows = queries[0]
    row_count = query_rows.shape[0]
    head_count = query_rows.shape[1] // HEAD
    query_pos = lax.axis_index("seq") * row_count + jnp.arange(row_count, dtype=jnp.int32)
    live = (block_mask[0] > 0) | jnp.eye(block_mask.shape[1], dtype=bool)
    block_ids = jnp.arange(block_mask.shape[1], dtype=jnp.int32)
    query_onehot = (query_pos[:, None] // BLOCK == block_ids[None, :]).astype(jnp.float32)
    query_live = jnp.dot(query_onehot, live.astype(jnp.float32), precision=lax.Precision.HIGHEST)
    query_heads = query_rows.reshape(row_count, head_count, HEAD)
    scale_factor = HEAD ** (-0.5)
    running_max = jnp.full((head_count, row_count), -1e30, jnp.float32)
    key_piece = lax.all_gather(keys, "seq", axis=1, tiled=True)[0]
    value_piece = lax.all_gather(values, "seq", axis=1, tiled=True)[0]
    width = key_piece.shape[0]
    key_pos = jnp.arange(width, dtype=jnp.int32)
    key_onehot = (key_pos[:, None] // BLOCK == block_ids[None, :]).astype(jnp.float32)
    block_ok = jnp.dot(query_live, key_onehot.T, precision=lax.Precision.HIGHEST) > 0.5
    allowed = block_ok & (key_pos[None, :] <= query_pos[:, None])
    key_heads = key_piece.reshape(width, head_count, HEAD)
    value_heads = value_piece.reshape(width, head_count, HEAD)
    scores = (
        jnp.einsum("rhd,nhd->hrn", query_heads, key_heads, preferred_element_type=jnp.float32)
        * scale_factor
    )
    scores = jnp.where(allowed[None], scores, -1e30)
    new_max = jnp.maximum(running_max, jnp.max(scores, axis=-1))
    weights = jnp.where(allowed[None], jnp.exp(scores - new_max[..., None]), 0.0)
    new_sum = jnp.sum(weights, axis=-1)
    update = jnp.einsum(
        "hrn,nhd->hrd",
        weights.astype(jnp.bfloat16),
        value_heads,
        preferred_element_type=jnp.float32,
    )
    attended = (
        (update / new_sum[..., None])
        .transpose(1, 0, 2)
        .reshape(row_count, head_count * HEAD)
        .astype(jnp.bfloat16)
    )
    projected = jnp.dot(
        attended,
        lax.all_gather(out_weight, "exp", axis=1, tiled=True),
        preferred_element_type=jnp.float32,
    ).astype(jnp.bfloat16)
    hidden_one = residual[0].astype(jnp.float32) + projected.astype(jnp.float32)
    meansq = jnp.mean(hidden_one * hidden_one, axis=-1, keepdims=True)
    normed = (hidden_one * lax.rsqrt(meansq + 1e-06) * norm_gain).astype(jnp.bfloat16)
    logits = jnp.dot(normed, router, preferred_element_type=jnp.float32)
    expert_count = router.shape[1]
    chosen_ids = route_ids[0]
    onehot = (chosen_ids[..., None] == jnp.arange(expert_count, dtype=jnp.int32)).astype(
        jnp.float32
    )
    chosen = jnp.sum(logits[:, None, :] * onehot, axis=-1)
    first_gate = jax.nn.sigmoid(chosen[:, 0] - chosen[:, 1])
    gates = jnp.stack([first_gate, 1.0 - first_gate], axis=-1)
    assign_rows = onehot.reshape(2 * row_count, expert_count)
    assign_ids = jnp.arange(2 * row_count, dtype=jnp.int32)
    lower = (assign_ids[:, None] > assign_ids[None, :]).astype(jnp.float32)
    earlier = jnp.dot(lower, assign_rows, precision=lax.Precision.HIGHEST)
    slots = jnp.sum(earlier * assign_rows, axis=-1)
    slot_ids = jnp.arange(CAP, dtype=jnp.float32)
    dispatch = assign_rows[:, :, None] * (slots[:, None, None] == slot_ids[None, None, :]).astype(
        jnp.float32
    )
    dispatch = dispatch.reshape(2 * row_count, expert_count * CAP).astype(jnp.bfloat16)
    event_rows = jnp.repeat(normed, 2, axis=0)
    buffer = jnp.dot(dispatch.T, event_rows, preferred_element_type=jnp.float32).astype(
        jnp.bfloat16
    )
    buffer = buffer.reshape(expert_count, CAP, normed.shape[1])
    gate_part = w_gate[0]
    up_part = w_up[0]
    down_part = w_down[0]
    arrived = lax.all_to_all(buffer, "seq", split_axis=0, concat_axis=0, tiled=True)
    active_all = activate(
        lax.all_gather(arrived[None], "exp", axis=0, tiled=True), gate_part, up_part
    )
    summed = lax.psum_scatter(
        jnp.einsum(
            "gecf,fd->gecd", active_all, down_part, preferred_element_type=jnp.float32
        ).astype(jnp.bfloat16),
        "exp",
        scatter_dimension=0,
        tiled=True,
    ).astype(jnp.float32)[0]
    expert_out = lax.all_to_all(
        summed.astype(jnp.bfloat16), "seq", split_axis=0, concat_axis=0, tiled=True
    )
    picked = jnp.dot(
        dispatch, expert_out.reshape(expert_count * CAP, -1), preferred_element_type=jnp.float32
    )
    picked = picked.reshape(row_count, 2, -1)
    moe = jnp.sum(picked * gates[..., None], axis=1)
    mixed = (hidden_one + moe).astype(jnp.bfloat16)
    return (attended[None], mixed[None])


def solution(mesh):
    placed = (
        P("exp", "seq", None),
        P("exp", "seq", None),
        P("exp", "seq", None),
        P("exp", "seq", None),
        P("exp", None, None),
        P(None, "exp"),
        P(),
        P(),
        P("exp", "seq", None),
        P("seq", None, "exp"),
        P("seq", None, "exp"),
        P("seq", "exp", None),
    )
    return jax.shard_map(
        shards,
        mesh=mesh,
        in_specs=placed,
        out_specs=(P("exp", "seq", None), P("exp", "seq", None)),
        check_vma=False,
    )
```

profile of v0, /device:TPU:1, one launch (start us, length us, event | category | flops | bytes accessed | tf_op | source)
XLA Modules:
  0.0 446.3 jit_solution(6194405348797075031)
XLA Ops:
  7.2 0.0 all-gather.6.cloned.1.call-start
  7.2 0.7 all-gather.6.cloned.1.call-update
  7.9 0.0 all-gather.8.cloned.1.call-start
  8.0 0.7 all-gather.8.cloned.1.call-update
  8.7 0.0 all-gather.10.cloned.1.call-start
  8.7 0.7 all-gather.10.cloned.1.call-update
  9.4 0.0 all-gather.12.cloned.1.call-start
  9.4 0.9 copy.66
  10.3 0.8 copy.54
  11.1 0.1 eq.83
  11.2 0.2 fusion.10
  11.4 0.9 fusion.27
  12.3 0.9 fusion.3
  13.2 89.2 %all-gather.6.cloned.1.call-done = bf16[1,2048,1024]{2,1,0:T(8,128)(2,1)} async-done(((bf16[1,32,1024]{2,1,0:T(8,128)(2,1)}), bf16[1,2048,1024]{2,1,0:T(8,128)(2,1)}) %all-gather.6.cloned.1.call-update) | async-done | bytes 4194320 | tf_op jit(solution)/shard_map/all_gather | solution.py:44
  102.5 6.5 %copy.47 = bf16[1,2048,1024]{1,2,0:T(8,128)(2,1)} copy(bf16[1,2048,1024]{2,1,0:T(8,128)(2,1)} %all-gather.6.cloned.1.call-done) | data formatting | bytes 8388608 | tf_op jit(solution)/shard_map/all_gather | solution.py:44
  108.9 78.7 %all-gather.8.cloned.1.call-done = bf16[1,2048,1024]{2,1,0:T(8,128)(2,1)} async-done(((bf16[1,32,1024]{2,1,0:T(8,128)(2,1)}), bf16[1,2048,1024]{2,1,0:T(8,128)(2,1)}) %all-gather.8.cloned.1.call-update) | async-done | bytes 4194320 | tf_op jit(solution)/shard_map/all_gather | solution.py:45
  187.6 6.5 %copy.50 = bf16[1,2048,1024]{1,2,0:T(8,128)(2,1)} copy(bf16[1,2048,1024]{2,1,0:T(8,128)(2,1)} %all-gather.8.cloned.1.call-done) | data formatting | bytes 8388608 | tf_op jit(solution)/shard_map/all_gather | solution.py:45
  194.1 3.2 fusion.39
  197.4 0.5 fusion.4
  197.9 1.6 fusion.9
  199.5 47.6 %all-gather.10.cloned.1.call-done = bf16[1024,2048]{1,0:T(8,128)(2,1)} async-done(((bf16[1024,256]{1,0:T(8,128)(2,1)}), bf16[1024,2048]{1,0:T(8,128)(2,1)}) %all-gather.10.cloned.1.call-update) | async-done | bytes 4194320 | tf_op jit(solution)/shard_map/all_gather | solution.py:75
  247.1 3.1 multiply_reduce_fusion
  250.2 0.1 multiply_convert_fusion
  250.3 0.1 broadcast_in_dim.30
  250.5 0.1 reshape.202
  250.6 0.3 convolution_convert_fusion.1
  250.9 0.3 reshape.203
  251.2 31.9 %all_to_all.10 = bf16[64,2,2048]{2,1,0:T(2,128)(2,1)} all-to-all(bf16[64,2,2048]{2,1,0:T(2,128)(2,1)S(1)} %reshape.203), channel_id=1, replica_groups=mesh['seq'=64,'exp'=8] {'seq'}, dimensions={0} | all-to-all | bytes 1048576 | tf_op jit(solution)/shard_map/all_to_all | solution.py:108
  283.1 0.0 reduce-scatter.2.cloned.1.call-start
  283.2 51.5 %all-gather.12.cloned.1.call-done = bf16[512,2,2048]{2,1,0:T(2,128)(2,1)} async-done(((bf16[64,2,2048]{2,1,0:T(2,128)(2,1)}), bf16[512,2,2048]{2,1,0:T(2,128)(2,1)}) %all-gather.12.cloned.1.call-update) | async-done | bytes 4194320 | tf_op jit(solution)/shard_map/all_gather | solution.py:110
  334.6 7.3 %reshape.204 = bf16[1024,2048]{1,0:T(8,128)(2,1)} reshape(bf16[512,2,2048]{2,1,0:T(2,128)(2,1)} %all-gather.12.cloned.1.call-done) | data formatting | bytes 8388608 | tf_op jit(solution)/shard_map/reshape | solution.py:12
  341.9 3.9 fusion.17
  345.8 1.6 fusion.6
  347.4 0.2 copy.56
  347.6 0.3 reshape.205
  347.9 3.2 convolution_convert_fusion
  351.1 56.9 %reduce-scatter.2.cloned.1.call-done = bf16[1,64,2,2048]{3,1,2,0:T(8,128)(2,1)} async-done(((bf16[8,64,2,2048]{3,1,2,0:T(8,128)(2,1)}), bf16[1,64,2,2048]{3,1,2,0:T(8,128)(2,1)}) %reduce-scatter.2.cloned.1.call-update) | async-done | bytes 524304 | tf_op jit(solution)/shard_map/reduce_scatter | solution.py:112
  407.9 2.4 copy.58
  410.3 11.0 %all-to-all-start.1 = ((bf16[64,2,2048]{2,1,0:T(2,128)(2,1)}), bf16[64,2,2048]{2,1,0:T(2,128)(2,1)S(1)}, u32[]{:S(2)}, u32[]{:S(2)}) async-start(bf16[64,2,2048]{2,1,0:T(2,128)(2,1)} %copy.58), calls=%async_computation.2 | async-start | bytes 1048576 | tf_op jit(solution)/shard_map/all_to_all | solution.py:120
  421.3 2.2 reshape.212
  423.5 1.1 copy.59
  424.7 0.7 convert_element_type.95
  425.4 0.2 fusion.40
  425.6 0.2 select_reduce_fusion
  425.8 12.8 %all-to-all-done.1 = bf16[64,2,2048]{2,1,0:T(2,128)(2,1)S(1)} async-done(((bf16[64,2,2048]{2,1,0:T(2,128)(2,1)}), bf16[64,2,2048]{2,1,0:T(2,128)(2,1)S(1)}, u32[]{:S(2)}, u32[]{:S(2)}) %all-to-all-start.1) | async-done | bytes 524320 | tf_op jit(solution)/shard_map/all_to_all | solution.py:120
  438.6 0.2 reshape.211
  438.8 0.2 fusion.7
  439.1 0.7 fusion.21
  (31 shorter events, 0.2 us)
Async XLA Ops:
  7.2 340.7 %copy-start = (bf16[1,176,2048]{2,1,0:T(8,128)(2,1)S(1)}, bf16[1,176,2048]{2,1,0:T(8,128)(2,1)}, u32[]{:S(2)}) copy-start(bf16[1,176,2048]{2,1,0:T(8,128)(2,1)} %param.23) | copy-start | bytes 2162692
  7.2 95.3 %all-gather.6.cloned.1.call-start = ((), (), s32[]{:S(2)}) async-start(), calls=%async_computation.3 | async-start | bytes 4259840 | tf_op jit(solution)/shard_map/all_gather | solution.py:44
  7.9 179.7 %all-gather.8.cloned.1.call-start = ((), (), s32[]{:S(2)}) async-start(), calls=%async_computation.4 | async-start | bytes 4259840 | tf_op jit(solution)/shard_map/all_gather | solution.py:45
  8.7 238.4 %all-gather.10.cloned.1.call-start = ((), (), s32[]{:S(2)}) async-start(), calls=%async_computation.5 | async-start | bytes 4718592 | tf_op jit(solution)/shard_map/all_gather | solution.py:75
  9.4 325.2 %all-gather.12.cloned.1.call-start = ((), (), s32[]{:S(2)}) async-start(), calls=%async_computation.7 | async-start | bytes 4718592 | tf_op jit(solution)/shard_map/all_gather | solution.py:110
  194.1 3.8 copy-start.1
  197.4 49.7 %copy-start.4 = (bf16[1,32,2048]{2,1,0:T(8,128)(2,1)S(1)}, bf16[1,32,2048]{2,1,0:T(8,128)(2,1)}, u32[]{:S(2)}) copy-start(bf16[1,32,2048]{2,1,0:T(8,128)(2,1)} %param.12) | copy-start | bytes 393220
  197.9 52.3 %copy-start.5 = (f32[2048]{0:T(1024)S(1)}, f32[2048]{0:T(1024)}, u32[]{:S(2)}) copy-start(f32[2048]{0:T(1024)} %param.18) | copy-start | bytes 24580
  283.1 58.8 %copy-start.7 = (bf16[1,2048,176]{1,2,0:T(8,128)(2,1)S(1)}, bf16[1,2048,176]{1,2,0:T(8,128)(2,1)}, u32[]{:S(2)}) copy-start(bf16[1,2048,176]{1,2,0:T(8,128)(2,1)} %param.21) | copy-start | bytes 2162692
  283.1 124.8 %reduce-scatter.2.cloned.1.call-start = ((), (), s32[]{:S(2)}) async-start(), calls=%async_computation.6 | async-start | bytes 4718592 | tf_op jit(solution)/shard_map/reduce_scatter | solution.py:112
  341.9 3.9 copy-start.2
  341.9 3.9 copy-start.8
  351.1 74.3 %copy-start.3 = (bf16[2048,64]{0,1:T(8,128)(2,1)S(1)}, bf16[2048,64]{0,1:T(8,128)(2,1)}, u32[]{:S(2)}) copy-start(bf16[2048,64]{0,1:T(8,128)(2,1)} %param.19) | copy-start | bytes 786436
  351.1 74.5 %copy-start.6 = (s32[1,32,2]{1,2,0:T(2,128)S(1)}, s32[1,32,2]{1,2,0:T(2,128)}, u32[]{:S(2)}) copy-start(s32[1,32,2]{1,2,0:T(2,128)} %param.20) | copy-start | bytes 772
  410.3 28.3 %all-to-all-start.1 = ((bf16[64,2,2048]{2,1,0:T(2,128)(2,1)}), bf16[64,2,2048]{2,1,0:T(2,128)(2,1)S(1)}, u32[]{:S(2)}, u32[]{:S(2)}) async-start(bf16[64,2,2048]{2,1,0:T(2,128)(2,1)} %copy.58), calls=%async_computation.2 | async-start | bytes 1048576 | tf_op jit(solution)/shard_map/all_to_all | solution.py:120
Sparse Core Ops, SparseCore 0:
  11.4 91.0 all-gather.5
  105.8 81.7 all-gather.7
  189.6 57.3 all-gather.9
  283.2 51.3 all-gather.11
  351.2 56.6 reduce-scatter.1
where the time goes:
time: 447 us; the launch traced here: 446 us
  waiting for transfers between devices  339 us (76%)
  blocking collectives  31.9 us (7%)
  local copies, waits for them, and re-layouts  29.7 us (7%)
  matrix products  19.2 us (4%)
  between operations  14 us (3%)
  starting transfers between devices  11.2 us (3%)
    all_gather x1, waiting for transfers between devices, shards(): key_piece = lax.all_gather(keys, 'seq', axis=1, tiled=True)[0]  89.2 us
    all_gather x1, waiting for transfers between devices, shards(): value_piece = lax.all_gather(values, 'seq', axis=1, tiled=True)[0]  78.7 us
    reduce_scatter x1, waiting for transfers between devices, shards(): lax.psum_scatter(jnp.einsum('gecf,fd->gecd', active_all, down_part, prefe...  56.9 us
    all_gather x1, waiting for transfers between devices, shards(): lax.all_gather(arrived[None], 'exp', axis=0, tiled=True)  51.5 us
    all_gather x1, waiting for transfers between devices, shards(): lax.all_gather(out_weight, 'exp', axis=1, tiled=True)  47.6 us
    all_to_all x1, blocking collectives, shards(): lax.all_to_all(buffer, 'seq', split_axis=0, concat_axis=0, tiled=True)  31.9 us
    all_to_all x1, waiting for transfers between devices, shards(): lax.all_to_all(summed.astype(jnp.bfloat16), 'seq', split_axis=0, concat_a...  12.8 us
    all_to_all x1, starting transfers between devices, shards(): lax.all_to_all(summed.astype(jnp.bfloat16), 'seq', split_axis=0, concat_a...  11 us
  transfers between devices with their start and end apart: 6, of which 6 were waited for; matrix products, arithmetic and copies ran while one was open for 6% of the time, Pallas kernels for 0%

commit v1 on v0

v1 whole, which is shorter than its diff:
```python
import jax
import jax.numpy as jnp
from jax import lax
from jax.experimental import pallas as pl
from jax.experimental.pallas import tpu as pltpu
from jax.sharding import Mesh
from jax.sharding import PartitionSpec as P

HEAD = 128
CAP = 2
BLOCK = 128
TOK = 32
D = 2048
F32 = jnp.float32
BF16 = jnp.bfloat16
VMEM_LIMIT = 48 * 1024 * 1024


def vmem_call(body, out_shape, n_in, smem=()):
    return pl.pallas_call(
        body,
        out_shape=out_shape,
        in_specs=[
            pl.BlockSpec(memory_space=pltpu.SMEM if i in smem else pltpu.VMEM) for i in range(n_in)
        ],
        out_specs=jax.tree.map(lambda _: pl.BlockSpec(memory_space=pltpu.VMEM), out_shape),
        compiler_params=pltpu.CompilerParams(vmem_limit_bytes=VMEM_LIMIT),
    )


def attend_kernel(place_ref, mask_ref, query_ref, kv_ref, out_ref):
    x, c = place_ref[0], place_ref[1]
    n_key = kv_ref.shape[0] * TOK
    keys = kv_ref[:, :TOK].reshape(n_key, HEAD)
    values = kv_ref[:, TOK:].reshape(n_key, HEAD)
    key_row = lax.broadcasted_iota(jnp.int32, (1, n_key), 1)
    key_x, key_c, key_z, key_t = key_row // 512, key_row // 256 % 2, key_row // 32 % 8, key_row % 32
    key_pos = key_x * 512 + key_z * 64 + key_c * 32 + key_t
    block_row = lax.broadcasted_iota(jnp.int32, (16, n_key), 0)
    key_onehot = (block_row == jnp.broadcast_to(key_pos // BLOCK, (16, n_key))).astype(BF16)
    row_i = lax.broadcasted_iota(jnp.int32, (16, 16), 0)
    col_i = lax.broadcasted_iota(jnp.int32, (16, 16), 1)
    live = ((mask_ref[...] > 0) | (row_i == col_i)).astype(BF16)
    seen = jnp.dot(live, key_onehot, preferred_element_type=F32)
    seen_row = lax.broadcasted_iota(jnp.int32, (16, n_key), 0)
    scale = HEAD ** (-0.5)
    for j in range(4):
        mine = jnp.sum(jnp.where(seen_row == x * 4 + j, seen, 0.0), axis=0, keepdims=True)
        rows = query_ref[2 * j : 2 * j + 2, :TOK].reshape(2 * TOK, HEAD)
        row = lax.broadcasted_iota(jnp.int32, (2 * TOK, 1), 0)
        query_pos = x * 512 + (2 * j + row // 32) * 64 + c * 32 + row % 32
        allowed = (jnp.broadcast_to(mine, (2 * TOK, n_key)) > 0.5) & (key_pos <= query_pos)
        scores = lax.dot_general(rows, keys, (((1,), (1,)), ((), ())), preferred_element_type=F32)
        scores = jnp.where(allowed, scores * scale, -1e30)
        top = jnp.max(scores, axis=-1, keepdims=True)
        weights = jnp.exp(scores - top)
        total = jnp.sum(weights, axis=-1, keepdims=True)
        update = jnp.dot(weights.astype(BF16), values, preferred_element_type=F32)
        out_ref[2 * j : 2 * j + 2] = (update / total).astype(BF16).reshape(2, TOK, HEAD)


def project_kernel(
    att_ref, weight_ref, residual_ref, gain_ref, router_ref, ids_ref, spread_ref,
    attended_ref, hidden_ref, gates_ref, buffer_ref,
):
    attended = jnp.concatenate([att_ref[h] for h in range(8)], axis=1)
    attended_ref[...] = attended
    low, high = attended[:, :512], attended[:, 512:]
    pieces = []
    for y in range(8):
        piece = jnp.dot(low, weight_ref[y], preferred_element_type=F32) + jnp.dot(
            high, weight_ref[8 + y], preferred_element_type=F32
        )
        pieces.append(piece.astype(BF16).astype(F32))
    hidden = residual_ref[...].astype(F32) + jnp.concatenate(pieces, axis=1)
    hidden_ref[...] = hidden
    meansq = jnp.mean(hidden * hidden, axis=-1, keepdims=True)
    normed = (hidden * lax.rsqrt(meansq + 1e-06) * gain_ref[...]).astype(BF16)
    logits = jnp.dot(normed, router_ref[...], preferred_element_type=F32)
    expert = lax.broadcasted_iota(jnp.int32, logits.shape, 1)
    first = jnp.sum(jnp.where(expert == ids_ref[:, 0:1], logits, 0.0), axis=-1, keepdims=True)
    second = jnp.sum(jnp.where(expert == ids_ref[:, 1:2], logits, 0.0), axis=-1, keepdims=True)
    gate = jax.nn.sigmoid(first - second)
    gates_ref[...] = jnp.concatenate([gate, 1.0 - gate], axis=1)
    buffer_ref[...] = jnp.dot(spread_ref[...], normed, preferred_element_type=F32).astype(BF16)


def expert_kernel(rows_ref, gate_ref, up_ref, down_ref, out_ref):
    rows = rows_ref[...]
    gate = jnp.dot(rows, gate_ref[...], preferred_element_type=F32)
    up = jnp.dot(rows, up_ref[...], preferred_element_type=F32)
    active = (gate / (1.0 + jnp.exp(-gate)) * up).astype(BF16)
    out_ref[...] = jnp.dot(active, down_ref[...], preferred_element_type=F32).astype(BF16)


def expert_call(rows, gate, up, down):
    step = 256
    whole = lambda a: pl.BlockSpec(a.shape, lambda i: (0, 0))
    return pl.pallas_call(
        expert_kernel,
        grid=(rows.shape[0] // step,),
        in_specs=[pl.BlockSpec((step, D), lambda i: (i, 0)), whole(gate), whole(up), whole(down)],
        out_specs=pl.BlockSpec((step, D), lambda i: (i, 0)),
        out_shape=jax.ShapeDtypeStruct(rows.shape, BF16),
        compiler_params=pltpu.CompilerParams(vmem_limit_bytes=VMEM_LIMIT),
    )(rows, gate, up, down)


def combine_kernel(hidden_ref, gates_ref, first_ref, second_ref, rows_ref, out_ref):
    rows = rows_ref[...]
    first = jnp.dot(first_ref[...], rows, preferred_element_type=F32)
    second = jnp.dot(second_ref[...], rows, preferred_element_type=F32)
    moe = first * gates_ref[:, 0:1] + second * gates_ref[:, 1:2]
    out_ref[...] = (hidden_ref[...] + moe).astype(BF16)


def shards(
    residual,
    queries,
    keys,
    values,
    block_mask,
    out_weight,
    norm_gain,
    router,
    route_ids,
    w_gate,
    w_up,
    w_down,
):
    x, c = lax.axis_index("x"), lax.axis_index("c")
    place = jnp.stack([x, c]).astype(jnp.int32)
    half = lax.dynamic_slice_in_dim(out_weight, c * 512, 512, axis=0)
    weight = lax.all_gather(half, ("c", "y"), axis=0)

    by_head = jnp.stack(
        [a[0].reshape(TOK, 8, HEAD).transpose(1, 0, 2) for a in (queries, keys, values)], axis=1
    ).reshape(8, 3 * TOK, HEAD)
    by_token = lax.all_to_all(by_head, "z", split_axis=0, concat_axis=0, tiled=True)
    kv = jnp.broadcast_to(by_token[None, :, TOK:], (8, 8, 2 * TOK, HEAD))
    kv = lax.all_to_all(kv, ("x", "c"), split_axis=0, concat_axis=0, tiled=True)
    att = vmem_call(attend_kernel, jax.ShapeDtypeStruct((8, TOK, HEAD), BF16), 4, smem=(0,))(
        place, block_mask[0], by_token, kv.reshape(64, 2 * TOK, HEAD)
    )
    att = lax.all_to_all(att, "z", split_axis=0, concat_axis=0, tiled=True)

    ids = route_ids[0]
    expert_count = router.shape[1]
    slot_count = expert_count * CAP
    assigned = ids.reshape(2 * TOK)
    onehot = (assigned[:, None] == jnp.arange(expert_count, dtype=jnp.int32)).astype(F32)
    order = jnp.arange(2 * TOK, dtype=jnp.int32)
    lower = (order[:, None] > order[None, :]).astype(F32)
    earlier = jnp.dot(lower, onehot)
    slots = jnp.sum(earlier * onehot, axis=-1).astype(jnp.int32).reshape(TOK, 2)
    spot = ids * CAP + slots
    spots = jnp.arange(slot_count, dtype=jnp.int32)
    first = (spot[:, 0:1] == spots).astype(BF16)
    second = (spot[:, 1:2] == spots).astype(BF16)
    spread = (first + second).T

    attended, hidden, gates, buffer = vmem_call(
        project_kernel,
        (
            jax.ShapeDtypeStruct((TOK, 8 * HEAD), BF16),
            jax.ShapeDtypeStruct((TOK, D), F32),
            jax.ShapeDtypeStruct((TOK, 2), F32),
            jax.ShapeDtypeStruct((slot_count, D), BF16),
        ),
        7,
    )(att, weight, residual[0], norm_gain[None], router, ids, spread)

    seq = ("x", "z", "c")
    arrived = lax.all_to_all(
        buffer.reshape(expert_count, CAP, D), seq, split_axis=0, concat_axis=0, tiled=True
    )
    rows = lax.all_gather(arrived.reshape(slot_count, D), "y", axis=0, tiled=True)
    parts = expert_call(rows, w_gate[0], w_up[0], w_down[0])
    summed = lax.psum_scatter(parts, "y", scatter_dimension=0, tiled=True)
    returned = lax.all_to_all(
        summed.reshape(expert_count, CAP, D), seq, split_axis=0, concat_axis=0, tiled=True
    )
    mixed = vmem_call(combine_kernel, jax.ShapeDtypeStruct((TOK, D), BF16), 5)(
        hidden, gates, first, second, returned.reshape(slot_count, D)
    )
    return (attended[None], mixed[None])


def solution(mesh):
    mesh = Mesh(mesh.devices.reshape(4, 8, 2, 8), ("x", "z", "c", "y"))
    seq = ("x", "z", "c")
    placed = (
        P("y", seq, None),
        P("y", seq, None),
        P("y", seq, None),
        P("y", seq, None),
        P("y", None, None),
        P(None, "y"),
        P(),
        P(),
        P("y", seq, None),
        P(seq, None, "y"),
        P(seq, None, "y"),
        P(seq, "y", None),
    )
    return jax.shard_map(
        shards,
        mesh=mesh,
        in_specs=placed,
        out_specs=(P("y", seq, None), P("y", seq, None)),
        check_vma=False,
    )
```

time: 447 us -> 254 us (0.57)
  waiting for transfers between devices: 339 us -> 148 us
  matrix products: 19.2 us -> 0.16 us
  local copies, waits for them, and re-layouts: 29.7 us -> 14.8 us
  Pallas kernels: 0 us -> 12.7 us
  blocking collectives: 31.9 us -> 42 us
  starting transfers between devices: 11.2 us -> 21.3 us
    all_gather x4 -> x2, waiting for transfers between devices: 267 us -> 52.3 us  [the longest x1 52.3 us: shards(): lax.all_gather(arrived.reshape(slot_count, D), 'y', axis=0, tiled=True)]
    all_to_all x1 -> x3, waiting for transfers between devices: 12.8 us -> 38.5 us  [the longest x1 17.2 us: shards(): lax.all_to_all(summed.reshape(expert_count, CAP, D), seq, split_axis=0, c...]
    dot_general x12 -> x1, matrix products: 19.2 us -> 0.16 us  [shards(): earlier = jnp.dot(lower, onehot)]
    all_gather x2 -> x0, local copies, waits for them, and re-layouts: 13 us -> none  [the longest x1 6.49 us: shards(): value_piece = lax.all_gather(values, 'seq', axis=1, tiled=True)[0]]
    pallas_call x0 -> x4, Pallas kernels: none -> 12.7 us  [the longest x1 7.24 us: expert_call(): pl.pallas_call(expert_kernel, grid=(rows.shape[0] // step,), in_specs=[pl...]
    all_to_all x1 -> x3, starting transfers between devices: 11 us -> 21.2 us  [the longest x1 11 us: shards(): lax.all_to_all(summed.reshape(expert_count, CAP, D), seq, split_axis=0, c...]
    all_to_all x1 -> x2, blocking collectives: 31.9 us -> 42 us  [the longest x1 22.5 us: shards(): lax.all_to_all(buffer.reshape(expert_count, CAP, D), seq, split_axis=0, c...]
    unnamed x20 -> x29, local copies, waits for them, and re-layouts: 1.67 us -> 8.72 us
  transfers between devices with their start and end apart: 6 -> 6, of which waited for: 6 -> 5; matrix products, arithmetic and copies ran while one was open for 6% -> 3% of each run, Pallas kernels for 0% -> 1%
where the time goes in v1:
time: 254 us; the launch traced here: 253 us
  waiting for transfers between devices  148 us (58%)
  blocking collectives  42 us (17%)
  starting transfers between devices  21.3 us (8%)
  local copies, waits for them, and re-layouts  14.8 us (6%)
  between operations  14 us (6%)
  Pallas kernels  12.7 us (5%)
    reduce_scatter x1, waiting for transfers between devices, shards(): summed = lax.psum_scatter(parts, 'y', scatter_dimension=0, tiled=True)  56.9 us
    all_gather x1, waiting for transfers between devices, shards(): lax.all_gather(arrived.reshape(slot_count, D), 'y', axis=0, tiled=True)  52.3 us
    all_to_all x1, blocking collectives, shards(): lax.all_to_all(buffer.reshape(expert_count, CAP, D), seq, split_axis=0, c...  22.5 us
    all_to_all x1, blocking collectives, shards(): lax.all_to_all(by_head, 'z', split_axis=0, concat_axis=0, tiled=True)  19.5 us
    all_to_all x1, waiting for transfers between devices, shards(): lax.all_to_all(summed.reshape(expert_count, CAP, D), seq, split_axis=0, c...  17.2 us
    all_to_all x1, waiting for transfers between devices, shards(): kv = lax.all_to_all(kv, ('x', 'c'), split_axis=0, concat_axis=0, tiled=True)  14.1 us
    all_to_all x1, starting transfers between devices, shards(): lax.all_to_all(summed.reshape(expert_count, CAP, D), seq, split_axis=0, c...  11 us
    unnamed x29, local copies, waits for them, and re-layouts  8.72 us
  transfers between devices with their start and end apart: 6, of which 5 were waited for; matrix products, arithmetic and copies ran while one was open for 3% of the time, Pallas kernels for 1%

profile of v1, /device:TPU:1, one launch (start us, length us, event | category | flops | bytes accessed | tf_op | source)
XLA Modules:
  0.0 252.9 jit_solution(924532778187971246)
XLA Ops:
  7.2 0.0 copy-start
  7.2 0.0 copy-start.10
  7.2 0.0 copy-start.9
  7.2 0.0 copy-start.6
  7.2 0.0 copy-start.5
  7.2 0.0 all-gather.6.cloned.1.call-start
  7.3 0.9 copy-done
  8.2 0.7 constant_dynamic-slice_fusion
  8.9 0.0 all-gather.6.cloned.1.call-update
  9.0 0.9 copy.33
  9.8 0.9 copy.34
  10.7 0.9 copy.32
  11.6 19.5 %all_to_all.25.query_ref = bf16[8,96,128]{2,1,0:T(8,128)(2,1)S(1)} all-to-all(bf16[8,96,128]{2,1,0:T(8,128)(2,1)S(1)} %bitcast.49), channel_id=1, replica_groups=mesh['x'=4,'z'=8,'c'=2,'y'=8] {'z'}, dimensions={0} | all-to-all | bytes 393216 | tf_op jit(solution)/shard_map/all_to_all | solution.py:139
  31.1 1.3 broadcast_in_dim.8
  32.4 6.9 %all-to-all-start.1 = ((bf16[8,8,64,128]{3,2,1,0:T(8,128)(2,1)}), bf16[8,8,64,128]{3,2,1,0:T(8,128)(2,1)S(1)}, u32[]{:S(2)}, u32[]{:S(2)}) async-start(bf16[8,8,64,128]{3,2,1,0:T(8,128)(2,1)} %broadcast_in_dim.8), calls=%async_computation.1 | async-start | bytes 2097152 | tf_op jit(solution)/shard_map/all_to_all | solution.py:141
  39.3 0.1 copy.26
  39.4 0.1 eq.57
  39.5 0.2 fusion
  39.6 0.1 convert_element_type.20
  39.8 0.1 copy.27
  39.8 0.3 copy.28.router_ref
  40.1 0.1 copy.29.ids_ref
  40.2 0.1 pad_add_fusion.place_ref
  40.3 14.1 %all-to-all-done.1 = bf16[8,8,64,128]{3,2,1,0:T(8,128)(2,1)S(1)} async-done(((bf16[8,8,64,128]{3,2,1,0:T(8,128)(2,1)}), bf16[8,8,64,128]{3,2,1,0:T(8,128)(2,1)S(1)}, u32[]{:S(2)}, u32[]{:S(2)}) %all-to-all-start.1) | async-done | bytes 1048608 | tf_op jit(solution)/shard_map/all_to_all | solution.py:141
  54.4 3.2 %shard_map.131 = bf16[8,32,128]{2,1,0:T(8,128)(2,1)} custom-call(s32[2]{0:T(128)S(1)} %pad_add_fusion.place_ref, s32[16,16]{1,0:T(8,128)S(1)} %bitcast.47, bf16[8,96,128]{2,1,0:T(8,128)(2,1)S(1)} %all_to_all.25.query_ref, bf16[64,64,128]{2,1,0:T(8,128)(2,1)S(1)} %bitcast.42), custom_call_target="tpu_custom_call" | custom-call | tf_op jit(solution)/shard_map/pallas_call | solution.py:142
  57.6 3.4 %all-to-all-start.2 = ((bf16[8,32,128]{2,1,0:T(8,128)(2,1)}), bf16[8,32,128]{2,1,0:T(8,128)(2,1)S(1)}, u32[]{:S(2)}, u32[]{:S(2)}) async-start(bf16[8,32,128]{2,1,0:T(8,128)(2,1)} %shard_map.131), calls=%async_computation.2 | async-start | bytes 131072 | tf_op jit(solution)/shard_map/all_to_all | solution.py:145
  61.0 0.0 all-gather.4.cloned.1.call-start
  61.1 7.2 %all-to-all-done.2.att_ref = bf16[8,32,128]{2,1,0:T(8,128)(2,1)S(1)} async-done(((bf16[8,32,128]{2,1,0:T(8,128)(2,1)}), bf16[8,32,128]{2,1,0:T(8,128)(2,1)S(1)}, u32[]{:S(2)}, u32[]{:S(2)}) %all-to-all-start.2) | async-done | bytes 65568 | tf_op jit(solution)/shard_map/all_to_all | solution.py:145
  68.2 2.2 copy-done.1
  70.4 1.3 shard_map.132
  71.7 0.7 copy-done.3
  72.4 0.3 reshape.29
  72.7 22.5 %all_to_all.26 = bf16[64,2,2048]{2,1,0:T(2,128)(2,1)S(1)} all-to-all(bf16[64,2,2048]{2,1,0:T(2,128)(2,1)S(1)} %reshape.29), channel_id=1, replica_groups=mesh['x'=4,'z'=8,'c'=2,'y'=8] {'x','z','c'}, dimensions={0} | all-to-all | bytes 1048576 | tf_op jit(solution)/shard_map/all_to_all | solution.py:174
  95.3 1.0 reshape.30
  96.3 0.0 all-gather.4.cloned.1.call-update
  96.3 0.0 reduce-scatter.2.cloned.1.call-start
  96.4 0.5 copy.30
  96.9 1.4 copy.31
  98.3 52.3 %all-gather.4.cloned.1.call-done.rows_ref = bf16[1024,2048]{1,0:T(8,128)(2,1)} async-done(((bf16[128,2048]{1,0:T(8,128)(2,1)}), bf16[1024,2048]{1,0:T(8,128)(2,1)}) %all-gather.4.cloned.1.call-update) | async-done | bytes 4194320 | tf_op jit(solution)/shard_map/all_gather | solution.py:177
  150.6 7.2 %shard_map.133 = bf16[1024,2048]{1,0:T(8,128)(2,1)} custom-call(bf16[1024,2048]{1,0:T(8,128)(2,1)} %all-gather.4.cloned.1.call-done.rows_ref, bf16[2048,176]{1,0:T(8,128)(2,1)S(1)} %bitcast.43, bf16[2048,176]{1,0:T(8,128)(2,1)S(1)} %bitcast.44, bf16[176,2048]{1,0:T(8,128)(2,1)S(1)} %bitcast.45), custom_call_target="tpu_custom_call" | custom-call | tf_op jit(solution)/shard_map/pallas_call | solution.py:99
  157.9 0.0 reduce-scatter.2.cloned.1.call-update
  157.9 56.9 %reduce-scatter.2.cloned.1.call-done = bf16[128,2048]{1,0:T(8,128)(2,1)} async-done(((bf16[1024,2048]{1,0:T(8,128)(2,1)}), bf16[128,2048]{1,0:T(8,128)(2,1)}) %reduce-scatter.2.cloned.1.call-update) | async-done | bytes 524304 | tf_op jit(solution)/shard_map/reduce_scatter | solution.py:179
  214.7 2.2 reshape.31
  216.9 11.0 %all-to-all-start.4 = ((bf16[64,2,2048]{2,1,0:T(2,128)(2,1)}), bf16[64,2,2048]{2,1,0:T(2,128)(2,1)S(1)}, u32[]{:S(2)}, u32[]{:S(2)}) async-start(bf16[64,2,2048]{2,1,0:T(2,128)(2,1)} %reshape.31), calls=%async_computation.5 | async-start | bytes 1048576 | tf_op jit(solution)/shard_map/all_to_all | solution.py:180
  227.9 0.1 fusion.5
  228.0 17.2 %all-to-all-done.4 = bf16[64,2,2048]{2,1,0:T(2,128)(2,1)S(1)} async-done(((bf16[64,2,2048]{2,1,0:T(2,128)(2,1)}), bf16[64,2,2048]{2,1,0:T(2,128)(2,1)S(1)}, u32[]{:S(2)}, u32[]{:S(2)}) %all-to-all-start.4) | async-done | bytes 524320 | tf_op jit(solution)/shard_map/all_to_all | solution.py:180
  245.2 0.2 reshape.32.rows_ref
  245.4 0.9 shard_map.134
  (23 shorter events, 0.1 us)
Async XLA Ops:
  7.2 1.0 copy-start
  7.2 32.1 %copy-start.10 = (s32[1,32,2]{1,2,0:T(2,128)S(1)}, s32[1,32,2]{1,2,0:T(2,128)}, u32[]{:S(2)}) copy-start(s32[1,32,2]{1,2,0:T(2,128)} %param.20) | copy-start | bytes 772
  7.2 32.6 %copy-start.9 = (bf16[2048,64]{0,1:T(8,128)(2,1)S(1)}, bf16[2048,64]{0,1:T(8,128)(2,1)}, u32[]{:S(2)}) copy-start(bf16[2048,64]{0,1:T(8,128)(2,1)} %param.19) | copy-start | bytes 786436
  7.2 47.2 %copy-start.6 = (s32[1,16,16]{2,1,0:T(8,128)S(1)}, s32[1,16,16]{2,1,0:T(8,128)}, u32[]{:S(2)}) copy-start(s32[1,16,16]{2,1,0:T(8,128)} %param.16) | copy-start | bytes 3076
  7.2 61.0 %copy-start.5 = (bf16[1,32,2048]{2,1,0:T(8,128)(2,1)S(1)}, bf16[1,32,2048]{2,1,0:T(8,128)(2,1)}, u32[]{:S(2)}) copy-start(bf16[1,32,2048]{2,1,0:T(8,128)(2,1)} %param.12) | copy-start | bytes 393220
  7.2 61.0 %copy-start.7 = (f32[2048]{0:T(1024)S(1)}, f32[2048]{0:T(1024)}, u32[]{:S(2)}) copy-start(f32[2048]{0:T(1024)} %param.18) | copy-start | bytes 24580
  7.2 61.0 %all-gather.6.cloned.1.call-start = ((), (), s32[]{:S(2)}) async-start(), calls=%async_computation.8 | async-start | bytes 4456448 | tf_op jit(solution)/shard_map/all_gather | solution.py:134
  32.4 22.0 %all-to-all-start.1 = ((bf16[8,8,64,128]{3,2,1,0:T(8,128)(2,1)}), bf16[8,8,64,128]{3,2,1,0:T(8,128)(2,1)S(1)}, u32[]{:S(2)}, u32[]{:S(2)}) async-start(bf16[8,8,64,128]{3,2,1,0:T(8,128)(2,1)} %broadcast_in_dim.8), calls=%async_computation.1 | async-start | bytes 2097152 | tf_op jit(solution)/shard_map/all_to_all | solution.py:141
  57.6 10.6 %all-to-all-start.2 = ((bf16[8,32,128]{2,1,0:T(8,128)(2,1)}), bf16[8,32,128]{2,1,0:T(8,128)(2,1)S(1)}, u32[]{:S(2)}, u32[]{:S(2)}) async-start(bf16[8,32,128]{2,1,0:T(8,128)(2,1)} %shard_map.131), calls=%async_computation.2 | async-start | bytes 131072 | tf_op jit(solution)/shard_map/all_to_all | solution.py:145
  61.0 89.6 %all-gather.4.cloned.1.call-start = ((), (), s32[]{:S(2)}) async-start(), calls=%async_computation.6 | async-start | bytes 4718592 | tf_op jit(solution)/shard_map/all_gather | solution.py:177
  68.2 2.2 copy-start.1
  70.4 25.9 %copy-start.8 = (bf16[1,2048,176]{1,2,0:T(8,128)(2,1)S(1)}, bf16[1,2048,176]{1,2,0:T(8,128)(2,1)}, u32[]{:S(2)}) copy-start(bf16[1,2048,176]{1,2,0:T(8,128)(2,1)} %param.21) | copy-start | bytes 2162692
  71.7 0.7 copy-start.3
  72.4 78.2 %copy-start.2 = (bf16[1,176,2048]{2,1,0:T(8,128)(2,1)S(1)}, bf16[1,176,2048]{2,1,0:T(8,128)(2,1)}, u32[]{:S(2)}) copy-start(bf16[1,176,2048]{2,1,0:T(8,128)(2,1)} %param.23) | copy-start | bytes 2162692
  96.3 118.4 %reduce-scatter.2.cloned.1.call-start = ((), (), s32[]{:S(2)}) async-start(), calls=%async_computation.7 | async-start | bytes 4718592 | tf_op jit(solution)/shard_map/reduce_scatter | solution.py:179
  157.9 87.6 %copy-start.4 = (f32[32,2048]{1,0:T(8,128)S(1)}, f32[32,2048]{1,0:T(8,128)}, u32[]{:S(2)}) copy-start(f32[32,2048]{1,0:T(8,128)} %copy-done.3) | copy-start | bytes 786436
  216.9 28.3 %all-to-all-start.4 = ((bf16[64,2,2048]{2,1,0:T(2,128)(2,1)}), bf16[64,2,2048]{2,1,0:T(2,128)(2,1)S(1)}, u32[]{:S(2)}, u32[]{:S(2)}) async-start(bf16[64,2,2048]{2,1,0:T(2,128)(2,1)} %reshape.31), calls=%async_computation.5 | async-start | bytes 1048576 | tf_op jit(solution)/shard_map/all_to_all | solution.py:180
Sparse Core Ops, SparseCore 0:
  10.2 50.4 all-gather.5
  96.4 54.1 all-gather.3
  158.0 56.6 reduce-scatter.1

commit v2 on v1

v2 whole, which is shorter than its diff:
```python
import jax
import jax.numpy as jnp
from jax import lax
from jax.experimental import pallas as pl
from jax.experimental.pallas import tpu as pltpu
from jax.sharding import Mesh
from jax.sharding import PartitionSpec as P

HEAD = 128
CAP = 2
BLOCK = 128
TOK = 32
D = 2048
CHUNK = 256
EXPERTS = 64
F32 = jnp.float32
BF16 = jnp.bfloat16
VMEM_LIMIT = 48 * 1024 * 1024


def vmem_call(body, out_shape, n_in, smem=()):
    return pl.pallas_call(
        body,
        out_shape=out_shape,
        in_specs=[
            pl.BlockSpec(memory_space=pltpu.SMEM if i in smem else pltpu.VMEM) for i in range(n_in)
        ],
        out_specs=jax.tree.map(lambda _: pl.BlockSpec(memory_space=pltpu.VMEM), out_shape),
        compiler_params=pltpu.CompilerParams(vmem_limit_bytes=VMEM_LIMIT),
    )


def slot_spots(ids):
    expert = lax.broadcasted_iota(jnp.int32, (TOK, EXPERTS), 1)
    first = jnp.where(expert == ids[:, 0:1], 1.0, 0.0)
    second = jnp.where(expert == ids[:, 1:2], 1.0, 0.0)
    row = lax.broadcasted_iota(jnp.int32, (TOK, TOK), 0)
    col = lax.broadcasted_iota(jnp.int32, (TOK, TOK), 1)
    lower = jnp.where(row > col, 1.0, 0.0).astype(BF16)
    earlier = jnp.dot(lower, (first + second).astype(BF16), preferred_element_type=F32)
    base = CAP * expert.astype(F32) + earlier
    spot_first = jnp.sum(first * base, axis=-1, keepdims=True)
    spot_second = jnp.sum(second * base, axis=-1, keepdims=True)
    return first, second, spot_first, spot_second


def pack_kernel(place_ref, query_ref, key_ref, value_ref, residual_ref, ids_ref, out_ref):
    z = place_ref[1]
    _, _, spot_first, spot_second = slot_spots(ids_ref[...])
    lane = lax.broadcasted_iota(jnp.int32, (TOK, 8 * TOK), 1)
    token = lax.broadcasted_iota(jnp.int32, (TOK, 8 * TOK), 0)
    here = lane == z * TOK + token
    spread_first = jnp.sum(jnp.where(here, spot_first, 0.0), axis=0, keepdims=True)
    spread_second = jnp.sum(jnp.where(here, spot_second, 0.0), axis=0, keepdims=True)
    row = lax.broadcasted_iota(jnp.int32, (16, HEAD), 0)
    tile = jnp.where(row == 0, spread_first[:, :HEAD], 0.0)
    tile = jnp.where(row == 1, spread_first[:, HEAD:], tile)
    tile = jnp.where(row == 2, spread_second[:, :HEAD], tile)
    tile = jnp.where(row == 3, spread_second[:, HEAD:], tile).astype(BF16)
    for h in range(8):
        cols = slice(h * HEAD, (h + 1) * HEAD)
        out_ref[h, 0:32] = query_ref[:, cols]
        out_ref[h, 32:64] = key_ref[:, cols]
        out_ref[h, 64:96] = value_ref[:, cols]
        out_ref[h, 96:128] = residual_ref[:, h * CHUNK : h * CHUNK + HEAD]
        out_ref[h, 128:160] = residual_ref[:, h * CHUNK + HEAD : (h + 1) * CHUNK]
        out_ref[h, 160:176] = tile


def attend_kernel(place_ref, mask_ref, packed_ref, kv_ref, out_ref):
    x, c = place_ref[0], place_ref[2]
    n_key = kv_ref.shape[0] * TOK
    keys = kv_ref[:, :TOK].reshape(n_key, HEAD)
    values = kv_ref[:, TOK:].reshape(n_key, HEAD)
    key_row = lax.broadcasted_iota(jnp.int32, (1, n_key), 1)
    key_x, key_c, key_z, key_t = key_row // 512, key_row // 256 % 2, key_row // 32 % 8, key_row % 32
    key_pos = key_x * 512 + key_z * 64 + key_c * 32 + key_t
    block_row = lax.broadcasted_iota(jnp.int32, (16, n_key), 0)
    key_onehot = (block_row == jnp.broadcast_to(key_pos // BLOCK, (16, n_key))).astype(BF16)
    row_i = lax.broadcasted_iota(jnp.int32, (16, 16), 0)
    col_i = lax.broadcasted_iota(jnp.int32, (16, 16), 1)
    live = ((mask_ref[...] > 0) | (row_i == col_i)).astype(BF16)
    seen = jnp.dot(live, key_onehot, preferred_element_type=F32)
    seen_row = lax.broadcasted_iota(jnp.int32, (16, n_key), 0)
    scale = HEAD ** (-0.5)
    for j in range(4):
        mine = jnp.sum(jnp.where(seen_row == x * 4 + j, seen, 0.0), axis=0, keepdims=True)
        rows = packed_ref[2 * j : 2 * j + 2, :TOK].reshape(2 * TOK, HEAD)
        row = lax.broadcasted_iota(jnp.int32, (2 * TOK, 1), 0)
        query_pos = x * 512 + (2 * j + row // 32) * 64 + c * 32 + row % 32
        allowed = (jnp.broadcast_to(mine, (2 * TOK, n_key)) > 0.5) & (key_pos <= query_pos)
        scores = lax.dot_general(rows, keys, (((1,), (1,)), ((), ())), preferred_element_type=F32)
        scores = jnp.where(allowed, scores * scale, -1e30)
        top = jnp.max(scores, axis=-1, keepdims=True)
        weights = jnp.exp(scores - top)
        total = jnp.sum(weights, axis=-1, keepdims=True)
        update = jnp.dot(weights.astype(BF16), values, preferred_element_type=F32)
        attended = (update / total).astype(BF16)
        for z in range(8):
            out_ref[z, 2 * j * TOK : 2 * (j + 1) * TOK] = attended


def project_kernel(
    place_ref, att_ref, weight_ref, packed_ref, gain_ref, attended_ref, projected_ref, buffer_ref
):
    z = place_ref[1]
    mine = pl.ds(pl.multiple_of(z * TOK, TOK), TOK)
    attended_ref[...] = jnp.concatenate([att_ref[h, mine] for h in range(8)], axis=1)
    attended = jnp.concatenate([att_ref[h] for h in range(8)], axis=1)
    projected = jnp.dot(attended, weight_ref[...], preferred_element_type=F32).astype(BF16)
    projected_ref[...] = projected.reshape(8, TOK, CHUNK)
    residual = jnp.concatenate(
        [packed_ref[:, 96:128].reshape(8 * TOK, HEAD), packed_ref[:, 128:160].reshape(8 * TOK, HEAD)],
        axis=1,
    )
    hidden = residual.astype(F32) + projected.astype(F32)
    scaled = (hidden * gain_ref[pl.ds(z, 1), :]).astype(BF16)
    spots = jnp.sum(packed_ref[:, 160:176].astype(F32), axis=0)
    spot_first = jnp.concatenate([spots[0:1], spots[1:2]], axis=1)
    spot_second = jnp.concatenate([spots[2:3], spots[3:4]], axis=1)
    row = lax.broadcasted_iota(jnp.int32, (8 * EXPERTS * CAP, 1), 0)
    row_spot = (row // 16 * CAP + row % CAP).astype(F32)
    row_block = row // CAP % 8
    col_block = lax.broadcasted_iota(jnp.int32, (1, 8 * TOK), 1) // TOK
    taken = (spot_first == row_spot) | (spot_second == row_spot)
    spread = jnp.where(taken & (row_block == col_block), 1.0, 0.0).astype(BF16)
    rows = jnp.dot(spread, scaled, preferred_element_type=F32).astype(BF16)
    buffer_ref[...] = rows.reshape(EXPERTS, 16, CHUNK)


def gates_kernel(
    projected_ref, residual_ref, gain_ref, router_ref, ids_ref,
    hidden_ref, gates_ref, first_ref, second_ref,
):
    projected = jnp.concatenate([projected_ref[z] for z in range(8)], axis=1)
    hidden = residual_ref[...].astype(F32) + projected.astype(F32)
    hidden_ref[...] = hidden
    meansq = jnp.mean(hidden * hidden, axis=-1, keepdims=True)
    normed = (hidden * lax.rsqrt(meansq + 1e-06) * gain_ref[...]).astype(BF16)
    logits = jnp.dot(normed, router_ref[...], preferred_element_type=F32)
    first, second, spot_first, spot_second = slot_spots(ids_ref[...])
    logit_first = jnp.sum(first * logits, axis=-1, keepdims=True)
    logit_second = jnp.sum(second * logits, axis=-1, keepdims=True)
    gate = jax.nn.sigmoid(logit_first - logit_second)
    gates_ref[...] = jnp.concatenate([gate, 1.0 - gate], axis=1)
    spot = lax.broadcasted_iota(jnp.int32, (TOK, EXPERTS * CAP), 1).astype(F32)
    first_ref[...] = jnp.where(spot == spot_first, 1.0, 0.0).astype(BF16)
    second_ref[...] = jnp.where(spot == spot_second, 1.0, 0.0).astype(BF16)


def expert_kernel(rows_ref, inverse_ref, gate_ref, up_ref, out_ref):
    count = rows_ref.shape[0] * 128
    gate = up = squares = None
    for z in range(8):
        piece = rows_ref[:, :, z].reshape(count, CHUNK)
        span = slice(z * CHUNK, (z + 1) * CHUNK)
        plain = piece.astype(F32) * inverse_ref[z : z + 1, :]
        gate_z = jnp.dot(piece, gate_ref[span], preferred_element_type=F32)
        up_z = jnp.dot(piece, up_ref[span], preferred_element_type=F32)
        squares_z = plain * plain
        if z == 0:
            gate, up, squares = gate_z, up_z, squares_z
        else:
            gate, up, squares = gate + gate_z, up + up_z, squares + squares_z
    meansq = jnp.sum(squares, axis=-1, keepdims=True) * (1.0 / D)
    factor = lax.rsqrt(meansq + 1e-06)
    gate, up = gate * factor, up * factor
    active = (gate / (1.0 + jnp.exp(-gate)) * up).astype(BF16)
    width = active.shape[1]
    row = lax.broadcasted_iota(jnp.int32, (width, width), 0)
    col = lax.broadcasted_iota(jnp.int32, (width, width), 1)
    same = jnp.where(row == col, 1.0, 0.0).astype(BF16)
    for s in range(rows_ref.shape[0]):
        out_ref[s] = lax.dot_general(
            same,
            active[s * 128 : (s + 1) * 128],
            (((1,), (1,)), ((), ())),
            preferred_element_type=F32,
        ).astype(BF16)


def expert_call(rows, inverse, gate, up):
    step = 2
    width = gate.shape[1]
    whole = lambda a: pl.BlockSpec(a.shape, lambda i: (0, 0))
    return pl.pallas_call(
        expert_kernel,
        grid=(8 // step,),
        in_specs=[
            pl.BlockSpec((step, 4, 8, 2, 16, CHUNK), lambda i: (i, 0, 0, 0, 0, 0)),
            whole(inverse),
            whole(gate),
            whole(up),
        ],
        out_specs=pl.BlockSpec((step, width, 128), lambda i: (i, 0, 0)),
        out_shape=jax.ShapeDtypeStruct((8, width, 128), BF16),
        compiler_params=pltpu.CompilerParams(vmem_limit_bytes=VMEM_LIMIT),
    )(rows, inverse, gate, up)


def down_kernel(active_ref, down_ref, out_ref):
    row = lax.broadcasted_iota(jnp.int32, (128, 128), 0)
    col = lax.broadcasted_iota(jnp.int32, (128, 128), 1)
    source = row // 32 * 32 + row // 2 % 2 * 16 + row // 4 % 8 * 2 + row % 2
    order = jnp.where(col == source, 1.0, 0.0).astype(BF16)
    total = None
    for y in range(8):
        active = lax.dot_general(
            order, active_ref[y], (((1,), (1,)), ((), ())), preferred_element_type=F32
        ).astype(BF16)
        part = jnp.dot(active, down_ref[y], preferred_element_type=F32)
        total = part if y == 0 else total + part
    out_ref[...] = total.astype(BF16)


def down_call(active, down):
    step = 512
    return pl.pallas_call(
        down_kernel,
        grid=(D // step,),
        in_specs=[
            pl.BlockSpec(active.shape, lambda i: (0, 0, 0)),
            pl.BlockSpec((8, down.shape[1], step), lambda i: (0, 0, i)),
        ],
        out_specs=pl.BlockSpec((128, step), lambda i: (0, i)),
        out_shape=jax.ShapeDtypeStruct((128, D), BF16),
        compiler_params=pltpu.CompilerParams(vmem_limit_bytes=VMEM_LIMIT),
    )(active, down)


def combine_kernel(hidden_ref, gates_ref, first_ref, second_ref, rows_ref, out_ref):
    rows = rows_ref[...]
    first = jnp.dot(first_ref[...], rows, preferred_element_type=F32)
    second = jnp.dot(second_ref[...], rows, preferred_element_type=F32)
    moe = first * gates_ref[:, 0:1] + second * gates_ref[:, 1:2]
    out_ref[...] = (hidden_ref[...] + moe).astype(BF16)


def shards(
    residual,
    queries,
    keys,
    values,
    block_mask,
    out_weight,
    norm_gain,
    router,
    route_ids,
    w_gate,
    w_up,
    w_down,
):
    seq = ("x", "z", "c")
    place = jnp.stack([lax.axis_index(a) for a in seq]).astype(jnp.int32)
    ids = route_ids[0]
    shape = lambda *s: jax.ShapeDtypeStruct(s, BF16)
    swap = lambda a, axes: lax.all_to_all(a, axes, split_axis=0, concat_axis=0, tiled=True)

    down = lax.all_gather(w_down[0], "y", axis=0)
    weight = lax.ppermute(
        out_weight, ("z", "y"), [(z * 8 + y, y * 8 + z) for z in range(8) for y in range(8)]
    )

    packed = vmem_call(pack_kernel, shape(8, 176, HEAD), 6, smem=(0,))(
        place, queries[0], keys[0], values[0], residual[0], ids
    )
    packed = swap(packed, "z")
    kv = jnp.broadcast_to(packed[None, :, 32:96], (8, 8, 2 * TOK, HEAD))
    kv = swap(kv, ("x", "c"))
    att = vmem_call(attend_kernel, shape(8, 8 * TOK, HEAD), 4, smem=(0,))(
        place, block_mask[0], packed, kv.reshape(64, 2 * TOK, HEAD)
    )
    att = swap(att, "z")
    attended, projected, buffer = vmem_call(
        project_kernel,
        (shape(TOK, 8 * HEAD), shape(8, TOK, CHUNK), shape(EXPERTS, 16, CHUNK)),
        5,
        smem=(0,),
    )(place, att, weight, packed, norm_gain.reshape(8, CHUNK))

    rows = lax.all_gather(swap(buffer, seq), "y", axis=0)
    projected = swap(projected, "z")
    hidden, gates, first, second = vmem_call(
        gates_kernel,
        (
            jax.ShapeDtypeStruct((TOK, D), F32),
            jax.ShapeDtypeStruct((TOK, 2), F32),
            shape(TOK, EXPERTS * CAP),
            shape(TOK, EXPERTS * CAP),
        ),
        5,
    )(projected, residual[0], norm_gain[None], router, ids)

    active = expert_call(
        rows.reshape(8, 4, 8, 2, 16, CHUNK), (1.0 / norm_gain).reshape(8, CHUNK), w_gate[0], w_up[0]
    )
    out = down_call(swap(active, "y"), down)
    returned = swap(out.reshape(EXPERTS, CAP, D), seq)
    mixed = vmem_call(combine_kernel, shape(TOK, D), 5)(
        hidden, gates, first, second, returned.reshape(EXPERTS * CAP, D)
    )
    return (attended[None], mixed[None])


def solution(mesh):
    mesh = Mesh(mesh.devices.reshape(4, 8, 2, 8), ("x", "z", "c", "y"))
    seq = ("x", "z", "c")
    placed = (
        P("y", seq, None),
        P("y", seq, None),
        P("y", seq, None),
        P("y", seq, None),
        P("y", None, None),
        P(None, "y"),
        P(),
        P(),
        P("y", seq, None),
        P(seq, None, "y"),
        P(seq, None, "y"),
        P(seq, "y", None),
    )
    return jax.shard_map(
        shards,
        mesh=mesh,
        in_specs=placed,
        out_specs=(P("y", seq, None), P("y", seq, None)),
        check_vma=False,
    )
```

time: 254 us -> 329 us (1.30)
  blocking collectives: 42 us -> 89.5 us
  waiting for transfers between devices: 148 us -> 173 us
  Pallas kernels: 12.7 us -> 20.2 us
  local copies, waits for them, and re-layouts: 14.8 us -> 8.71 us
    reduce_scatter x1 -> x0, waiting for transfers between devices: 56.9 us -> none  [shards(): summed = lax.psum_scatter(parts, 'y', scatter_dimension=0, tiled=True)]
    all_gather x2, waiting for transfers between devices: 52.3 us -> 101 us  [the longest x1 54.3 us: shards(): rows = lax.all_gather(swap(buffer, seq), 'y', axis=0)]
    all_to_all x2 -> x4, blocking collectives: 42 us -> 89.5 us  [shards(): lax.all_to_all(a, axes, split_axis=0, concat_axis=0, tiled=True)]
    all_to_all x3, waiting for transfers between devices: 38.5 us -> 71.5 us  [shards(): lax.all_to_all(a, axes, split_axis=0, concat_axis=0, tiled=True)]
    pallas_call x4 -> x7, Pallas kernels: 12.7 us -> 20.2 us  [the longest x1 7.18 us: down_call(): pl.pallas_call(down_kernel, grid=(D // step,), in_specs=[pl.BlockSpec(act...]
    unnamed x29 -> x23, local copies, waits for them, and re-layouts: 8.72 us -> 6.35 us
  transfers between devices with their start and end apart: 6 -> 6, of which waited for: 5 -> 4; matrix products, arithmetic and copies ran while one was open for 3% -> 1% of each run, Pallas kernels for 1% -> 4%
where the time goes in v2:
time: 329 us; the launch traced here: 328 us
  waiting for transfers between devices  173 us (53%)
  blocking collectives  89.5 us (27%)
  starting transfers between devices  22.2 us (7%)
  Pallas kernels  20.2 us (6%)
  between operations  14.2 us (4%)
  local copies, waits for them, and re-layouts  8.71 us (3%)
    all_to_all x4, blocking collectives, shards(): lax.all_to_all(a, axes, split_axis=0, concat_axis=0, tiled=True)  89.5 us
    all_to_all x3, waiting for transfers between devices, shards(): lax.all_to_all(a, axes, split_axis=0, concat_axis=0, tiled=True)  71.5 us
    all_gather x1, waiting for transfers between devices, shards(): rows = lax.all_gather(swap(buffer, seq), 'y', axis=0)  54.3 us
    all_gather x1, waiting for transfers between devices, shards(): down = lax.all_gather(w_down[0], 'y', axis=0)  46.3 us
    all_to_all x3, starting transfers between devices, shards(): lax.all_to_all(a, axes, split_axis=0, concat_axis=0, tiled=True)  21.4 us
    pallas_call x1, Pallas kernels, down_call(): pl.pallas_call(down_kernel, grid=(D // step,), in_specs=[pl.BlockSpec(act...  7.18 us
  transfers between devices with their start and end apart: 6, of which 4 were waited for; matrix products, arithmetic and copies ran while one was open for 1% of the time, Pallas kernels for 4%

profile of v2, /device:TPU:1, one launch (start us, length us, event | category | flops | bytes accessed | tf_op | source)
XLA Modules:
  0.0 327.8 jit_solution(7557701694756582100)
XLA Ops:
  7.2 0.0 copy-start.2
  7.2 0.8 copy.19.ids_ref
  7.9 0.1 pad_add_fusion.place_ref
  8.0 0.0 copy-start
  8.0 0.9 copy-done
  8.9 0.0 copy-start.3
  8.9 0.8 copy-done.3
  9.8 0.8 copy-done.4
  10.6 0.8 copy-done.5
  11.4 0.8 shard_map.131
  12.3 23.6 %all_to_all.35.packed_ref = bf16[8,176,128]{2,1,0:T(8,128)(2,1)S(1)} all-to-all(bf16[8,176,128]{2,1,0:T(8,128)(2,1)S(1)} %shard_map.131), channel_id=1, replica_groups=mesh['x'=4,'z'=8,'c'=2,'y'=8] {'z'}, dimensions={0} | all-to-all | bytes 720896 | tf_op jit(solution)/shard_map/all_to_all | solution.py:257
  35.9 0.2 broadcast_in_dim.15
  36.1 21.2 %all_to_all.36 = bf16[8,8,64,128]{3,2,1,0:T(8,128)(2,1)S(1)} all-to-all(bf16[8,8,64,128]{3,2,1,0:T(8,128)(2,1)S(1)} %broadcast_in_dim.15), channel_id=1, replica_groups=mesh['x'=4,'z'=8,'c'=2,'y'=8] {'x','c'}, dimensions={0} | all-to-all | bytes 2097152 | tf_op jit(solution)/shard_map/all_to_all | solution.py:257
  57.3 0.7 copy-done.6
  58.0 3.5 %shard_map.132 = bf16[8,256,128]{2,1,0:T(8,128)(2,1)} custom-call(s32[3]{0:T(128)S(1)} %pad_add_fusion.place_ref, s32[16,16]{1,0:T(8,128)S(1)} %bitcast.25, bf16[8,176,128]{2,1,0:T(8,128)(2,1)S(1)} %all_to_all.35.packed_ref, bf16[64,64,128]{2,1,0:T(8,128)(2,1)S(1)} %bitcast.18), custom_call_target="tpu_custom_call" | custom-call | tf_op jit(solution)/shard_map/pallas_call | solution.py:270
  61.5 3.5 %all-to-all-start.2 = ((bf16[8,256,128]{2,1,0:T(8,128)(2,1)}), bf16[8,256,128]{2,1,0:T(8,128)(2,1)S(1)}, u32[]{:S(2)}, u32[]{:S(2)}) async-start(bf16[8,256,128]{2,1,0:T(8,128)(2,1)} %shard_map.132), calls=%async_computation.2 | async-start | bytes 1048576 | tf_op jit(solution)/shard_map/all_to_all | solution.py:257
  65.0 0.0 all-gather.6.cloned.1.call-start
  65.0 0.0 copy-done.9
  65.0 0.7 collective-permute-start
  65.7 0.0 copy-done.2
  65.8 0.0 collective-permute-done.weight_ref
  65.8 54.9 %all-to-all-done.2.att_ref = bf16[8,256,128]{2,1,0:T(8,128)(2,1)S(1)} async-done(((bf16[8,256,128]{2,1,0:T(8,128)(2,1)}), bf16[8,256,128]{2,1,0:T(8,128)(2,1)S(1)}, u32[]{:S(2)}, u32[]{:S(2)}) %all-to-all-start.2) | async-done | bytes 524320 | tf_op jit(solution)/shard_map/all_to_all | solution.py:257
  120.7 1.9 shard_map.133
  122.6 27.6 %all_to_all.37 = bf16[64,16,256]{2,1,0:T(8,128)(2,1)} all-to-all(bf16[64,16,256]{2,1,0:T(8,128)(2,1)S(1)} %get-tuple-element.15), channel_id=1, replica_groups=mesh['x'=4,'z'=8,'c'=2,'y'=8] {'x','z','c'}, dimensions={0} | all-to-all | bytes 1048576 | tf_op jit(solution)/shard_map/all_to_all | solution.py:257
  150.2 0.0 all-gather.6.cloned.1.call-update
  150.2 0.0 all-gather.4.cloned.1.call-start
  150.2 0.7 all-gather.4.cloned.1.call-update
  151.0 0.0 copy-done.7
  151.0 0.5 copy.22
  151.5 1.4 copy.23
  152.9 54.3 %all-gather.6.cloned.1.call-done = bf16[512,16,256]{2,1,0:T(8,128)(2,1)} async-done(((bf16[64,16,256]{2,1,0:T(8,128)(2,1)}), bf16[512,16,256]{2,1,0:T(8,128)(2,1)}) %all-gather.6.cloned.1.call-update) | async-done | bytes 4194320 | tf_op jit(solution)/shard_map/all_gather | solution.py:281
  207.2 5.5 %shard_map.135 = bf16[8,176,128]{2,1,0:T(8,128)(2,1)S(1)} custom-call(bf16[8,4,8,2,16,256]{5,4,3,2,1,0:T(8,128)(2,1)} %bitcast.26, f32[8,256]{1,0:T(8,128)S(1)} %reshape.26.inverse_ref, bf16[2048,176]{1,0:T(8,128)(2,1)S(1)} %bitcast.16, bf16[2048,176]{1,0:T(8,128)(2,1)S(1)} %bitcast.17), custom_call_target="tpu_custom_call" | custom-call | tf_op jit(solution)/shard_map/pallas_call | solution.py:186
  212.7 0.0 copy-start.8
  212.7 0.0 copy-start.1
  212.7 17.2 %all_to_all.38.active_ref = bf16[8,176,128]{2,1,0:T(8,128)(2,1)S(1)} all-to-all(bf16[8,176,128]{2,1,0:T(8,128)(2,1)S(1)} %shard_map.135), channel_id=1, replica_groups=mesh['x'=4,'z'=8,'c'=2,'y'=8] {'y'}, dimensions={0} | all-to-all | bytes 720896 | tf_op jit(solution)/shard_map/all_to_all | solution.py:257
  229.9 7.1 %all-to-all-start.3 = ((bf16[8,32,256]{2,1,0:T(8,128)(2,1)}), bf16[8,32,256]{2,1,0:T(8,128)(2,1)S(1)}, u32[]{:S(2)}, u32[]{:S(2)}) async-start(bf16[8,32,256]{2,1,0:T(8,128)(2,1)} %get-tuple-element.10), calls=%async_computation.3 | async-start | bytes 262144 | tf_op jit(solution)/shard_map/all_to_all | solution.py:257
  237.0 46.3 %all-gather.4.cloned.1.call-done.down_ref = bf16[8,176,2048]{2,1,0:T(8,128)(2,1)} async-done(((bf16[1,176,2048]{2,1,0:T(8,128)(2,1)}), bf16[8,176,2048]{2,1,0:T(8,128)(2,1)}) %all-gather.4.cloned.1.call-update) | async-done | bytes 5767184 | tf_op jit(solution)/shard_map/all_gather | solution.py:259
  283.3 7.2 %shard_map.136 = bf16[128,2048]{1,0:T(8,128)(2,1)S(1)} custom-call(bf16[8,176,128]{2,1,0:T(8,128)(2,1)S(1)} %all_to_all.38.active_ref, bf16[8,176,2048]{2,1,0:T(8,128)(2,1)} %all-gather.4.cloned.1.call-done.down_ref), custom_call_target="tpu_custom_call" | custom-call | tf_op jit(solution)/shard_map/pallas_call | solution.py:218
  290.5 1.1 reshape.27
  291.7 0.0 all-to-all-done.3.projected_ref
  291.7 10.8 %all-to-all-start.6 = ((bf16[64,2,2048]{2,1,0:T(2,128)(2,1)}), bf16[64,2,2048]{2,1,0:T(2,128)(2,1)S(1)}, u32[]{:S(2)}, u32[]{:S(2)}) async-start(bf16[64,2,2048]{2,1,0:T(2,128)(2,1)} %reshape.27), calls=%async_computation.6 | async-start | bytes 1048576 | tf_op jit(solution)/shard_map/all_to_all | solution.py:257
  302.5 0.0 copy-done.8
  302.5 0.3 copy.20.router_ref
  302.8 0.0 copy-done.1
  302.8 0.4 shard_map.134
  303.2 16.6 %all-to-all-done.6 = bf16[64,2,2048]{2,1,0:T(2,128)(2,1)S(1)} async-done(((bf16[64,2,2048]{2,1,0:T(2,128)(2,1)}), bf16[64,2,2048]{2,1,0:T(2,128)(2,1)S(1)}, u32[]{:S(2)}, u32[]{:S(2)}) %all-to-all-start.6) | async-done | bytes 524320 | tf_op jit(solution)/shard_map/all_to_all | solution.py:257
  319.8 0.2 reshape.28.rows_ref
  320.0 0.9 shard_map.137
  (9 shorter events, 0.0 us)
Async XLA Ops:
  7.2 58.6 %copy-start.2 = (f32[2048]{0:T(1024)S(1)}, f32[2048]{0:T(1024)}, u32[]{:S(2)}) copy-start(f32[2048]{0:T(1024)} %param.18) | copy-start | bytes 24580
  8.0 0.9 copy-start
  8.9 0.8 copy-start.3
  9.8 0.8 copy-start.4
  10.6 0.8 copy-start.5
  11.4 53.6 %copy-start.9 = (bf16[1024,256]{1,0:T(8,128)(2,1)S(1)}, bf16[1024,256]{1,0:T(8,128)(2,1)}, u32[]{:S(2)}) copy-start(bf16[1024,256]{1,0:T(8,128)(2,1)} %param.17) | copy-start | bytes 1572868
  11.4 139.5 %copy-start.7 = (bf16[1,2048,176]{1,2,0:T(8,128)(2,1)S(1)}, bf16[1,2048,176]{1,2,0:T(8,128)(2,1)}, u32[]{:S(2)}) copy-start(bf16[1,2048,176]{1,2,0:T(8,128)(2,1)} %param.21) | copy-start | bytes 2162692
  57.3 0.7 copy-start.6
  61.5 59.2 %all-to-all-start.2 = ((bf16[8,256,128]{2,1,0:T(8,128)(2,1)}), bf16[8,256,128]{2,1,0:T(8,128)(2,1)S(1)}, u32[]{:S(2)}, u32[]{:S(2)}) async-start(bf16[8,256,128]{2,1,0:T(8,128)(2,1)} %shard_map.132), calls=%async_computation.2 | async-start | bytes 1048576 | tf_op jit(solution)/shard_map/all_to_all | solution.py:257
  65.0 142.2 %all-gather.6.cloned.1.call-start = ((), (), s32[]{:S(2)}) async-start(), calls=%async_computation.8 | async-start | bytes 4718592 | tf_op jit(solution)/shard_map/all_gather | solution.py:281
  65.0 0.7 collective-permute-start
  150.2 133.1 %all-gather.4.cloned.1.call-start = ((), (), s32[]{:S(2)}) async-start(), calls=%async_computation.7 | async-start | bytes 6488064 | tf_op jit(solution)/shard_map/all_gather | solution.py:259
  212.7 89.8 %copy-start.8 = (bf16[2048,64]{0,1:T(8,128)(2,1)S(1)}, bf16[2048,64]{0,1:T(8,128)(2,1)}, u32[]{:S(2)}) copy-start(bf16[2048,64]{0,1:T(8,128)(2,1)} %param.19) | copy-start | bytes 786436
  212.7 90.1 %copy-start.1 = (bf16[1,32,2048]{2,1,0:T(8,128)(2,1)S(1)}, bf16[1,32,2048]{2,1,0:T(8,128)(2,1)}, u32[]{:S(2)}) copy-start(bf16[1,32,2048]{2,1,0:T(8,128)(2,1)} %param.12) | copy-start | bytes 393220
  229.9 61.8 %all-to-all-start.3 = ((bf16[8,32,256]{2,1,0:T(8,128)(2,1)}), bf16[8,32,256]{2,1,0:T(8,128)(2,1)S(1)}, u32[]{:S(2)}, u32[]{:S(2)}) async-start(bf16[8,32,256]{2,1,0:T(8,128)(2,1)} %get-tuple-element.10), calls=%async_computation.3 | async-start | bytes 262144 | tf_op jit(solution)/shard_map/all_to_all | solution.py:257
  291.7 28.1 %all-to-all-start.6 = ((bf16[64,2,2048]{2,1,0:T(2,128)(2,1)}), bf16[64,2,2048]{2,1,0:T(2,128)(2,1)S(1)}, u32[]{:S(2)}, u32[]{:S(2)}) async-start(bf16[64,2,2048]{2,1,0:T(2,128)(2,1)} %reshape.27), calls=%async_computation.6 | async-start | bytes 1048576 | tf_op jit(solution)/shard_map/all_to_all | solution.py:257
Sparse Core Ops, SparseCore 0:
  150.3 56.8 all-gather.5
  209.3 74.0 all-gather.3

commit v3 on v2

--- a/solution.py
+++ b/solution.py
@@ -18,15 +18,15 @@
 VMEM_LIMIT = 48 * 1024 * 1024
 
 
-def vmem_call(body, out_shape, n_in, smem=()):
+def vmem_call(body, out_shape, n_in, smem=(), hbm=(), scratch=(), limit=VMEM_LIMIT):
+    space = lambda i: pltpu.SMEM if i in smem else pl.ANY if i in hbm else pltpu.VMEM
     return pl.pallas_call(
         body,
         out_shape=out_shape,
-        in_specs=[
-            pl.BlockSpec(memory_space=pltpu.SMEM if i in smem else pltpu.VMEM) for i in range(n_in)
-        ],
+        in_specs=[pl.BlockSpec(memory_space=space(i)) for i in range(n_in)],
         out_specs=jax.tree.map(lambda _: pl.BlockSpec(memory_space=pltpu.VMEM), out_shape),
-        compiler_params=pltpu.CompilerParams(vmem_limit_bytes=VMEM_LIMIT),
+        scratch_shapes=list(scratch),
+        compiler_params=pltpu.CompilerParams(vmem_limit_bytes=limit),
     )
 
 
@@ -44,30 +44,64 @@
     return first, second, spot_first, spot_second
 
 
-def pack_kernel(place_ref, query_ref, key_ref, value_ref, residual_ref, ids_ref, out_ref):
-    z = place_ref[1]
-    _, _, spot_first, spot_second = slot_spots(ids_ref[...])
-    lane = lax.broadcasted_iota(jnp.int32, (TOK, 8 * TOK), 1)
-    token = lax.broadcasted_iota(jnp.int32, (TOK, 8 * TOK), 0)
-    here = lane == z * TOK + token
-    spread_first = jnp.sum(jnp.where(here, spot_first, 0.0), axis=0, keepdims=True)
-    spread_second = jnp.sum(jnp.where(here, spot_second, 0.0), axis=0, keepdims=True)
+def chunk_of(z, y):
+    return lax.rem(z - y + 8, 8)
+
+
+def holder_of(chunk, y):
+    return lax.rem(chunk + y, 8)
+
+
+def pack_kernel(
+    place_ref, query_hbm, key_hbm, value_hbm, residual_hbm, ids_hbm, out_ref,
+    query_ref, key_ref, value_ref, residual_ref, ids_ref, sems,
+):
+    pairs = (
+        (ids_hbm, ids_ref), (query_hbm, query_ref), (key_hbm, key_ref), (value_hbm, value_ref),
+        (residual_hbm, residual_ref),
+    )
+    copies = [pltpu.make_async_copy(a, b, sems.at[i]) for i, (a, b) in enumerate(pairs)]
+    for copy in copies:
+        copy.start()
+    z, y = place_ref[1], place_ref[3]
+    copies[0].wait()
+    expert = lax.broadcasted_iota(jnp.int32, (EXPERTS, TOK), 0)
+    first = jnp.where(expert == ids_ref[0:1], 1.0, 0.0)
+    second = jnp.where(expert == ids_ref[1:2], 1.0, 0.0)
+    row = lax.broadcasted_iota(jnp.int32, (TOK, TOK), 0)
+    col = lax.broadcasted_iota(jnp.int32, (TOK, TOK), 1)
+    upper = jnp.where(row < col, 1.0, 0.0).astype(BF16)
+    earlier = jnp.dot((first + second).astype(BF16), upper, preferred_element_type=F32)
+    base = CAP * expert.astype(F32) + earlier
+    spot_first = jnp.sum(first * base, axis=0, keepdims=True)
+    spot_second = jnp.sum(second * base, axis=0, keepdims=True)
+    row = lax.broadcasted_iota(jnp.int32, (16, TOK), 0)
+    tile = jnp.where(row < 2, spot_first, jnp.where(row < 4, spot_second, 0.0)).astype(BF16)
+    lane = lax.broadcasted_iota(jnp.int32, (TOK, 2 * HEAD), 1)
+    token = lax.broadcasted_iota(jnp.int32, (TOK, 2 * HEAD), 0)
+    here = jnp.where(lane == z * TOK + token, 1.0, 0.0).astype(BF16)
+    tile = jnp.dot(tile, here, preferred_element_type=F32)
     row = lax.broadcasted_iota(jnp.int32, (16, HEAD), 0)
-    tile = jnp.where(row == 0, spread_first[:, :HEAD], 0.0)
-    tile = jnp.where(row == 1, spread_first[:, HEAD:], tile)
-    tile = jnp.where(row == 2, spread_second[:, :HEAD], tile)
-    tile = jnp.where(row == 3, spread_second[:, HEAD:], tile).astype(BF16)
+    tile = jnp.where(row % 2 == 0, tile[:, :HEAD], tile[:, HEAD:]).astype(BF16)
+    for copy in copies[1:]:
+        copy.wait()
     for h in range(8):
         cols = slice(h * HEAD, (h + 1) * HEAD)
         out_ref[h, 0:32] = query_ref[:, cols]
         out_ref[h, 32:64] = key_ref[:, cols]
         out_ref[h, 64:96] = value_ref[:, cols]
-        out_ref[h, 96:128] = residual_ref[:, h * CHUNK : h * CHUNK + HEAD]
-        out_ref[h, 128:160] = residual_ref[:, h * CHUNK + HEAD : (h + 1) * CHUNK]
         out_ref[h, 160:176] = tile
-
-
-def attend_kernel(place_ref, mask_ref, packed_ref, kv_ref, out_ref):
+        holder = holder_of(h, y)
+        out_ref[holder, 96:128] = residual_ref[:, h * CHUNK : h * CHUNK + HEAD]
+        out_ref[holder, 128:160] = residual_ref[:, h * CHUNK + HEAD : (h + 1) * CHUNK]
+
+
+def spread_kernel(packed_ref, out_ref):
+    for i in range(8):
+        out_ref[i] = packed_ref[:, 32:96]
+
+
+def attend_kernel(place_ref, mask_ref, packed_ref, kv_ref, _, out_ref):
     x, c = place_ref[0], place_ref[2]
     n_key = kv_ref.shape[0] * TOK
     keys = kv_ref[:, :TOK].reshape(n_key, HEAD)
@@ -101,20 +135,26 @@
 
 
 def project_kernel(
-    place_ref, att_ref, weight_ref, packed_ref, gain_ref, attended_ref, projected_ref, buffer_ref
+    place_ref, att_ref, own_ref, core_ref, x_ref, x_core_ref, packed_ref, gain_ref, attended_ref, projected_ref, buffer_ref
 ):
-    z = place_ref[1]
+    z, y = place_ref[1], place_ref[3]
     mine = pl.ds(pl.multiple_of(z * TOK, TOK), TOK)
     attended_ref[...] = jnp.concatenate([att_ref[h, mine] for h in range(8)], axis=1)
-    attended = jnp.concatenate([att_ref[h] for h in range(8)], axis=1)
-    projected = jnp.dot(attended, weight_ref[...], preferred_element_type=F32).astype(BF16)
+    quarter = place_ref[0] % 2 * 2 + place_ref[2]
+    total = None
+    for ref, flip in ((own_ref, 0), (core_ref, 1), (x_ref, 2), (x_core_ref, 3)):
+        rows = quarter ^ flip
+        attended = jnp.concatenate([att_ref[2 * rows], att_ref[2 * rows + 1]], axis=1)
+        part = jnp.dot(attended, ref[...], preferred_element_type=F32)
+        total = part if total is None else total + part
+    projected = total.astype(BF16)
     projected_ref[...] = projected.reshape(8, TOK, CHUNK)
     residual = jnp.concatenate(
         [packed_ref[:, 96:128].reshape(8 * TOK, HEAD), packed_ref[:, 128:160].reshape(8 * TOK, HEAD)],
         axis=1,
     )
     hidden = residual.astype(F32) + projected.astype(F32)
-    scaled = (hidden * gain_ref[pl.ds(z, 1), :]).astype(BF16)
+    scaled = (hidden * gain_ref[pl.ds(chunk_of(z, y), 1), :]).astype(BF16)
     spots = jnp.sum(packed_ref[:, 160:176].astype(F32), axis=0)
     spot_first = jnp.concatenate([spots[0:1], spots[1:2]], axis=1)
     spot_second = jnp.concatenate([spots[2:3], spots[3:4]], axis=1)
@@ -129,10 +169,11 @@
 
 
 def gates_kernel(
-    projected_ref, residual_ref, gain_ref, router_ref, ids_ref,
+    place_ref, projected_ref, residual_ref, gain_ref, router_ref, ids_ref,
     hidden_ref, gates_ref, first_ref, second_ref,
 ):
-    projected = jnp.concatenate([projected_ref[z] for z in range(8)], axis=1)
+    y = place_ref[3]
+    projected = jnp.concatenate([projected_ref[holder_of(k, y)] for k in range(8)], axis=1)
     hidden = residual_ref[...].astype(F32) + projected.astype(F32)
     hidden_ref[...] = hidden
     meansq = jnp.mean(hidden * hidden, axis=-1, keepdims=True)
@@ -148,20 +189,27 @@
     second_ref[...] = jnp.where(spot == spot_second, 1.0, 0.0).astype(BF16)
 
 
-def expert_kernel(rows_ref, inverse_ref, gate_ref, up_ref, out_ref):
-    count = rows_ref.shape[0] * 128
+def expert_kernel(rows_ref, inverse_ref, gate_ref, up_ref, _, out_ref):
+    streams = rows_ref.shape[0]
+    first_stream = pl.program_id(0) * streams
     gate = up = squares = None
-    for z in range(8):
-        piece = rows_ref[:, :, z].reshape(count, CHUNK)
-        span = slice(z * CHUNK, (z + 1) * CHUNK)
-        plain = piece.astype(F32) * inverse_ref[z : z + 1, :]
-        gate_z = jnp.dot(piece, gate_ref[span], preferred_element_type=F32)
-        up_z = jnp.dot(piece, up_ref[span], preferred_element_type=F32)
-        squares_z = plain * plain
-        if z == 0:
-            gate, up, squares = gate_z, up_z, squares_z
+    for k in range(8):
+        piece = jnp.concatenate(
+            [
+                rows_ref[s, :, holder_of(k, first_stream + s)].reshape(128, CHUNK)
+                for s in range(streams)
+            ],
+            axis=0,
+        )
+        span = slice(k * CHUNK, (k + 1) * CHUNK)
+        plain = piece.astype(F32) * inverse_ref[k : k + 1, :]
+        gate_k = jnp.dot(piece, gate_ref[span], preferred_element_type=F32)
+        up_k = jnp.dot(piece, up_ref[span], preferred_element_type=F32)
+        squares_k = plain * plain
+        if k == 0:
+            gate, up, squares = gate_k, up_k, squares_k
         else:
-            gate, up, squares = gate + gate_z, up + up_z, squares + squares_z
+            gate, up, squares = gate + gate_k, up + up_k, squares + squares_k
     meansq = jnp.sum(squares, axis=-1, keepdims=True) * (1.0 / D)
     factor = lax.rsqrt(meansq + 1e-06)
     gate, up = gate * factor, up * factor
@@ -179,23 +227,24 @@
         ).astype(BF16)
 
 
-def expert_call(rows, inverse, gate, up):
+def expert_call(rows, inverse, gate, up, after):
     step = 2
     width = gate.shape[1]
-    whole = lambda a: pl.BlockSpec(a.shape, lambda i: (0, 0))
+    whole = pl.BlockSpec(memory_space=pltpu.VMEM)
     return pl.pallas_call(
         expert_kernel,
         grid=(8 // step,),
         in_specs=[
             pl.BlockSpec((step, 4, 8, 2, 16, CHUNK), lambda i: (i, 0, 0, 0, 0, 0)),
-            whole(inverse),
-            whole(gate),
-            whole(up),
+            whole,
+            whole,
+            whole,
+            pl.BlockSpec(memory_space=pl.ANY),
         ],
         out_specs=pl.BlockSpec((step, width, 128), lambda i: (i, 0, 0)),
         out_shape=jax.ShapeDtypeStruct((8, width, 128), BF16),
         compiler_params=pltpu.CompilerParams(vmem_limit_bytes=VMEM_LIMIT),
-    )(rows, inverse, gate, up)
+    )(rows, inverse, gate, up, after)
 
 
 def down_kernel(active_ref, down_ref, out_ref):
@@ -203,29 +252,17 @@
     col = lax.broadcasted_iota(jnp.int32, (128, 128), 1)
     source = row // 32 * 32 + row // 2 % 2 * 16 + row // 4 % 8 * 2 + row % 2
     order = jnp.where(col == source, 1.0, 0.0).astype(BF16)
-    total = None
-    for y in range(8):
-        active = lax.dot_general(
-            order, active_ref[y], (((1,), (1,)), ((), ())), preferred_element_type=F32
-        ).astype(BF16)
-        part = jnp.dot(active, down_ref[y], preferred_element_type=F32)
-        total = part if y == 0 else total + part
-    out_ref[...] = total.astype(BF16)
-
-
-def down_call(active, down):
-    step = 512
-    return pl.pallas_call(
-        down_kernel,
-        grid=(D // step,),
-        in_specs=[
-            pl.BlockSpec(active.shape, lambda i: (0, 0, 0)),
-            pl.BlockSpec((8, down.shape[1], step), lambda i: (0, 0, i)),
-        ],
-        out_specs=pl.BlockSpec((128, step), lambda i: (0, i)),
-        out_shape=jax.ShapeDtypeStruct((128, D), BF16),
-        compiler_params=pltpu.CompilerParams(vmem_limit_bytes=VMEM_LIMIT),
-    )(active, down)
+    hidden = active_ref.shape[0] * active_ref.shape[1]
+    active = lax.dot_general(
+        order,
+        active_ref[...].reshape(hidden, 128),
+        (((1,), (1,)), ((), ())),
+        preferred_element_type=F32,
+    ).astype(BF16)
+    for k in range(4):
+        cols = slice(k * 512, (k + 1) * 512)
+        down = down_ref[:, :, cols].reshape(hidden, 512)
+        out_ref[:, cols] = jnp.dot(active, down, preferred_element_type=F32).astype(BF16)
 
 
 def combine_kernel(hidden_ref, gates_ref, first_ref, second_ref, rows_ref, out_ref):
@@ -251,34 +288,54 @@
     w_down,
 ):
     seq = ("x", "z", "c")
-    place = jnp.stack([lax.axis_index(a) for a in seq]).astype(jnp.int32)
+    place = jnp.stack([lax.axis_index(a) for a in ("x", "z", "c", "y")]).astype(jnp.int32)
     ids = route_ids[0]
     shape = lambda *s: jax.ShapeDtypeStruct(s, BF16)
     swap = lambda a, axes: lax.all_to_all(a, axes, split_axis=0, concat_axis=0, tiled=True)
 
     down = lax.all_gather(w_down[0], "y", axis=0)
+    share = out_weight.shape[0] // 4
+    quarter = lax.axis_index("x") % 2 * 2 + lax.axis_index("c")
+    weight = lax.dynamic_slice_in_dim(out_weight, quarter * share, share, axis=0)
     weight = lax.ppermute(
-        out_weight, ("z", "y"), [(z * 8 + y, y * 8 + z) for z in range(8) for y in range(8)]
-    )
-
-    packed = vmem_call(pack_kernel, shape(8, 176, HEAD), 6, smem=(0,))(
-        place, queries[0], keys[0], values[0], residual[0], ids
-    )
+        weight, ("z", "y"), [(z * 8 + y, z * 8 + (z - y) % 8) for z in range(8) for y in range(8)]
+    )
+
+    packed = vmem_call(
+        pack_kernel,
+        shape(8, 176, HEAD),
+        6,
+        smem=(0,),
+        hbm=(1, 2, 3, 4, 5),
+        scratch=(
+            *(pltpu.VMEM((TOK, 8 * HEAD), BF16) for _ in range(3)),
+            pltpu.VMEM((TOK, D), BF16),
+            pltpu.VMEM((2, TOK), jnp.int32),
+            pltpu.SemaphoreType.DMA((5,)),
+        ),
+        limit=60 * 1024 * 1024,
+    )(place, queries[0], keys[0], values[0], residual[0], ids.T)
     packed = swap(packed, "z")
-    kv = jnp.broadcast_to(packed[None, :, 32:96], (8, 8, 2 * TOK, HEAD))
+    kv = vmem_call(spread_kernel, shape(8, 8, 2 * TOK, HEAD), 1)(packed)
     kv = swap(kv, ("x", "c"))
-    att = vmem_call(attend_kernel, shape(8, 8 * TOK, HEAD), 4, smem=(0,))(
-        place, block_mask[0], packed, kv.reshape(64, 2 * TOK, HEAD)
+    att = vmem_call(attend_kernel, shape(8, 8 * TOK, HEAD), 5, smem=(0,), hbm=(4,))(
+        place, block_mask[0], packed, kv.reshape(64, 2 * TOK, HEAD), weight
+    )
+    other_core = [(0, 1), (1, 0)]
+    beside = lax.ppermute(weight, "x", [(0, 1), (1, 0), (2, 3), (3, 2)])
+    weights = (
+        weight, lax.ppermute(weight, "c", other_core), beside, lax.ppermute(beside, "c", other_core)
     )
     att = swap(att, "z")
     attended, projected, buffer = vmem_call(
         project_kernel,
         (shape(TOK, 8 * HEAD), shape(8, TOK, CHUNK), shape(EXPERTS, 16, CHUNK)),
-        5,
+        8,
         smem=(0,),
-    )(place, att, weight, packed, norm_gain.reshape(8, CHUNK))
-
-    rows = lax.all_gather(swap(buffer, seq), "y", axis=0)
+    )(place, att, *weights, packed, norm_gain.reshape(8, CHUNK))
+
+    arrived = swap(buffer, seq) + down[0, 0, 0] * 0
+    rows = lax.all_gather(arrived, "y", axis=0)
     projected = swap(projected, "z")
     hidden, gates, first, second = vmem_call(
         gates_kernel,
@@ -288,13 +345,18 @@
             shape(TOK, EXPERTS * CAP),
             shape(TOK, EXPERTS * CAP),
         ),
-        5,
-    )(projected, residual[0], norm_gain[None], router, ids)
+        6,
+        smem=(0,),
+    )(place, projected, residual[0], norm_gain[None], router, ids)
 
     active = expert_call(
-        rows.reshape(8, 4, 8, 2, 16, CHUNK), (1.0 / norm_gain).reshape(8, CHUNK), w_gate[0], w_up[0]
-    )
-    out = down_call(swap(active, "y"), down)
+        rows.reshape(8, 4, 8, 2, 16, CHUNK),
+        (1.0 / norm_gain).reshape(8, CHUNK),
+        w_gate[0],
+        w_up[0],
+        gates,
+    )
+    out = vmem_call(down_kernel, shape(128, D), 2)(swap(active, "y"), down)
     returned = swap(out.reshape(EXPERTS, CAP, D), seq)
     mixed = vmem_call(combine_kernel, shape(TOK, D), 5)(
         hidden, gates, first, second, returned.reshape(EXPERTS * CAP, D)

time: 329 us -> 227 us (0.69)
  waiting for transfers between devices: 173 us -> 84.8 us
  blocking collectives: 89.5 us -> 70.3 us
  starting transfers between devices: 22.2 us -> 28 us
    all_gather x1, waiting for transfers between devices: 46.3 us -> 3.34 us  [shards(): down = lax.all_gather(w_down[0], 'y', axis=0)]
    all_to_all x3 -> x4, waiting for transfers between devices: 71.5 us -> 38.3 us  [shards(): lax.all_to_all(a, axes, split_axis=0, concat_axis=0, tiled=True)]
    all_to_all x4 -> x3, blocking collectives: 89.5 us -> 70.3 us  [shards(): lax.all_to_all(a, axes, split_axis=0, concat_axis=0, tiled=True)]
    all_gather x1, waiting for transfers between devices: 54.3 us -> 40.7 us  [shards(): rows = lax.all_gather(arrived, 'y', axis=0)]
    ppermute x1 -> x4, starting transfers between devices: 0.69 us -> 9.49 us  [the longest x1 3.57 us: shards(): lax.ppermute(beside, 'c', other_core)]
    all_to_all x3 -> x4, starting transfers between devices: 21.4 us -> 18.4 us  [shards(): lax.all_to_all(a, axes, split_axis=0, concat_axis=0, tiled=True)]
    pallas_call x3 -> x4, Pallas kernels: 11.5 us -> 11 us  [the longest x1 3.73 us: shards(): out = vmem_call(down_kernel, shape(128, D), 2)(swap(active, 'y'), down)]
  transfers between devices with their start and end apart: 6 -> 10, of which waited for: 4 -> 8; matrix products, arithmetic and copies ran while one was open for 1% -> 2% of each run, Pallas kernels for 4% -> 5%
where the time goes in v3:
time: 227 us; the launch traced here: 226 us
  waiting for transfers between devices  84.8 us (37%)
  blocking collectives  70.3 us (31%)
  starting transfers between devices  28 us (12%)
  Pallas kernels  20.6 us (9%)
  between operations  14.9 us (7%)
  local copies, waits for them, and re-layouts  6.35 us (3%)
    all_to_all x3, blocking collectives, shards(): lax.all_to_all(a, axes, split_axis=0, concat_axis=0, tiled=True)  70.3 us
    all_gather x1, waiting for transfers between devices, shards(): rows = lax.all_gather(arrived, 'y', axis=0)  40.7 us
    all_to_all x4, waiting for transfers between devices, shards(): lax.all_to_all(a, axes, split_axis=0, concat_axis=0, tiled=True)  38.3 us
    all_to_all x4, starting transfers between devices, shards(): lax.all_to_all(a, axes, split_axis=0, concat_axis=0, tiled=True)  18.4 us
    pallas_call x1, Pallas kernels, expert_call(): pl.pallas_call(expert_kernel, grid=(8 // step,), in_specs=[pl.BlockSpec((...  5.58 us
  transfers between devices with their start and end apart: 10, of which 8 were waited for; matrix products, arithmetic and copies ran while one was open for 2% of the time, Pallas kernels for 5%

profile of v3, /device:TPU:1, one launch (start us, length us, event | category | flops | bytes accessed | tf_op | source)
XLA Modules:
  0.0 226.5 jit_solution(7063290795508079245)
XLA Ops:
  7.2 0.0 copy-start
  7.2 0.0 all-gather.4.cloned.1.call-start
  7.2 0.7 all-gather.4.cloned.1.call-update
  7.9 0.6 pad_add_fusion.place_ref
  8.5 2.7 %shard_map.131 = bf16[8,176,128]{2,1,0:T(8,128)(2,1)} custom-call(s32[4]{0:T(128)} %pad_add_fusion.place_ref, bf16[32,1024]{1,0:T(8,128)(2,1)} %bitcast.29, bf16[32,1024]{1,0:T(8,128)(2,1)} %bitcast.30, bf16[32,1024]{1,0:T(8,128)(2,1)} %bitcast.31, bf16[32,2048]{1,0:T(8,128)(2,1)} %bitcast.23, s32[2,32]{1,0:T(2,128)} %bitcast.32), custom_call_target="tpu_custom_call" | custom-call | tf_op jit(solution)/shard_map/pallas_call | solution.py:304
  11.2 23.8 %all_to_all.35.packed_ref = bf16[8,176,128]{2,1,0:T(8,128)(2,1)S(1)} all-to-all(bf16[8,176,128]{2,1,0:T(8,128)(2,1)} %shard_map.131), channel_id=1, replica_groups=mesh['x'=4,'z'=8,'c'=2,'y'=8] {'z'}, dimensions={0} | all-to-all | bytes 720896 | tf_op jit(solution)/shard_map/all_to_all | solution.py:294
  35.0 1.1 shard_map.132
  36.2 6.3 %all-to-all-start.1 = ((bf16[8,8,64,128]{3,2,1,0:T(8,128)(2,1)}), bf16[8,8,64,128]{3,2,1,0:T(8,128)(2,1)S(1)}, u32[]{:S(2)}, u32[]{:S(2)}) async-start(bf16[8,8,64,128]{3,2,1,0:T(8,128)(2,1)} %shard_map.132), calls=%async_computation.1 | async-start | bytes 2097152 | tf_op jit(solution)/shard_map/all_to_all | solution.py:294
  42.5 0.0 copy-done
  42.5 0.7 collective-permute-start
  43.2 0.0 collective-permute-done._.own_ref
  43.2 14.4 %all-to-all-done.1 = bf16[8,8,64,128]{3,2,1,0:T(8,128)(2,1)S(1)} async-done(((bf16[8,8,64,128]{3,2,1,0:T(8,128)(2,1)}), bf16[8,8,64,128]{3,2,1,0:T(8,128)(2,1)S(1)}, u32[]{:S(2)}, u32[]{:S(2)}) %all-to-all-start.1) | async-done | bytes 1048608 | tf_op jit(solution)/shard_map/all_to_all | solution.py:294
  57.6 0.6 copy-done.5
  58.2 3.5 %shard_map.133 = bf16[8,256,128]{2,1,0:T(8,128)(2,1)} custom-call(s32[4]{0:T(128)S(1)} %copy-done.5, s32[16,16]{1,0:T(8,128)S(1)} %bitcast.26, bf16[8,176,128]{2,1,0:T(8,128)(2,1)S(1)} %all_to_all.35.packed_ref, bf16[64,64,128]{2,1,0:T(8,128)(2,1)S(1)} %bitcast.22, bf16[256,256]{1,0:T(8,128)(2,1)S(1)} %collective-permute-done._.own_ref), custom_call_target="tpu_custom_call" | custom-call | tf_op jit(solution)/shard_map/pallas_call | solution.py:321
  61.6 3.5 %all-to-all-start.2 = ((bf16[8,256,128]{2,1,0:T(8,128)(2,1)}), bf16[8,256,128]{2,1,0:T(8,128)(2,1)S(1)}, u32[]{:S(2)}, u32[]{:S(2)}) async-start(bf16[8,256,128]{2,1,0:T(8,128)(2,1)} %shard_map.133), calls=%async_computation.2 | async-start | bytes 1048576 | tf_op jit(solution)/shard_map/all_to_all | solution.py:294
  65.1 2.3 %collective-permute-start.2 = (bf16[256,256]{1,0:T(8,128)(2,1)S(1)}, bf16[256,256]{1,0:T(8,128)(2,1)S(1)}, u32[]{:S(2)}, u32[]{:S(2)}) collective-permute-start(bf16[256,256]{1,0:T(8,128)(2,1)S(1)} %collective-permute-done._.own_ref), channel_id=1, source_target_pairs={{0,128},{128,0},{256,384},{384,256},{1,129},{129,1},{257,385},{385... | collective-permute-start | bytes 393224 | tf_op jit(solution)/shard_map/ppermute | solution.py:325
  67.4 3.0 %collective-permute-start.1 = (bf16[256,256]{1,0:T(8,128)(2,1)S(1)}, bf16[256,256]{1,0:T(8,128)(2,1)S(1)}, u32[]{:S(2)}, u32[]{:S(2)}) collective-permute-start(bf16[256,256]{1,0:T(8,128)(2,1)S(1)} %collective-permute-done._.own_ref), channel_id=1, source_target_pairs={{0,8},{8,0},{1,9},{9,1},{2,10},{10,2},{3,11},{11,3},{4,12},{12,4},... | collective-permute-start | bytes 393224 | tf_op jit(solution)/shard_map/ppermute | solution.py:327
  70.4 0.9 collective-permute-done.2.x_ref
  71.3 3.6 %collective-permute-start.3 = (bf16[256,256]{1,0:T(8,128)(2,1)S(1)}, bf16[256,256]{1,0:T(8,128)(2,1)S(1)}, u32[]{:S(2)}, u32[]{:S(2)}) collective-permute-start(bf16[256,256]{1,0:T(8,128)(2,1)S(1)} %collective-permute-done.2.x_ref), channel_id=1, source_target_pairs={{0,8},{8,0},{1,9},{9,1},{2,10},{10,2},{3,11},{11,3},{4,12},{12,4},... | collective-permute-start | bytes 393224 | tf_op jit(solution)/shard_map/ppermute | solution.py:327
  74.9 0.0 collective-permute-done.1.core_ref
  74.9 0.9 collective-permute-done.3.x_core_ref
  75.8 7.2 %all-to-all-done.2.att_ref = bf16[8,256,128]{2,1,0:T(8,128)(2,1)S(1)} async-done(((bf16[8,256,128]{2,1,0:T(8,128)(2,1)}), bf16[8,256,128]{2,1,0:T(8,128)(2,1)S(1)}, u32[]{:S(2)}, u32[]{:S(2)}) %all-to-all-start.2) | async-done | bytes 524320 | tf_op jit(solution)/shard_map/all_to_all | solution.py:294
  83.0 2.2 shard_map.134
  85.2 4.6 %all-to-all-start.4 = ((bf16[64,16,256]{2,1,0:T(8,128)(2,1)}), bf16[64,16,256]{2,1,0:T(8,128)(2,1)S(1)}, u32[]{:S(2)}, u32[]{:S(2)}) async-start(bf16[64,16,256]{2,1,0:T(8,128)(2,1)} %get-tuple-element.15), calls=%async_computation.4 | async-start | bytes 1048576 | tf_op jit(solution)/shard_map/all_to_all | solution.py:294
  89.7 0.0 all-gather.6.cloned.1.call-start
  89.8 3.3 %all-gather.4.cloned.1.call-done.down_ref = bf16[8,176,2048]{2,1,0:T(8,128)(2,1)} async-done(((bf16[1,176,2048]{2,1,0:T(8,128)(2,1)}), bf16[8,176,2048]{2,1,0:T(8,128)(2,1)}) %all-gather.4.cloned.1.call-update) | async-done | bytes 5767184 | tf_op jit(solution)/shard_map/all_gather | solution.py:296
  93.1 1.2 slice.4
  95.0 12.1 %all-to-all-done.4 = bf16[64,16,256]{2,1,0:T(8,128)(2,1)S(1)} async-done(((bf16[64,16,256]{2,1,0:T(8,128)(2,1)}), bf16[64,16,256]{2,1,0:T(8,128)(2,1)S(1)}, u32[]{:S(2)}, u32[]{:S(2)}) %all-to-all-start.4) | async-done | bytes 524320 | tf_op jit(solution)/shard_map/all_to_all | solution.py:294
  107.1 0.9 broadcast_add_fusion
  108.0 0.0 all-gather.6.cloned.1.call-update
  108.0 4.1 %all-to-all-start.3 = ((bf16[8,32,256]{2,1,0:T(8,128)(2,1)}), bf16[8,32,256]{2,1,0:T(8,128)(2,1)S(1)}, u32[]{:S(2)}, u32[]{:S(2)}) async-start(bf16[8,32,256]{2,1,0:T(8,128)(2,1)} %get-tuple-element.10), calls=%async_computation.3 | async-start | bytes 262144 | tf_op jit(solution)/shard_map/all_to_all | solution.py:294
  112.1 0.1 copy.19.ids_ref
  112.2 1.2 copy.18.router_ref
  113.4 0.0 copy-done.8
  113.4 0.5 copy.20
  113.9 1.4 copy.21
  115.4 4.6 %all-to-all-done.3.projected_ref = bf16[8,32,256]{2,1,0:T(8,128)(2,1)S(1)} async-done(((bf16[8,32,256]{2,1,0:T(8,128)(2,1)}), bf16[8,32,256]{2,1,0:T(8,128)(2,1)S(1)}, u32[]{:S(2)}, u32[]{:S(2)}) %all-to-all-start.3) | async-done | bytes 131104 | tf_op jit(solution)/shard_map/all_to_all | solution.py:294
  119.9 0.0 copy-done.1
  119.9 0.9 shard_map.135
  120.9 0.7 copy-done.2
  121.6 40.7 %all-gather.6.cloned.1.call-done = bf16[512,16,256]{2,1,0:T(8,128)(2,1)} async-done(((bf16[64,16,256]{2,1,0:T(8,128)(2,1)}), bf16[512,16,256]{2,1,0:T(8,128)(2,1)}) %all-gather.6.cloned.1.call-update) | async-done | bytes 4194320 | tf_op jit(solution)/shard_map/all_gather | solution.py:338
  162.3 5.6 %shard_map.136 = bf16[8,176,128]{2,1,0:T(8,128)(2,1)S(1)} custom-call(bf16[8,4,8,2,16,256]{5,4,3,2,1,0:T(8,128)(2,1)} %bitcast.27, f32[8,256]{1,0:T(8,128)S(1)} %reshape.27.inverse_ref, bf16[2048,176]{1,0:T(8,128)(2,1)S(1)} %bitcast.20, bf16[2048,176]{1,0:T(8,128)(2,1)S(1)} %bitcast.21, f32[32,2]{1,0:T(8,128)S(1)} %get-tuple-element.12._.gates_ref), custom_call_target="tpu_custom_call" | custom-call | tf_op jit(solution)/shard_map/pallas_call | solution.py:234
  167.9 17.1 %all_to_all.36.active_ref = bf16[8,176,128]{2,1,0:T(8,128)(2,1)S(1)} all-to-all(bf16[8,176,128]{2,1,0:T(8,128)(2,1)S(1)} %shard_map.136), channel_id=1, replica_groups=mesh['x'=4,'z'=8,'c'=2,'y'=8] {'y'}, dimensions={0} | all-to-all | bytes 720896 | tf_op jit(solution)/shard_map/all_to_all | solution.py:294
  184.9 3.7 %shard_map.137 = bf16[128,2048]{1,0:T(8,128)(2,1)S(1)} custom-call(bf16[8,176,128]{2,1,0:T(8,128)(2,1)S(1)} %all_to_all.36.active_ref, bf16[8,176,2048]{2,1,0:T(8,128)(2,1)} %all-gather.4.cloned.1.call-done.down_ref), custom_call_target="tpu_custom_call" | custom-call | tf_op jit(solution)/shard_map/pallas_call | solution.py:359
  188.7 0.3 reshape.28
  189.0 29.5 %all_to_all.37 = bf16[64,2,2048]{2,1,0:T(2,128)(2,1)S(1)} all-to-all(bf16[64,2,2048]{2,1,0:T(2,128)(2,1)S(1)} %reshape.28), channel_id=1, replica_groups=mesh['x'=4,'z'=8,'c'=2,'y'=8] {'x','z','c'}, dimensions={0} | all-to-all | bytes 1048576 | tf_op jit(solution)/shard_map/all_to_all | solution.py:294
  218.5 0.2 reshape.29.rows_ref
  218.7 0.9 shard_map.138
  (18 shorter events, 0.0 us)
Async XLA Ops:
  7.2 35.3 %copy-start = (bf16[1024,256]{1,0:T(8,128)(2,1)S(1)}, bf16[1024,256]{1,0:T(8,128)(2,1)}, u32[]{:S(2)}) copy-start(bf16[1024,256]{1,0:T(8,128)(2,1)} %param.17) | copy-start | bytes 1572868
  7.2 50.4 %copy-start.7 = (s32[1,16,16]{2,1,0:T(8,128)S(1)}, s32[1,16,16]{2,1,0:T(8,128)}, u32[]{:S(2)}) copy-start(s32[1,16,16]{2,1,0:T(8,128)} %param.16) | copy-start | bytes 3076
  7.2 67.7 %copy-start.4 = (f32[2048]{0:T(1024)S(1)}, f32[2048]{0:T(1024)}, u32[]{:S(2)}) copy-start(f32[2048]{0:T(1024)} %param.18) | copy-start | bytes 24580
  7.2 85.9 %all-gather.4.cloned.1.call-start = ((), (), s32[]{:S(2)}) async-start(), calls=%async_computation.7 | async-start | bytes 6488064 | tf_op jit(solution)/shard_map/all_gather | solution.py:296
  8.5 74.5 %copy-start.6 = (s32[4]{0:T(128)S(1)}, s32[4]{0:T(128)}, u32[]{:S(2)}) copy-start(s32[4]{0:T(128)} %pad_add_fusion.place_ref) | copy-start | bytes 52
  35.0 77.1 %copy-start.9 = (s32[1,32,2]{1,2,0:T(2,128)S(1)}, s32[1,32,2]{1,2,0:T(2,128)}, u32[]{:S(2)}) copy-start(s32[1,32,2]{1,2,0:T(2,128)} %param.20) | copy-start | bytes 772
  35.0 78.4 %copy-start.8 = (bf16[1,2048,176]{1,2,0:T(8,128)(2,1)S(1)}, bf16[1,2048,176]{1,2,0:T(8,128)(2,1)}, u32[]{:S(2)}) copy-start(bf16[1,2048,176]{1,2,0:T(8,128)(2,1)} %param.21) | copy-start | bytes 2162692
  36.2 21.4 %all-to-all-start.1 = ((bf16[8,8,64,128]{3,2,1,0:T(8,128)(2,1)}), bf16[8,8,64,128]{3,2,1,0:T(8,128)(2,1)S(1)}, u32[]{:S(2)}, u32[]{:S(2)}) async-start(bf16[8,8,64,128]{3,2,1,0:T(8,128)(2,1)} %shard_map.132), calls=%async_computation.1 | async-start | bytes 2097152 | tf_op jit(solution)/shard_map/all_to_all | solution.py:294
  42.5 0.7 collective-permute-start
  57.6 0.6 copy-start.5
  58.2 61.8 %copy-start.1 = (bf16[1,32,2048]{2,1,0:T(8,128)(2,1)S(1)}, bf16[1,32,2048]{2,1,0:T(8,128)(2,1)}, u32[]{:S(2)}) copy-start(bf16[1,32,2048]{2,1,0:T(8,128)(2,1)} %param.12) | copy-start | bytes 393220
  61.6 21.4 %all-to-all-start.2 = ((bf16[8,256,128]{2,1,0:T(8,128)(2,1)}), bf16[8,256,128]{2,1,0:T(8,128)(2,1)S(1)}, u32[]{:S(2)}, u32[]{:S(2)}) async-start(bf16[8,256,128]{2,1,0:T(8,128)(2,1)} %shard_map.133), calls=%async_computation.2 | async-start | bytes 1048576 | tf_op jit(solution)/shard_map/all_to_all | solution.py:294
  65.1 6.1 %collective-permute-start.2 = (bf16[256,256]{1,0:T(8,128)(2,1)S(1)}, bf16[256,256]{1,0:T(8,128)(2,1)S(1)}, u32[]{:S(2)}, u32[]{:S(2)}) collective-permute-start(bf16[256,256]{1,0:T(8,128)(2,1)S(1)} %collective-permute-done._.own_ref), channel_id=1, source_target_pairs={{0,128},{128,0},{256,384},{384,256},{1,129},{129,1},{257,385},{385... | collective-permute-start | bytes 393224 | tf_op jit(solution)/shard_map/ppermute | solution.py:325
  67.4 7.4 %collective-permute-start.1 = (bf16[256,256]{1,0:T(8,128)(2,1)S(1)}, bf16[256,256]{1,0:T(8,128)(2,1)S(1)}, u32[]{:S(2)}, u32[]{:S(2)}) collective-permute-start(bf16[256,256]{1,0:T(8,128)(2,1)S(1)} %collective-permute-done._.own_ref), channel_id=1, source_target_pairs={{0,8},{8,0},{1,9},{9,1},{2,10},{10,2},{3,11},{11,3},{4,12},{12,4},... | collective-permute-start | bytes 393224 | tf_op jit(solution)/shard_map/ppermute | solution.py:327
  71.3 4.5 %collective-permute-start.3 = (bf16[256,256]{1,0:T(8,128)(2,1)S(1)}, bf16[256,256]{1,0:T(8,128)(2,1)S(1)}, u32[]{:S(2)}, u32[]{:S(2)}) collective-permute-start(bf16[256,256]{1,0:T(8,128)(2,1)S(1)} %collective-permute-done.2.x_ref), channel_id=1, source_target_pairs={{0,8},{8,0},{1,9},{9,1},{2,10},{10,2},{3,11},{11,3},{4,12},{12,4},... | collective-permute-start | bytes 393224 | tf_op jit(solution)/shard_map/ppermute | solution.py:327
  85.2 21.9 %all-to-all-start.4 = ((bf16[64,16,256]{2,1,0:T(8,128)(2,1)}), bf16[64,16,256]{2,1,0:T(8,128)(2,1)S(1)}, u32[]{:S(2)}, u32[]{:S(2)}) async-start(bf16[64,16,256]{2,1,0:T(8,128)(2,1)} %get-tuple-element.15), calls=%async_computation.4 | async-start | bytes 1048576 | tf_op jit(solution)/shard_map/all_to_all | solution.py:294
  89.7 72.5 %all-gather.6.cloned.1.call-start = ((), (), s32[]{:S(2)}) async-start(), calls=%async_computation.8 | async-start | bytes 4718592 | tf_op jit(solution)/shard_map/all_gather | solution.py:338
  108.0 11.9 %all-to-all-start.3 = ((bf16[8,32,256]{2,1,0:T(8,128)(2,1)}), bf16[8,32,256]{2,1,0:T(8,128)(2,1)S(1)}, u32[]{:S(2)}, u32[]{:S(2)}) async-start(bf16[8,32,256]{2,1,0:T(8,128)(2,1)} %get-tuple-element.10), calls=%async_computation.3 | async-start | bytes 262144 | tf_op jit(solution)/shard_map/all_to_all | solution.py:294
  120.9 0.7 copy-start.2
  167.9 50.8 %copy-start.3 = (f32[32,2048]{1,0:T(8,128)S(1)}, f32[32,2048]{1,0:T(8,128)}, u32[]{:S(2)}) copy-start(f32[32,2048]{1,0:T(8,128)} %copy-done.2) | copy-start | bytes 786436
Sparse Core Ops, SparseCore 0:
  10.1 82.9 all-gather.3
  108.1 54.1 all-gather.5

commit v4 on v3

--- a/solution.py
+++ b/solution.py
@@ -15,17 +15,18 @@
 EXPERTS = 64
 F32 = jnp.float32
 BF16 = jnp.bfloat16
-VMEM_LIMIT = 48 * 1024 * 1024
-
-
-def vmem_call(body, out_shape, n_in, smem=(), hbm=(), scratch=(), limit=VMEM_LIMIT):
-    space = lambda i: pltpu.SMEM if i in smem else pl.ANY if i in hbm else pltpu.VMEM
+VMEM_LIMIT = 32 * 1024 * 1024
+
+
+def vmem_call(body, out_shape, n_in, hbm=(), unread=(), scratch=(), limit=VMEM_LIMIT, flops=0):
+    space = lambda i: pltpu.HBM if i in hbm else pl.ANY if i in unread else pltpu.VMEM
     return pl.pallas_call(
         body,
         out_shape=out_shape,
         in_specs=[pl.BlockSpec(memory_space=space(i)) for i in range(n_in)],
         out_specs=jax.tree.map(lambda _: pl.BlockSpec(memory_space=pltpu.VMEM), out_shape),
         scratch_shapes=list(scratch),
+        cost_estimate=pl.CostEstimate(flops=flops, bytes_accessed=flops // 512, transcendentals=0),
         compiler_params=pltpu.CompilerParams(vmem_limit_bytes=limit),
     )
 
@@ -53,7 +54,7 @@
 
 
 def pack_kernel(
-    place_ref, query_hbm, key_hbm, value_hbm, residual_hbm, ids_hbm, out_ref,
+    mask_ref, query_hbm, key_hbm, value_hbm, residual_hbm, ids_hbm, out_ref, mask_out_ref,
     query_ref, key_ref, value_ref, residual_ref, ids_ref, sems,
 ):
     pairs = (
@@ -63,7 +64,8 @@
     copies = [pltpu.make_async_copy(a, b, sems.at[i]) for i, (a, b) in enumerate(pairs)]
     for copy in copies:
         copy.start()
-    z, y = place_ref[1], place_ref[3]
+    z, y = lax.axis_index("z"), lax.axis_index("y")
+    mask_out_ref[...] = mask_ref[...]
     copies[0].wait()
     expert = lax.broadcasted_iota(jnp.int32, (EXPERTS, TOK), 0)
     first = jnp.where(expert == ids_ref[0:1], 1.0, 0.0)
@@ -96,18 +98,20 @@
         out_ref[holder, 128:160] = residual_ref[:, h * CHUNK + HEAD : (h + 1) * CHUNK]
 
 
-def spread_kernel(packed_ref, out_ref):
-    for i in range(8):
+def spread_kernel(packed_ref, _, out_ref):
+    for i in range(4):
         out_ref[i] = packed_ref[:, 32:96]
 
 
-def attend_kernel(place_ref, mask_ref, packed_ref, kv_ref, _, out_ref):
-    x, c = place_ref[0], place_ref[2]
-    n_key = kv_ref.shape[0] * TOK
-    keys = kv_ref[:, :TOK].reshape(n_key, HEAD)
-    values = kv_ref[:, TOK:].reshape(n_key, HEAD)
+def attend_kernel(mask_ref, packed_ref, own_ref, other_ref, out_ref):
+    x, c = lax.axis_index("x"), lax.axis_index("c")
+    refs = (own_ref, other_ref)
+    n_key = 2 * own_ref.shape[0] * TOK
+    keys = jnp.concatenate([ref[:, :TOK].reshape(n_key // 2, HEAD) for ref in refs], axis=0)
+    values = jnp.concatenate([ref[:, TOK:].reshape(n_key // 2, HEAD) for ref in refs], axis=0)
     key_row = lax.broadcasted_iota(jnp.int32, (1, n_key), 1)
-    key_x, key_c, key_z, key_t = key_row // 512, key_row // 256 % 2, key_row // 32 % 8, key_row % 32
+    key_x, key_z, key_t = key_row // 256 % 4, key_row // 32 % 8, key_row % 32
+    key_c = jnp.where(key_row < n_key // 2, c, 1 - c)
     key_pos = key_x * 512 + key_z * 64 + key_c * 32 + key_t
     block_row = lax.broadcasted_iota(jnp.int32, (16, n_key), 0)
     key_onehot = (block_row == jnp.broadcast_to(key_pos // BLOCK, (16, n_key))).astype(BF16)
@@ -134,13 +138,26 @@
             out_ref[z, 2 * j * TOK : 2 * (j + 1) * TOK] = attended
 
 
+def route_kernel(packed_ref, out_ref):
+    spots = jnp.sum(packed_ref[:, 160:176].astype(F32), axis=0)
+    spot_first = jnp.concatenate([spots[0:1], spots[1:2]], axis=1)
+    spot_second = jnp.concatenate([spots[2:3], spots[3:4]], axis=1)
+    row = lax.broadcasted_iota(jnp.int32, (8 * EXPERTS * CAP, 1), 0)
+    row_spot = (row // 16 * CAP + row % CAP).astype(F32)
+    row_block = row // CAP % 8
+    col_block = lax.broadcasted_iota(jnp.int32, (1, 8 * TOK), 1) // TOK
+    taken = (spot_first == row_spot) | (spot_second == row_spot)
+    out_ref[...] = jnp.where(taken & (row_block == col_block), 1.0, 0.0).astype(BF16)
+
+
 def project_kernel(
-    place_ref, att_ref, own_ref, core_ref, x_ref, x_core_ref, packed_ref, gain_ref, attended_ref, projected_ref, buffer_ref
+    att_ref, own_ref, core_ref, x_ref, x_core_ref, packed_ref, gain_ref, route_ref,
+    attended_ref, projected_ref, buffer_ref,
 ):
-    z, y = place_ref[1], place_ref[3]
+    z, y = lax.axis_index("z"), lax.axis_index("y")
     mine = pl.ds(pl.multiple_of(z * TOK, TOK), TOK)
     attended_ref[...] = jnp.concatenate([att_ref[h, mine] for h in range(8)], axis=1)
-    quarter = place_ref[0] % 2 * 2 + place_ref[2]
+    quarter = lax.axis_index("x") % 2 * 2 + lax.axis_index("c")
     total = None
     for ref, flip in ((own_ref, 0), (core_ref, 1), (x_ref, 2), (x_core_ref, 3)):
         rows = quarter ^ flip
@@ -155,24 +172,17 @@
     )
     hidden = residual.astype(F32) + projected.astype(F32)
     scaled = (hidden * gain_ref[pl.ds(chunk_of(z, y), 1), :]).astype(BF16)
-    spots = jnp.sum(packed_ref[:, 160:176].astype(F32), axis=0)
-    spot_first = jnp.concatenate([spots[0:1], spots[1:2]], axis=1)
-    spot_second = jnp.concatenate([spots[2:3], spots[3:4]], axis=1)
-    row = lax.broadcasted_iota(jnp.int32, (8 * EXPERTS * CAP, 1), 0)
-    row_spot = (row // 16 * CAP + row % CAP).astype(F32)
-    row_block = row // CAP % 8
-    col_block = lax.broadcasted_iota(jnp.int32, (1, 8 * TOK), 1) // TOK
-    taken = (spot_first == row_spot) | (spot_second == row_spot)
-    spread = jnp.where(taken & (row_block == col_block), 1.0, 0.0).astype(BF16)
-    rows = jnp.dot(spread, scaled, preferred_element_type=F32).astype(BF16)
+    rows = jnp.dot(route_ref[...], scaled, preferred_element_type=F32).astype(BF16)
     buffer_ref[...] = rows.reshape(EXPERTS, 16, CHUNK)
 
 
 def gates_kernel(
-    place_ref, projected_ref, residual_ref, gain_ref, router_ref, ids_ref,
-    hidden_ref, gates_ref, first_ref, second_ref,
+    projected_ref, residual_ref, gain_ref, router_ref, ids_ref, down_hbm,
+    hidden_ref, gates_ref, first_ref, second_ref, down_ref, sem,
 ):
-    y = place_ref[3]
+    copy = pltpu.make_async_copy(down_hbm, down_ref, sem)
+    copy.start()
+    y = lax.axis_index("y")
     projected = jnp.concatenate([projected_ref[holder_of(k, y)] for k in range(8)], axis=1)
     hidden = residual_ref[...].astype(F32) + projected.astype(F32)
     hidden_ref[...] = hidden
@@ -187,12 +197,14 @@
     spot = lax.broadcasted_iota(jnp.int32, (TOK, EXPERTS * CAP), 1).astype(F32)
     first_ref[...] = jnp.where(spot == spot_first, 1.0, 0.0).astype(BF16)
     second_ref[...] = jnp.where(spot == spot_second, 1.0, 0.0).astype(BF16)
-
-
-def expert_kernel(rows_ref, inverse_ref, gate_ref, up_ref, _, out_ref):
+    copy.wait()
+
+
+def expert_kernel(rows_ref, inverse_ref, weight_ref, _, out_ref):
+    transposed = (((1,), (1,)), ((), ()))
     streams = rows_ref.shape[0]
     first_stream = pl.program_id(0) * streams
-    gate = up = squares = None
+    units = squares = None
     for k in range(8):
         piece = jnp.concatenate(
             [
@@ -201,35 +213,27 @@
             ],
             axis=0,
         )
-        span = slice(k * CHUNK, (k + 1) * CHUNK)
         plain = piece.astype(F32) * inverse_ref[k : k + 1, :]
-        gate_k = jnp.dot(piece, gate_ref[span], preferred_element_type=F32)
-        up_k = jnp.dot(piece, up_ref[span], preferred_element_type=F32)
-        squares_k = plain * plain
-        if k == 0:
-            gate, up, squares = gate_k, up_k, squares_k
-        else:
-            gate, up, squares = gate + gate_k, up + up_k, squares + squares_k
-    meansq = jnp.sum(squares, axis=-1, keepdims=True) * (1.0 / D)
-    factor = lax.rsqrt(meansq + 1e-06)
-    gate, up = gate * factor, up * factor
+        weight = weight_ref[:, k * CHUNK : (k + 1) * CHUNK]
+        part = lax.dot_general(weight, piece, transposed, preferred_element_type=F32)
+        units = part if k == 0 else units + part
+        squares = plain * plain if k == 0 else squares + plain * plain
+    high = squares.astype(BF16)
+    low = (squares - high.astype(F32)).astype(BF16)
+    ones = jnp.ones((16, CHUNK), BF16)
+    sums = [lax.dot_general(ones, a, transposed, preferred_element_type=F32) for a in (high, low)]
+    factor = lax.rsqrt((sums[0] + sums[1])[0:1] * (1.0 / D) + 1e-06)
+    units = units * factor
+    width = units.shape[0] // 2
+    gate, up = units[:width], units[width:]
     active = (gate / (1.0 + jnp.exp(-gate)) * up).astype(BF16)
-    width = active.shape[1]
-    row = lax.broadcasted_iota(jnp.int32, (width, width), 0)
-    col = lax.broadcasted_iota(jnp.int32, (width, width), 1)
-    same = jnp.where(row == col, 1.0, 0.0).astype(BF16)
-    for s in range(rows_ref.shape[0]):
-        out_ref[s] = lax.dot_general(
-            same,
-            active[s * 128 : (s + 1) * 128],
-            (((1,), (1,)), ((), ())),
-            preferred_element_type=F32,
-        ).astype(BF16)
-
-
-def expert_call(rows, inverse, gate, up, after):
+    for s in range(streams):
+        out_ref[s] = active[:, s * 128 : (s + 1) * 128]
+
+
+def expert_call(rows, inverse, weight, after):
     step = 2
-    width = gate.shape[1]
+    width = weight.shape[0] // 2
     whole = pl.BlockSpec(memory_space=pltpu.VMEM)
     return pl.pallas_call(
         expert_kernel,
@@ -238,13 +242,12 @@
             pl.BlockSpec((step, 4, 8, 2, 16, CHUNK), lambda i: (i, 0, 0, 0, 0, 0)),
             whole,
             whole,
-            whole,
             pl.BlockSpec(memory_space=pl.ANY),
         ],
         out_specs=pl.BlockSpec((step, width, 128), lambda i: (i, 0, 0)),
         out_shape=jax.ShapeDtypeStruct((8, width, 128), BF16),
-        compiler_params=pltpu.CompilerParams(vmem_limit_bytes=VMEM_LIMIT),
-    )(rows, inverse, gate, up, after)
+        compiler_params=pltpu.CompilerParams(vmem_limit_bytes=48 * 1024 * 1024),
+    )(rows, inverse, weight, after)
 
 
 def down_kernel(active_ref, down_ref, out_ref):
@@ -288,7 +291,6 @@
     w_down,
 ):
     seq = ("x", "z", "c")
-    place = jnp.stack([lax.axis_index(a) for a in ("x", "z", "c", "y")]).astype(jnp.int32)
     ids = route_ids[0]
     shape = lambda *s: jax.ShapeDtypeStruct(s, BF16)
     swap = lambda a, axes: lax.all_to_all(a, axes, split_axis=0, concat_axis=0, tiled=True)
@@ -301,11 +303,10 @@
         weight, ("z", "y"), [(z * 8 + y, z * 8 + (z - y) % 8) for z in range(8) for y in range(8)]
     )
 
-    packed = vmem_call(
+    packed, mask = vmem_call(
         pack_kernel,
-        shape(8, 176, HEAD),
+        (shape(8, 176, HEAD), jax.ShapeDtypeStruct(block_mask.shape[1:], jnp.int32)),
         6,
-        smem=(0,),
         hbm=(1, 2, 3, 4, 5),
         scratch=(
             *(pltpu.VMEM((TOK, 8 * HEAD), BF16) for _ in range(3)),
@@ -314,46 +315,46 @@
             pltpu.SemaphoreType.DMA((5,)),
         ),
         limit=60 * 1024 * 1024,
-    )(place, queries[0], keys[0], values[0], residual[0], ids.T)
+    )(block_mask[0], queries[0], keys[0], values[0], residual[0], ids.T)
     packed = swap(packed, "z")
-    kv = vmem_call(spread_kernel, shape(8, 8, 2 * TOK, HEAD), 1)(packed)
-    kv = swap(kv, ("x", "c"))
-    att = vmem_call(attend_kernel, shape(8, 8 * TOK, HEAD), 5, smem=(0,), hbm=(4,))(
-        place, block_mask[0], packed, kv.reshape(64, 2 * TOK, HEAD), weight
-    )
     other_core = [(0, 1), (1, 0)]
+    kv = vmem_call(spread_kernel, shape(4, 8, 2 * TOK, HEAD), 2, unread=(1,))(packed, weight)
+    kv = swap(kv, "x").reshape(32, 2 * TOK, HEAD)
+    other_kv = lax.ppermute(kv, "c", other_core)
+    att = vmem_call(attend_kernel, shape(8, 8 * TOK, HEAD), 4)(mask, packed, kv, other_kv)
     beside = lax.ppermute(weight, "x", [(0, 1), (1, 0), (2, 3), (3, 2)])
     weights = (
         weight, lax.ppermute(weight, "c", other_core), beside, lax.ppermute(beside, "c", other_core)
     )
     att = swap(att, "z")
+    route = vmem_call(route_kernel, shape(8 * EXPERTS * CAP, 8 * TOK), 1, flops=2_000_000_000)(packed)
     attended, projected, buffer = vmem_call(
         project_kernel,
         (shape(TOK, 8 * HEAD), shape(8, TOK, CHUNK), shape(EXPERTS, 16, CHUNK)),
         8,
-        smem=(0,),
-    )(place, att, *weights, packed, norm_gain.reshape(8, CHUNK))
+    )(att, *weights, packed, norm_gain.reshape(8, CHUNK), route)
 
     arrived = swap(buffer, seq) + down[0, 0, 0] * 0
     rows = lax.all_gather(arrived, "y", axis=0)
     projected = swap(projected, "z")
-    hidden, gates, first, second = vmem_call(
+    hidden, gates, first, second, down = vmem_call(
         gates_kernel,
         (
             jax.ShapeDtypeStruct((TOK, D), F32),
             jax.ShapeDtypeStruct((TOK, 2), F32),
             shape(TOK, EXPERTS * CAP),
             shape(TOK, EXPERTS * CAP),
+            shape(*down.shape),
         ),
         6,
-        smem=(0,),
-    )(place, projected, residual[0], norm_gain[None], router, ids)
+        hbm=(5,),
+        scratch=(pltpu.SemaphoreType.DMA(()),),
+    )(projected, residual[0], norm_gain[None], router, ids, down)
 
     active = expert_call(
         rows.reshape(8, 4, 8, 2, 16, CHUNK),
         (1.0 / norm_gain).reshape(8, CHUNK),
-        w_gate[0],
-        w_up[0],
+        jnp.concatenate([w_gate[0].T, w_up[0].T], axis=0),
         gates,
     )
     out = vmem_call(down_kernel, shape(128, D), 2)(swap(active, "y"), down)

time: 227 us -> 220 us (0.969)
  blocking collectives: 70.3 us -> 57.2 us
  starting transfers between devices: 28 us -> 39.8 us
  Pallas kernels: 20.6 us -> 13.5 us
  local copies, waits for them, and re-layouts: 6.35 us -> 9.56 us
  waiting for transfers between devices: 84.8 us -> 82 us
    all_to_all x3, blocking collectives: 70.3 us -> 57.2 us  [shards(): lax.all_to_all(a, axes, split_axis=0, concat_axis=0, tiled=True)]
    all_to_all x4, starting transfers between devices: 18.4 us -> 25.4 us  [shards(): lax.all_to_all(a, axes, split_axis=0, concat_axis=0, tiled=True)]
    ppermute x0 -> x1, starting transfers between devices: none -> 5.35 us  [shards(): other_kv = lax.ppermute(kv, 'c', other_core)]
    all_gather x1, waiting for transfers between devices: 40.7 us -> 36.6 us  [shards(): rows = lax.all_gather(arrived, 'y', axis=0)]
    unnamed x23 -> x21, local copies, waits for them, and re-layouts: 4.49 us -> 7.64 us
    pallas_call x1, Pallas kernels: 3.73 us -> 1.09 us  [shards(): out = vmem_call(down_kernel, shape(128, D), 2)(swap(active, 'y'), down)]
    pallas_call x1, Pallas kernels: 5.58 us -> 3.12 us  [expert_call(): pl.pallas_call(expert_kernel, grid=(8 // step,), in_specs=[pl.BlockSpec((...]
    pallas_call x3 -> x4, Pallas kernels: 7.27 us -> 5.9 us  [the longest x1 2.96 us: shards(): vmem_call(attend_kernel, shape(8, 8 * TOK, HEAD), 4)]
  transfers between devices with their start and end apart: 10 -> 11, of which waited for: 8 -> 9; matrix products, arithmetic and copies ran while one was open for 2% -> 1% of each run, Pallas kernels for 5% -> 4%
where the time goes in v4:
time: 220 us; the launch traced here: 219 us
  waiting for transfers between devices  82 us (37%)
  blocking collectives  57.2 us (26%)
  starting transfers between devices  39.8 us (18%)
  between operations  15 us (7%)
  Pallas kernels  13.5 us (6%)
  local copies, waits for them, and re-layouts  9.56 us (4%)
  other arithmetic  2.29 us (1%)
    all_to_all x3, blocking collectives, shards(): lax.all_to_all(a, axes, split_axis=0, concat_axis=0, tiled=True)  57.2 us
    all_to_all x4, waiting for transfers between devices, shards(): lax.all_to_all(a, axes, split_axis=0, concat_axis=0, tiled=True)  37.8 us
    all_gather x1, waiting for transfers between devices, shards(): rows = lax.all_gather(arrived, 'y', axis=0)  36.6 us
    all_to_all x4, starting transfers between devices, shards(): lax.all_to_all(a, axes, split_axis=0, concat_axis=0, tiled=True)  25.4 us
    unnamed x21, local copies, waits for them, and re-layouts  7.64 us
    ppermute x1, starting transfers between devices, shards(): other_kv = lax.ppermute(kv, 'c', other_core)  5.35 us
  transfers between devices with their start and end apart: 11, of which 9 were waited for; matrix products, arithmetic and copies ran while one was open for 1% of the time, Pallas kernels for 4%

profile of v4, /device:TPU:1, one launch (start us, length us, event | category | flops | bytes accessed | tf_op | source)
XLA Modules:
  0.0 219.3 jit_solution(4081276598109178268)
XLA Ops:
  7.2 0.0 copy-start
  7.2 0.0 all-gather.4.cloned.1.call-start
  7.2 0.7 all-gather.4.cloned.1.call-update
  7.9 2.6 %shard_map.131 = (bf16[8,176,128]{2,1,0:T(8,128)(2,1)}, s32[16,16]{1,0:T(8,128)}) custom-call(s32[16,16]{1,0:T(8,128)} %bitcast.32, bf16[32,1024]{1,0:T(8,128)(2,1)} %bitcast.29, bf16[32,1024]{1,0:T(8,128)(2,1)} %bitcast.30, bf16[32,1024]{1,0:T(8,128)(2,1)} %bitcast.31, bf16[32,2048]{1,0:T(8,128)(2,1)} %bitcast.23, s32[2,32]{1,0:T(2,128)} %bitcast.33), custom_call_target="tpu_custom_call" | custom-call | tf_op jit(solution)/shard_map/pallas_call | solution.py:306
  10.5 0.0 copy-start.7
  10.5 0.0 copy-start.6
  10.5 10.9 %all-to-all-start = ((bf16[8,176,128]{2,1,0:T(8,128)(2,1)}), bf16[8,176,128]{2,1,0:T(8,128)(2,1)S(1)}, u32[]{:S(2)}, u32[]{:S(2)}) async-start(bf16[8,176,128]{2,1,0:T(8,128)(2,1)} %get-tuple-element.13), calls=%async_computation | async-start | bytes 720896 | tf_op jit(solution)/shard_map/all_to_all | solution.py:296
  21.4 0.7 collective-permute-start
  22.1 12.2 %all-to-all-done.packed_ref = bf16[8,176,128]{2,1,0:T(8,128)(2,1)S(1)} async-done(((bf16[8,176,128]{2,1,0:T(8,128)(2,1)}), bf16[8,176,128]{2,1,0:T(8,128)(2,1)S(1)}, u32[]{:S(2)}, u32[]{:S(2)}) %all-to-all-start) | async-done | bytes 360480 | tf_op jit(solution)/shard_map/all_to_all | solution.py:296
  34.3 0.1 shard_map.132
  34.4 10.8 %all_to_all.35 = bf16[4,8,64,128]{3,2,1,0:T(8,128)(2,1)S(1)} all-to-all(bf16[4,8,64,128]{3,2,1,0:T(8,128)(2,1)S(1)} %shard_map.132), channel_id=1, replica_groups=mesh['x'=4,'z'=8,'c'=2,'y'=8] {'x'}, dimensions={0} | all-to-all | bytes 1048576 | tf_op jit(solution)/shard_map/all_to_all | solution.py:296
  45.2 5.3 %collective-permute-start.1 = (bf16[32,64,128]{2,1,0:T(8,128)(2,1)S(1)}, bf16[32,64,128]{2,1,0:T(8,128)(2,1)S(1)}, u32[]{:S(2)}, u32[]{:S(2)}) collective-permute-start(bf16[32,64,128]{2,1,0:T(8,128)(2,1)S(1)} %bitcast.21), channel_id=1, source_target_pairs={{0,8},{8,0},{1,9},{9,1},{2,10},{10,2},{3,11},{11,3},{4,12},{12,4},... | collective-permute-start | bytes 1572872 | tf_op jit(solution)/shard_map/ppermute | solution.py:323
  50.5 1.5 collective-permute-done.1.other_ref
  52.1 3.0 %shard_map.133 = bf16[8,256,128]{2,1,0:T(8,128)(2,1)} custom-call(s32[16,16]{1,0:T(8,128)S(1)} %copy-done.7, bf16[8,176,128]{2,1,0:T(8,128)(2,1)S(1)} %all-to-all-done.packed_ref, bf16[32,64,128]{2,1,0:T(8,128)(2,1)S(1)} %bitcast.22, bf16[32,64,128]{2,1,0:T(8,128)(2,1)S(1)} %collective-permute-done.1.other_ref), custom_call_target="tpu_custom_call" | custom-call | tf_op jit(solution)/shard_map/pallas_call | solution.py:324
  55.0 5.9 %all-to-all-start.2 = ((bf16[8,256,128]{2,1,0:T(8,128)(2,1)}), bf16[8,256,128]{2,1,0:T(8,128)(2,1)S(1)}, u32[]{:S(2)}, u32[]{:S(2)}) async-start(bf16[8,256,128]{2,1,0:T(8,128)(2,1)} %shard_map.133), calls=%async_computation.2 | async-start | bytes 1048576 | tf_op jit(solution)/shard_map/all_to_all | solution.py:296
  60.9 2.2 collective-permute-start.3
  63.1 2.8 %collective-permute-start.2 = (bf16[256,256]{1,0:T(8,128)(2,1)S(1)}, bf16[256,256]{1,0:T(8,128)(2,1)S(1)}, u32[]{:S(2)}, u32[]{:S(2)}) collective-permute-start(bf16[256,256]{1,0:T(8,128)(2,1)S(1)} %collective-permute-done._.own_ref), channel_id=1, source_target_pairs={{0,8},{8,0},{1,9},{9,1},{2,10},{10,2},{3,11},{11,3},{4,12},{12,4},... | collective-permute-start | bytes 393224 | tf_op jit(solution)/shard_map/ppermute | solution.py:327
  66.0 1.3 collective-permute-done.3.x_ref
  67.3 3.3 %collective-permute-start.4 = (bf16[256,256]{1,0:T(8,128)(2,1)S(1)}, bf16[256,256]{1,0:T(8,128)(2,1)S(1)}, u32[]{:S(2)}, u32[]{:S(2)}) collective-permute-start(bf16[256,256]{1,0:T(8,128)(2,1)S(1)} %collective-permute-done.3.x_ref), channel_id=1, source_target_pairs={{0,8},{8,0},{1,9},{9,1},{2,10},{10,2},{3,11},{11,3},{4,12},{12,4},... | collective-permute-start | bytes 393224 | tf_op jit(solution)/shard_map/ppermute | solution.py:327
  70.6 0.3 shard_map.134.route_ref
  70.9 0.0 copy-start.8
  70.9 0.6 collective-permute-done.4.x_core_ref
  71.6 7.3 %all-to-all-done.2.att_ref = bf16[8,256,128]{2,1,0:T(8,128)(2,1)S(1)} async-done(((bf16[8,256,128]{2,1,0:T(8,128)(2,1)}), bf16[8,256,128]{2,1,0:T(8,128)(2,1)S(1)}, u32[]{:S(2)}, u32[]{:S(2)}) %all-to-all-start.2) | async-done | bytes 524320 | tf_op jit(solution)/shard_map/all_to_all | solution.py:296
  78.9 1.6 shard_map.135
  80.5 4.6 %all-to-all-start.4 = ((bf16[64,16,256]{2,1,0:T(8,128)(2,1)}), bf16[64,16,256]{2,1,0:T(8,128)(2,1)S(1)}, u32[]{:S(2)}, u32[]{:S(2)}) async-start(bf16[64,16,256]{2,1,0:T(8,128)(2,1)} %get-tuple-element.20), calls=%async_computation.4 | async-start | bytes 1048576 | tf_op jit(solution)/shard_map/all_to_all | solution.py:296
  85.1 0.0 all-gather.6.cloned.1.call-start
  85.1 3.4 %all-gather.4.cloned.1.call-done.down_hbm = bf16[8,176,2048]{2,1,0:T(8,128)(2,1)} async-done(((bf16[1,176,2048]{2,1,0:T(8,128)(2,1)}), bf16[8,176,2048]{2,1,0:T(8,128)(2,1)}) %all-gather.4.cloned.1.call-update) | async-done | bytes 5767184 | tf_op jit(solution)/shard_map/all_gather | solution.py:298
  88.5 1.3 slice.4
  90.5 11.9 %all-to-all-done.4 = bf16[64,16,256]{2,1,0:T(8,128)(2,1)S(1)} async-done(((bf16[64,16,256]{2,1,0:T(8,128)(2,1)}), bf16[64,16,256]{2,1,0:T(8,128)(2,1)S(1)}, u32[]{:S(2)}, u32[]{:S(2)}) %all-to-all-start.4) | async-done | bytes 524320 | tf_op jit(solution)/shard_map/all_to_all | solution.py:296
  102.4 0.9 broadcast_add_fusion
  103.3 0.0 all-gather.6.cloned.1.call-update
  103.3 0.3 copy.16.router_ref
  103.6 0.1 copy.17.ids_ref
  103.7 4.1 %all-to-all-start.3 = ((bf16[8,32,256]{2,1,0:T(8,128)(2,1)}), bf16[8,32,256]{2,1,0:T(8,128)(2,1)S(1)}, u32[]{:S(2)}, u32[]{:S(2)}) async-start(bf16[8,32,256]{2,1,0:T(8,128)(2,1)} %get-tuple-element.15), calls=%async_computation.3 | async-start | bytes 262144 | tf_op jit(solution)/shard_map/all_to_all | solution.py:296
  107.8 1.4 pad_maximum_fusion.weight_ref
  109.2 6.4 %all-to-all-done.3.projected_ref = bf16[8,32,256]{2,1,0:T(8,128)(2,1)S(1)} async-done(((bf16[8,32,256]{2,1,0:T(8,128)(2,1)}), bf16[8,32,256]{2,1,0:T(8,128)(2,1)S(1)}, u32[]{:S(2)}, u32[]{:S(2)}) %all-to-all-start.3) | async-done | bytes 131104 | tf_op jit(solution)/shard_map/all_to_all | solution.py:296
  115.6 2.6 %copy-done.1 = bf16[8,176,2048]{2,1,0:T(8,128)(2,1)S(1)} copy-done((bf16[8,176,2048]{2,1,0:T(8,128)(2,1)S(1)}, bf16[8,176,2048]{2,1,0:T(8,128)(2,1)}, u32[]{:S(2)}) %copy-start.1) | copy-done | bytes 5767192
  118.3 0.8 shard_map.136
  119.1 2.5 %copy-done.2 = bf16[8,176,2048]{2,1,0:T(8,128)(2,1)} copy-done((bf16[8,176,2048]{2,1,0:T(8,128)(2,1)}, bf16[8,176,2048]{2,1,0:T(8,128)(2,1)S(1)}, u32[]{:S(2)}) %copy-start.2) | copy-done | bytes 5767192
  121.6 36.6 %all-gather.6.cloned.1.call-done = bf16[512,16,256]{2,1,0:T(8,128)(2,1)} async-done(((bf16[64,16,256]{2,1,0:T(8,128)(2,1)}), bf16[512,16,256]{2,1,0:T(8,128)(2,1)}) %all-gather.6.cloned.1.call-update) | async-done | bytes 4194320 | tf_op jit(solution)/shard_map/all_gather | solution.py:338
  158.2 2.2 copy-done.4
  160.4 3.1 %shard_map.137 = bf16[8,176,128]{2,1,0:T(8,128)(2,1)S(1)} custom-call(bf16[8,4,8,2,16,256]{5,4,3,2,1,0:T(8,128)(2,1)S(1)} %bitcast.20, f32[8,256]{1,0:T(8,128)S(1)} %reshape.27.inverse_ref, bf16[352,2048]{1,0:T(8,128)(2,1)S(1)} %pad_maximum_fusion.weight_ref, f32[32,2]{1,0:T(8,128)S(1)} %get-tuple-element.17._.gates_ref), custom_call_target="tpu_custom_call" | custom-call | tf_op jit(solution)/shard_map/pallas_call | solution.py:238
  163.5 16.9 %all_to_all.36.active_ref = bf16[8,176,128]{2,1,0:T(8,128)(2,1)S(1)} all-to-all(bf16[8,176,128]{2,1,0:T(8,128)(2,1)S(1)} %shard_map.137), channel_id=1, replica_groups=mesh['x'=4,'z'=8,'c'=2,'y'=8] {'y'}, dimensions={0} | all-to-all | bytes 720896 | tf_op jit(solution)/shard_map/all_to_all | solution.py:296
  180.4 1.1 shard_map.138
  181.5 0.3 reshape.28
  181.9 29.5 %all_to_all.37 = bf16[64,2,2048]{2,1,0:T(2,128)(2,1)S(1)} all-to-all(bf16[64,2,2048]{2,1,0:T(2,128)(2,1)S(1)} %reshape.28), channel_id=1, replica_groups=mesh['x'=4,'z'=8,'c'=2,'y'=8] {'x','z','c'}, dimensions={0} | all-to-all | bytes 1048576 | tf_op jit(solution)/shard_map/all_to_all | solution.py:296
  211.3 0.2 reshape.29.rows_ref
  211.5 0.9 shard_map.139
  (19 shorter events, 0.1 us)
Async XLA Ops:
  7.2 14.2 %copy-start = (bf16[1024,256]{1,0:T(8,128)(2,1)S(1)}, bf16[1024,256]{1,0:T(8,128)(2,1)}, u32[]{:S(2)}) copy-start(bf16[1024,256]{1,0:T(8,128)(2,1)} %param.17) | copy-start | bytes 1572868
  7.2 81.3 %all-gather.4.cloned.1.call-start = ((), (), s32[]{:S(2)}) async-start(), calls=%async_computation.7 | async-start | bytes 6488064 | tf_op jit(solution)/shard_map/all_gather | solution.py:298
  10.5 41.6 %copy-start.7 = (s32[16,16]{1,0:T(8,128)S(1)}, s32[16,16]{1,0:T(8,128)}, u32[]{:S(2)}) copy-start(s32[16,16]{1,0:T(8,128)} %get-tuple-element.12.mask_ref) | copy-start | bytes 3076
  10.5 52.6 %copy-start.6 = (f32[2048]{0:T(1024)S(1)}, f32[2048]{0:T(1024)}, u32[]{:S(2)}) copy-start(f32[2048]{0:T(1024)} %param.18) | copy-start | bytes 24580
  10.5 23.8 %all-to-all-start = ((bf16[8,176,128]{2,1,0:T(8,128)(2,1)}), bf16[8,176,128]{2,1,0:T(8,128)(2,1)S(1)}, u32[]{:S(2)}, u32[]{:S(2)}) async-start(bf16[8,176,128]{2,1,0:T(8,128)(2,1)} %get-tuple-element.13), calls=%async_computation | async-start | bytes 720896 | tf_op jit(solution)/shard_map/all_to_all | solution.py:296
  21.4 0.7 collective-permute-start
  45.2 6.9 %collective-permute-start.1 = (bf16[32,64,128]{2,1,0:T(8,128)(2,1)S(1)}, bf16[32,64,128]{2,1,0:T(8,128)(2,1)S(1)}, u32[]{:S(2)}, u32[]{:S(2)}) collective-permute-start(bf16[32,64,128]{2,1,0:T(8,128)(2,1)S(1)} %bitcast.21), channel_id=1, source_target_pairs={{0,8},{8,0},{1,9},{9,1},{2,10},{10,2},{3,11},{11,3},{4,12},{12,4},... | collective-permute-start | bytes 1572872 | tf_op jit(solution)/shard_map/ppermute | solution.py:323
  55.0 23.8 %all-to-all-start.2 = ((bf16[8,256,128]{2,1,0:T(8,128)(2,1)}), bf16[8,256,128]{2,1,0:T(8,128)(2,1)S(1)}, u32[]{:S(2)}, u32[]{:S(2)}) async-start(bf16[8,256,128]{2,1,0:T(8,128)(2,1)} %shard_map.133), calls=%async_computation.2 | async-start | bytes 1048576 | tf_op jit(solution)/shard_map/all_to_all | solution.py:296
  60.9 6.4 %collective-permute-start.3 = (bf16[256,256]{1,0:T(8,128)(2,1)S(1)}, bf16[256,256]{1,0:T(8,128)(2,1)S(1)}, u32[]{:S(2)}, u32[]{:S(2)}) collective-permute-start(bf16[256,256]{1,0:T(8,128)(2,1)S(1)} %collective-permute-done._.own_ref), channel_id=1, source_target_pairs={{0,128},{128,0},{256,384},{384,256},{1,129},{129,1},{257,385},{385... | collective-permute-start | bytes 393224 | tf_op jit(solution)/shard_map/ppermute | solution.py:325
  63.1 7.8 %collective-permute-start.2 = (bf16[256,256]{1,0:T(8,128)(2,1)S(1)}, bf16[256,256]{1,0:T(8,128)(2,1)S(1)}, u32[]{:S(2)}, u32[]{:S(2)}) collective-permute-start(bf16[256,256]{1,0:T(8,128)(2,1)S(1)} %collective-permute-done._.own_ref), channel_id=1, source_target_pairs={{0,8},{8,0},{1,9},{9,1},{2,10},{10,2},{3,11},{11,3},{4,12},{12,4},... | collective-permute-start | bytes 393224 | tf_op jit(solution)/shard_map/ppermute | solution.py:327
  67.3 4.3 %collective-permute-start.4 = (bf16[256,256]{1,0:T(8,128)(2,1)S(1)}, bf16[256,256]{1,0:T(8,128)(2,1)S(1)}, u32[]{:S(2)}, u32[]{:S(2)}) collective-permute-start(bf16[256,256]{1,0:T(8,128)(2,1)S(1)} %collective-permute-done.3.x_ref), channel_id=1, source_target_pairs={{0,8},{8,0},{1,9},{9,1},{2,10},{10,2},{3,11},{11,3},{4,12},{12,4},... | collective-permute-start | bytes 393224 | tf_op jit(solution)/shard_map/ppermute | solution.py:327
  70.9 32.4 %copy-start.8 = (bf16[2048,64]{0,1:T(8,128)(2,1)S(1)}, bf16[2048,64]{0,1:T(8,128)(2,1)}, u32[]{:S(2)}) copy-start(bf16[2048,64]{0,1:T(8,128)(2,1)} %param.19) | copy-start | bytes 786436
  70.9 32.7 %copy-start.9 = (s32[1,32,2]{1,2,0:T(2,128)S(1)}, s32[1,32,2]{1,2,0:T(2,128)}, u32[]{:S(2)}) copy-start(s32[1,32,2]{1,2,0:T(2,128)} %param.20) | copy-start | bytes 772
  80.5 21.9 %all-to-all-start.4 = ((bf16[64,16,256]{2,1,0:T(8,128)(2,1)}), bf16[64,16,256]{2,1,0:T(8,128)(2,1)S(1)}, u32[]{:S(2)}, u32[]{:S(2)}) async-start(bf16[64,16,256]{2,1,0:T(8,128)(2,1)} %get-tuple-element.20), calls=%async_computation.4 | async-start | bytes 1048576 | tf_op jit(solution)/shard_map/all_to_all | solution.py:296
  85.0 30.6 %copy-start.5 = (bf16[1,32,2048]{2,1,0:T(8,128)(2,1)S(1)}, bf16[1,32,2048]{2,1,0:T(8,128)(2,1)}, u32[]{:S(2)}) copy-start(bf16[1,32,2048]{2,1,0:T(8,128)(2,1)} %param.12) | copy-start | bytes 393220
  85.1 73.1 %all-gather.6.cloned.1.call-start = ((), (), s32[]{:S(2)}) async-start(), calls=%async_computation.8 | async-start | bytes 4718592 | tf_op jit(solution)/shard_map/all_gather | solution.py:338
  103.7 11.9 %all-to-all-start.3 = ((bf16[8,32,256]{2,1,0:T(8,128)(2,1)}), bf16[8,32,256]{2,1,0:T(8,128)(2,1)S(1)}, u32[]{:S(2)}, u32[]{:S(2)}) async-start(bf16[8,32,256]{2,1,0:T(8,128)(2,1)} %get-tuple-element.15), calls=%async_computation.3 | async-start | bytes 262144 | tf_op jit(solution)/shard_map/all_to_all | solution.py:296
  115.6 2.6 %copy-start.1 = (bf16[8,176,2048]{2,1,0:T(8,128)(2,1)S(1)}, bf16[8,176,2048]{2,1,0:T(8,128)(2,1)}, u32[]{:S(2)}) copy-start(bf16[8,176,2048]{2,1,0:T(8,128)(2,1)} %all-gather.4.cloned.1.call-done.down_hbm) | copy-start | bytes 17301508
  119.1 2.5 %copy-start.2 = (bf16[8,176,2048]{2,1,0:T(8,128)(2,1)}, bf16[8,176,2048]{2,1,0:T(8,128)(2,1)S(1)}, u32[]{:S(2)}) copy-start(bf16[8,176,2048]{2,1,0:T(8,128)(2,1)S(1)} %get-tuple-element.21.down_ref) | copy-start | bytes 17301508
  158.2 2.2 copy-start.4
  160.4 20.1 %copy-start.3 = (bf16[8,176,2048]{2,1,0:T(8,128)(2,1)S(1)}, bf16[8,176,2048]{2,1,0:T(8,128)(2,1)}, u32[]{:S(2)}) copy-start(bf16[8,176,2048]{2,1,0:T(8,128)(2,1)} %copy-done.2) | copy-start | bytes 17301508
Sparse Core Ops, SparseCore 0:
  10.1 78.3 all-gather.3
  103.4 54.7 all-gather.5

commit v5 on v4

--- a/solution.py
+++ b/solution.py
@@ -121,21 +121,23 @@
     seen = jnp.dot(live, key_onehot, preferred_element_type=F32)
     seen_row = lax.broadcasted_iota(jnp.int32, (16, n_key), 0)
     scale = HEAD ** (-0.5)
-    for j in range(4):
-        mine = jnp.sum(jnp.where(seen_row == x * 4 + j, seen, 0.0), axis=0, keepdims=True)
-        rows = packed_ref[2 * j : 2 * j + 2, :TOK].reshape(2 * TOK, HEAD)
-        row = lax.broadcasted_iota(jnp.int32, (2 * TOK, 1), 0)
-        query_pos = x * 512 + (2 * j + row // 32) * 64 + c * 32 + row % 32
-        allowed = (jnp.broadcast_to(mine, (2 * TOK, n_key)) > 0.5) & (key_pos <= query_pos)
-        scores = lax.dot_general(rows, keys, (((1,), (1,)), ((), ())), preferred_element_type=F32)
-        scores = jnp.where(allowed, scores * scale, -1e30)
-        top = jnp.max(scores, axis=-1, keepdims=True)
-        weights = jnp.exp(scores - top)
-        total = jnp.sum(weights, axis=-1, keepdims=True)
-        update = jnp.dot(weights.astype(BF16), values, preferred_element_type=F32)
-        attended = (update / total).astype(BF16)
-        for z in range(8):
-            out_ref[z, 2 * j * TOK : 2 * (j + 1) * TOK] = attended
+    mine = [
+        jnp.sum(jnp.where(seen_row == x * 4 + j, seen, 0.0), axis=0, keepdims=True) for j in range(4)
+    ]
+    mine = jnp.concatenate([jnp.broadcast_to(m, (2 * TOK, n_key)) for m in mine], axis=0)
+    rows = packed_ref[:, :TOK].reshape(8 * TOK, HEAD)
+    row = lax.broadcasted_iota(jnp.int32, (8 * TOK, 1), 0)
+    query_pos = x * 512 + row // 32 * 64 + c * 32 + row % 32
+    allowed = (mine > 0.5) & (key_pos <= query_pos)
+    scores = lax.dot_general(rows, keys, (((1,), (1,)), ((), ())), preferred_element_type=F32)
+    scores = jnp.where(allowed, scores * scale, -1e30)
+    top = jnp.max(scores, axis=-1, keepdims=True)
+    weights = jnp.exp(scores - top)
+    total = jnp.sum(weights, axis=-1, keepdims=True)
+    update = jnp.dot(weights.astype(BF16), values, preferred_element_type=F32)
+    attended = (update / total).astype(BF16)
+    for z in range(8):
+        out_ref[z] = attended
 
 
 def route_kernel(packed_ref, out_ref):
@@ -246,7 +248,7 @@
         ],
         out_specs=pl.BlockSpec((step, width, 128), lambda i: (i, 0, 0)),
         out_shape=jax.ShapeDtypeStruct((8, width, 128), BF16),
-        compiler_params=pltpu.CompilerParams(vmem_limit_bytes=48 * 1024 * 1024),
+        compiler_params=pltpu.CompilerParams(vmem_limit_bytes=51 * 1024 * 1024),
     )(rows, inverse, weight, after)
 
 

time: 220 us -> 219 us (level)
  local copies, waits for them, and re-layouts: 9.56 us -> 7.28 us
    unnamed x21 -> x19, local copies, waits for them, and re-layouts: 7.64 us -> 5.44 us
  transfers between devices with their start and end apart: 11 -> 11, of which waited for: 9 -> 9; matrix products, arithmetic and copies ran while one was open for 1% -> 1% of each run, Pallas kernels for 4% -> 3%
where the time goes in v5:
time: 219 us; the launch traced here: 218 us
  waiting for transfers between devices  82.1 us (37%)
  blocking collectives  57.2 us (26%)
  starting transfers between devices  39.8 us (18%)
  between operations  14.9 us (7%)
  Pallas kernels  14.7 us (7%)
  local copies, waits for them, and re-layouts  7.28 us (3%)
  other arithmetic  2.28 us (1%)
    all_to_all x3, blocking collectives, shards(): lax.all_to_all(a, axes, split_axis=0, concat_axis=0, tiled=True)  57.2 us
    all_to_all x4, waiting for transfers between devices, shards(): lax.all_to_all(a, axes, split_axis=0, concat_axis=0, tiled=True)  37.2 us
    all_gather x1, waiting for transfers between devices, shards(): rows = lax.all_gather(arrived, 'y', axis=0)  36.6 us
    all_to_all x4, starting transfers between devices, shards(): lax.all_to_all(a, axes, split_axis=0, concat_axis=0, tiled=True)  25.4 us
    unnamed x19, local copies, waits for them, and re-layouts  5.44 us
    ppermute x1, starting transfers between devices, shards(): other_kv = lax.ppermute(kv, 'c', other_core)  5.35 us
    pallas_call x1, Pallas kernels, expert_call(): pl.pallas_call(expert_kernel, grid=(8 // step,), in_specs=[pl.BlockSpec((...  5.12 us
  transfers between devices with their start and end apart: 11, of which 9 were waited for; matrix products, arithmetic and copies ran while one was open for 1% of the time, Pallas kernels for 3%

profile of v5, /device:TPU:1, one launch (start us, length us, event | category | flops | bytes accessed | tf_op | source)
XLA Modules:
  0.0 218.3 jit_solution(14849519333444960117)
XLA Ops:
  7.2 0.0 copy-start
  7.2 0.0 all-gather.4.cloned.1.call-start
  7.2 0.7 all-gather.4.cloned.1.call-update
  7.9 2.6 %shard_map.131 = (bf16[8,176,128]{2,1,0:T(8,128)(2,1)}, s32[16,16]{1,0:T(8,128)}) custom-call(s32[16,16]{1,0:T(8,128)} %bitcast.32, bf16[32,1024]{1,0:T(8,128)(2,1)} %bitcast.29, bf16[32,1024]{1,0:T(8,128)(2,1)} %bitcast.30, bf16[32,1024]{1,0:T(8,128)(2,1)} %bitcast.31, bf16[32,2048]{1,0:T(8,128)(2,1)} %bitcast.22, s32[2,32]{1,0:T(2,128)} %bitcast.33), custom_call_target="tpu_custom_call" | custom-call | tf_op jit(solution)/shard_map/pallas_call | solution.py:308
  10.5 0.0 copy-start.6
  10.5 0.0 copy-start.5
  10.5 10.9 %all-to-all-start = ((bf16[8,176,128]{2,1,0:T(8,128)(2,1)}), bf16[8,176,128]{2,1,0:T(8,128)(2,1)S(1)}, u32[]{:S(2)}, u32[]{:S(2)}) async-start(bf16[8,176,128]{2,1,0:T(8,128)(2,1)} %get-tuple-element.13), calls=%async_computation | async-start | bytes 720896 | tf_op jit(solution)/shard_map/all_to_all | solution.py:298
  21.4 0.7 collective-permute-start
  22.1 12.2 %all-to-all-done.packed_ref = bf16[8,176,128]{2,1,0:T(8,128)(2,1)S(1)} async-done(((bf16[8,176,128]{2,1,0:T(8,128)(2,1)}), bf16[8,176,128]{2,1,0:T(8,128)(2,1)S(1)}, u32[]{:S(2)}, u32[]{:S(2)}) %all-to-all-start) | async-done | bytes 360480 | tf_op jit(solution)/shard_map/all_to_all | solution.py:298
  34.3 0.1 shard_map.132
  34.4 10.8 %all_to_all.35 = bf16[4,8,64,128]{3,2,1,0:T(8,128)(2,1)S(1)} all-to-all(bf16[4,8,64,128]{3,2,1,0:T(8,128)(2,1)S(1)} %shard_map.132), channel_id=1, replica_groups=mesh['x'=4,'z'=8,'c'=2,'y'=8] {'x'}, dimensions={0} | all-to-all | bytes 1048576 | tf_op jit(solution)/shard_map/all_to_all | solution.py:298
  45.2 5.3 %collective-permute-start.1 = (bf16[32,64,128]{2,1,0:T(8,128)(2,1)S(1)}, bf16[32,64,128]{2,1,0:T(8,128)(2,1)S(1)}, u32[]{:S(2)}, u32[]{:S(2)}) collective-permute-start(bf16[32,64,128]{2,1,0:T(8,128)(2,1)S(1)} %bitcast.20), channel_id=1, source_target_pairs={{0,8},{8,0},{1,9},{9,1},{2,10},{10,2},{3,11},{11,3},{4,12},{12,4},... | collective-permute-start | bytes 1572872 | tf_op jit(solution)/shard_map/ppermute | solution.py:325
  50.5 1.5 collective-permute-done.1.other_ref
  52.0 2.2 shard_map.133
  54.2 5.8 %all-to-all-start.2 = ((bf16[8,256,128]{2,1,0:T(8,128)(2,1)}), bf16[8,256,128]{2,1,0:T(8,128)(2,1)S(1)}, u32[]{:S(2)}, u32[]{:S(2)}) async-start(bf16[8,256,128]{2,1,0:T(8,128)(2,1)} %shard_map.133), calls=%async_computation.2 | async-start | bytes 1048576 | tf_op jit(solution)/shard_map/all_to_all | solution.py:298
  60.1 2.2 %collective-permute-start.3 = (bf16[256,256]{1,0:T(8,128)(2,1)S(1)}, bf16[256,256]{1,0:T(8,128)(2,1)S(1)}, u32[]{:S(2)}, u32[]{:S(2)}) collective-permute-start(bf16[256,256]{1,0:T(8,128)(2,1)S(1)} %collective-permute-done._.own_ref), channel_id=1, source_target_pairs={{0,128},{128,0},{256,384},{384,256},{1,129},{129,1},{257,385},{385... | collective-permute-start | bytes 393224 | tf_op jit(solution)/shard_map/ppermute | solution.py:327
  62.3 2.8 %collective-permute-start.2 = (bf16[256,256]{1,0:T(8,128)(2,1)S(1)}, bf16[256,256]{1,0:T(8,128)(2,1)S(1)}, u32[]{:S(2)}, u32[]{:S(2)}) collective-permute-start(bf16[256,256]{1,0:T(8,128)(2,1)S(1)} %collective-permute-done._.own_ref), channel_id=1, source_target_pairs={{0,8},{8,0},{1,9},{9,1},{2,10},{10,2},{3,11},{11,3},{4,12},{12,4},... | collective-permute-start | bytes 393224 | tf_op jit(solution)/shard_map/ppermute | solution.py:329
  65.1 1.3 collective-permute-done.3.x_ref
  66.4 3.3 %collective-permute-start.4 = (bf16[256,256]{1,0:T(8,128)(2,1)S(1)}, bf16[256,256]{1,0:T(8,128)(2,1)S(1)}, u32[]{:S(2)}, u32[]{:S(2)}) collective-permute-start(bf16[256,256]{1,0:T(8,128)(2,1)S(1)} %collective-permute-done.3.x_ref), channel_id=1, source_target_pairs={{0,8},{8,0},{1,9},{9,1},{2,10},{10,2},{3,11},{11,3},{4,12},{12,4},... | collective-permute-start | bytes 393224 | tf_op jit(solution)/shard_map/ppermute | solution.py:329
  69.8 0.3 shard_map.134.route_ref
  70.1 0.0 copy-start.7
  70.1 0.6 collective-permute-done.4.x_core_ref
  70.7 7.3 %all-to-all-done.2.att_ref = bf16[8,256,128]{2,1,0:T(8,128)(2,1)S(1)} async-done(((bf16[8,256,128]{2,1,0:T(8,128)(2,1)}), bf16[8,256,128]{2,1,0:T(8,128)(2,1)S(1)}, u32[]{:S(2)}, u32[]{:S(2)}) %all-to-all-start.2) | async-done | bytes 524320 | tf_op jit(solution)/shard_map/all_to_all | solution.py:298
  78.0 1.6 shard_map.135
  79.6 4.6 %all-to-all-start.4 = ((bf16[64,16,256]{2,1,0:T(8,128)(2,1)}), bf16[64,16,256]{2,1,0:T(8,128)(2,1)S(1)}, u32[]{:S(2)}, u32[]{:S(2)}) async-start(bf16[64,16,256]{2,1,0:T(8,128)(2,1)} %get-tuple-element.20), calls=%async_computation.4 | async-start | bytes 1048576 | tf_op jit(solution)/shard_map/all_to_all | solution.py:298
  84.2 0.0 copy-start.4
  84.2 0.0 all-gather.6.cloned.1.call-start
  84.3 4.2 %all-gather.4.cloned.1.call-done.down_hbm = bf16[8,176,2048]{2,1,0:T(8,128)(2,1)} async-done(((bf16[1,176,2048]{2,1,0:T(8,128)(2,1)}), bf16[8,176,2048]{2,1,0:T(8,128)(2,1)}) %all-gather.4.cloned.1.call-update) | async-done | bytes 5767184 | tf_op jit(solution)/shard_map/all_gather | solution.py:300
  88.5 1.2 slice.4
  90.3 11.2 %all-to-all-done.4 = bf16[64,16,256]{2,1,0:T(8,128)(2,1)S(1)} async-done(((bf16[64,16,256]{2,1,0:T(8,128)(2,1)}), bf16[64,16,256]{2,1,0:T(8,128)(2,1)S(1)}, u32[]{:S(2)}, u32[]{:S(2)}) %all-to-all-start.4) | async-done | bytes 524320 | tf_op jit(solution)/shard_map/all_to_all | solution.py:298
  101.6 0.9 broadcast_add_fusion
  102.4 0.0 all-gather.6.cloned.1.call-update
  102.5 0.3 copy.16.router_ref
  102.7 0.1 copy.17.ids_ref
  102.8 4.1 %all-to-all-start.3 = ((bf16[8,32,256]{2,1,0:T(8,128)(2,1)}), bf16[8,32,256]{2,1,0:T(8,128)(2,1)S(1)}, u32[]{:S(2)}, u32[]{:S(2)}) async-start(bf16[8,32,256]{2,1,0:T(8,128)(2,1)} %get-tuple-element.15), calls=%async_computation.3 | async-start | bytes 262144 | tf_op jit(solution)/shard_map/all_to_all | solution.py:298
  106.9 1.4 pad_maximum_fusion.weight_ref
  108.4 6.4 %all-to-all-done.3.projected_ref = bf16[8,32,256]{2,1,0:T(8,128)(2,1)S(1)} async-done(((bf16[8,32,256]{2,1,0:T(8,128)(2,1)}), bf16[8,32,256]{2,1,0:T(8,128)(2,1)S(1)}, u32[]{:S(2)}, u32[]{:S(2)}) %all-to-all-start.3) | async-done | bytes 131104 | tf_op jit(solution)/shard_map/all_to_all | solution.py:298
  114.8 2.6 %copy-done.1 = bf16[8,176,2048]{2,1,0:T(8,128)(2,1)S(1)} copy-done((bf16[8,176,2048]{2,1,0:T(8,128)(2,1)S(1)}, bf16[8,176,2048]{2,1,0:T(8,128)(2,1)}, u32[]{:S(2)}) %copy-start.1) | copy-done | bytes 5767192
  117.4 0.8 shard_map.136
  118.2 2.5 %copy-done.2 = bf16[8,176,2048]{2,1,0:T(8,128)(2,1)} copy-done((bf16[8,176,2048]{2,1,0:T(8,128)(2,1)}, bf16[8,176,2048]{2,1,0:T(8,128)(2,1)S(1)}, u32[]{:S(2)}) %copy-start.2) | copy-done | bytes 5767192
  120.7 36.6 %all-gather.6.cloned.1.call-done = bf16[512,16,256]{2,1,0:T(8,128)(2,1)} async-done(((bf16[64,16,256]{2,1,0:T(8,128)(2,1)}), bf16[512,16,256]{2,1,0:T(8,128)(2,1)}) %all-gather.6.cloned.1.call-update) | async-done | bytes 4194320 | tf_op jit(solution)/shard_map/all_gather | solution.py:340
  157.3 5.1 %shard_map.137 = bf16[8,176,128]{2,1,0:T(8,128)(2,1)S(1)} custom-call(bf16[8,4,8,2,16,256]{5,4,3,2,1,0:T(8,128)(2,1)} %bitcast.25, f32[8,256]{1,0:T(8,128)S(1)} %reshape.27.inverse_ref, bf16[352,2048]{1,0:T(8,128)(2,1)S(1)} %pad_maximum_fusion.weight_ref, f32[32,2]{1,0:T(8,128)S(1)} %get-tuple-element.17._.gates_ref), custom_call_target="tpu_custom_call" | custom-call | tf_op jit(solution)/shard_map/pallas_call | solution.py:240
  162.4 16.9 %all_to_all.36.active_ref = bf16[8,176,128]{2,1,0:T(8,128)(2,1)S(1)} all-to-all(bf16[8,176,128]{2,1,0:T(8,128)(2,1)S(1)} %shard_map.137), channel_id=1, replica_groups=mesh['x'=4,'z'=8,'c'=2,'y'=8] {'y'}, dimensions={0} | all-to-all | bytes 720896 | tf_op jit(solution)/shard_map/all_to_all | solution.py:298
  179.4 1.1 shard_map.138
  180.5 0.3 reshape.28
  180.8 29.5 %all_to_all.37 = bf16[64,2,2048]{2,1,0:T(2,128)(2,1)S(1)} all-to-all(bf16[64,2,2048]{2,1,0:T(2,128)(2,1)S(1)} %reshape.28), channel_id=1, replica_groups=mesh['x'=4,'z'=8,'c'=2,'y'=8] {'x','z','c'}, dimensions={0} | all-to-all | bytes 1048576 | tf_op jit(solution)/shard_map/all_to_all | solution.py:298
  210.3 0.2 reshape.29.rows_ref
  210.5 0.9 shard_map.139
  (17 shorter events, 0.1 us)
Async XLA Ops:
  7.2 14.2 %copy-start = (bf16[1024,256]{1,0:T(8,128)(2,1)S(1)}, bf16[1024,256]{1,0:T(8,128)(2,1)}, u32[]{:S(2)}) copy-start(bf16[1024,256]{1,0:T(8,128)(2,1)} %param.17) | copy-start | bytes 1572868
  7.2 81.3 %all-gather.4.cloned.1.call-start = ((), (), s32[]{:S(2)}) async-start(), calls=%async_computation.7 | async-start | bytes 6488064 | tf_op jit(solution)/shard_map/all_gather | solution.py:300
  10.5 41.6 %copy-start.6 = (s32[16,16]{1,0:T(8,128)S(1)}, s32[16,16]{1,0:T(8,128)}, u32[]{:S(2)}) copy-start(s32[16,16]{1,0:T(8,128)} %get-tuple-element.12.mask_ref) | copy-start | bytes 3076
  10.5 51.8 %copy-start.5 = (f32[2048]{0:T(1024)S(1)}, f32[2048]{0:T(1024)}, u32[]{:S(2)}) copy-start(f32[2048]{0:T(1024)} %param.18) | copy-start | bytes 24580
  10.5 23.8 %all-to-all-start = ((bf16[8,176,128]{2,1,0:T(8,128)(2,1)}), bf16[8,176,128]{2,1,0:T(8,128)(2,1)S(1)}, u32[]{:S(2)}, u32[]{:S(2)}) async-start(bf16[8,176,128]{2,1,0:T(8,128)(2,1)} %get-tuple-element.13), calls=%async_computation | async-start | bytes 720896 | tf_op jit(solution)/shard_map/all_to_all | solution.py:298
  21.4 0.7 collective-permute-start
  45.2 6.9 %collective-permute-start.1 = (bf16[32,64,128]{2,1,0:T(8,128)(2,1)S(1)}, bf16[32,64,128]{2,1,0:T(8,128)(2,1)S(1)}, u32[]{:S(2)}, u32[]{:S(2)}) collective-permute-start(bf16[32,64,128]{2,1,0:T(8,128)(2,1)S(1)} %bitcast.20), channel_id=1, source_target_pairs={{0,8},{8,0},{1,9},{9,1},{2,10},{10,2},{3,11},{11,3},{4,12},{12,4},... | collective-permute-start | bytes 1572872 | tf_op jit(solution)/shard_map/ppermute | solution.py:325
  54.2 23.8 %all-to-all-start.2 = ((bf16[8,256,128]{2,1,0:T(8,128)(2,1)}), bf16[8,256,128]{2,1,0:T(8,128)(2,1)S(1)}, u32[]{:S(2)}, u32[]{:S(2)}) async-start(bf16[8,256,128]{2,1,0:T(8,128)(2,1)} %shard_map.133), calls=%async_computation.2 | async-start | bytes 1048576 | tf_op jit(solution)/shard_map/all_to_all | solution.py:298
  60.1 6.4 %collective-permute-start.3 = (bf16[256,256]{1,0:T(8,128)(2,1)S(1)}, bf16[256,256]{1,0:T(8,128)(2,1)S(1)}, u32[]{:S(2)}, u32[]{:S(2)}) collective-permute-start(bf16[256,256]{1,0:T(8,128)(2,1)S(1)} %collective-permute-done._.own_ref), channel_id=1, source_target_pairs={{0,128},{128,0},{256,384},{384,256},{1,129},{129,1},{257,385},{385... | collective-permute-start | bytes 393224 | tf_op jit(solution)/shard_map/ppermute | solution.py:327
  62.3 7.8 %collective-permute-start.2 = (bf16[256,256]{1,0:T(8,128)(2,1)S(1)}, bf16[256,256]{1,0:T(8,128)(2,1)S(1)}, u32[]{:S(2)}, u32[]{:S(2)}) collective-permute-start(bf16[256,256]{1,0:T(8,128)(2,1)S(1)} %collective-permute-done._.own_ref), channel_id=1, source_target_pairs={{0,8},{8,0},{1,9},{9,1},{2,10},{10,2},{3,11},{11,3},{4,12},{12,4},... | collective-permute-start | bytes 393224 | tf_op jit(solution)/shard_map/ppermute | solution.py:329
  66.4 4.3 %collective-permute-start.4 = (bf16[256,256]{1,0:T(8,128)(2,1)S(1)}, bf16[256,256]{1,0:T(8,128)(2,1)S(1)}, u32[]{:S(2)}, u32[]{:S(2)}) collective-permute-start(bf16[256,256]{1,0:T(8,128)(2,1)S(1)} %collective-permute-done.3.x_ref), channel_id=1, source_target_pairs={{0,8},{8,0},{1,9},{9,1},{2,10},{10,2},{3,11},{11,3},{4,12},{12,4},... | collective-permute-start | bytes 393224 | tf_op jit(solution)/shard_map/ppermute | solution.py:329
  70.1 32.4 %copy-start.7 = (bf16[2048,64]{0,1:T(8,128)(2,1)S(1)}, bf16[2048,64]{0,1:T(8,128)(2,1)}, u32[]{:S(2)}) copy-start(bf16[2048,64]{0,1:T(8,128)(2,1)} %param.19) | copy-start | bytes 786436
  70.1 32.7 %copy-start.8 = (s32[1,32,2]{1,2,0:T(2,128)S(1)}, s32[1,32,2]{1,2,0:T(2,128)}, u32[]{:S(2)}) copy-start(s32[1,32,2]{1,2,0:T(2,128)} %param.20) | copy-start | bytes 772
  79.6 21.9 %all-to-all-start.4 = ((bf16[64,16,256]{2,1,0:T(8,128)(2,1)}), bf16[64,16,256]{2,1,0:T(8,128)(2,1)S(1)}, u32[]{:S(2)}, u32[]{:S(2)}) async-start(bf16[64,16,256]{2,1,0:T(8,128)(2,1)} %get-tuple-element.20), calls=%async_computation.4 | async-start | bytes 1048576 | tf_op jit(solution)/shard_map/all_to_all | solution.py:298
  84.2 30.6 %copy-start.4 = (bf16[1,32,2048]{2,1,0:T(8,128)(2,1)S(1)}, bf16[1,32,2048]{2,1,0:T(8,128)(2,1)}, u32[]{:S(2)}) copy-start(bf16[1,32,2048]{2,1,0:T(8,128)(2,1)} %param.12) | copy-start | bytes 393220
  84.2 73.1 %all-gather.6.cloned.1.call-start = ((), (), s32[]{:S(2)}) async-start(), calls=%async_computation.8 | async-start | bytes 4718592 | tf_op jit(solution)/shard_map/all_gather | solution.py:340
  102.8 11.9 %all-to-all-start.3 = ((bf16[8,32,256]{2,1,0:T(8,128)(2,1)}), bf16[8,32,256]{2,1,0:T(8,128)(2,1)S(1)}, u32[]{:S(2)}, u32[]{:S(2)}) async-start(bf16[8,32,256]{2,1,0:T(8,128)(2,1)} %get-tuple-element.15), calls=%async_computation.3 | async-start | bytes 262144 | tf_op jit(solution)/shard_map/all_to_all | solution.py:298
  114.8 2.6 %copy-start.1 = (bf16[8,176,2048]{2,1,0:T(8,128)(2,1)S(1)}, bf16[8,176,2048]{2,1,0:T(8,128)(2,1)}, u32[]{:S(2)}) copy-start(bf16[8,176,2048]{2,1,0:T(8,128)(2,1)} %all-gather.4.cloned.1.call-done.down_hbm) | copy-start | bytes 17301508
  118.2 2.5 %copy-start.2 = (bf16[8,176,2048]{2,1,0:T(8,128)(2,1)}, bf16[8,176,2048]{2,1,0:T(8,128)(2,1)S(1)}, u32[]{:S(2)}) copy-start(bf16[8,176,2048]{2,1,0:T(8,128)(2,1)S(1)} %get-tuple-element.21.down_ref) | copy-start | bytes 17301508
  157.3 22.1 %copy-start.3 = (bf16[8,176,2048]{2,1,0:T(8,128)(2,1)S(1)}, bf16[8,176,2048]{2,1,0:T(8,128)(2,1)}, u32[]{:S(2)}) copy-start(bf16[8,176,2048]{2,1,0:T(8,128)(2,1)} %copy-done.2) | copy-start | bytes 17301508
Sparse Core Ops, SparseCore 0:
  10.1 78.3 all-gather.3
  102.6 54.6 all-gather.5

commit v6 on v5

--- a/solution.py
+++ b/solution.py
@@ -234,7 +234,7 @@
 
 
 def expert_call(rows, inverse, weight, after):
-    step = 2
+    step = 4
     width = weight.shape[0] // 2
     whole = pl.BlockSpec(memory_space=pltpu.VMEM)
     return pl.pallas_call(

time: 219 us -> 218 us (level)
  no operation moved by 1% of the time
where the time goes in v6:
time: 218 us; the launch traced here: 217 us
  waiting for transfers between devices  82.1 us (38%)
  blocking collectives  57.2 us (26%)
  starting transfers between devices  39.8 us (18%)
  between operations  14.9 us (7%)
  Pallas kernels  13.8 us (6%)
  local copies, waits for them, and re-layouts  7.28 us (3%)
  other arithmetic  2.28 us (1%)
    all_to_all x3, blocking collectives, shards(): lax.all_to_all(a, axes, split_axis=0, concat_axis=0, tiled=True)  57.2 us
    all_to_all x4, waiting for transfers between devices, shards(): lax.all_to_all(a, axes, split_axis=0, concat_axis=0, tiled=True)  37.2 us
    all_gather x1, waiting for transfers between devices, shards(): rows = lax.all_gather(arrived, 'y', axis=0)  36.6 us
    all_to_all x4, starting transfers between devices, shards(): lax.all_to_all(a, axes, split_axis=0, concat_axis=0, tiled=True)  25.4 us
    unnamed x19, local copies, waits for them, and re-layouts  5.44 us
    ppermute x1, starting transfers between devices, shards(): other_kv = lax.ppermute(kv, 'c', other_core)  5.35 us
  transfers between devices with their start and end apart: 11, of which 9 were waited for; matrix products, arithmetic and copies ran while one was open for 1% of the time, Pallas kernels for 3%

profile of v6, /device:TPU:1, one launch (start us, length us, event | category | flops | bytes accessed | tf_op | source)
XLA Modules:
  0.0 217.5 jit_solution(8473075203894111982)
XLA Ops:
  7.2 0.0 copy-start
  7.2 0.0 all-gather.4.cloned.1.call-start
  7.2 0.7 all-gather.4.cloned.1.call-update
  7.9 2.6 %shard_map.131 = (bf16[8,176,128]{2,1,0:T(8,128)(2,1)}, s32[16,16]{1,0:T(8,128)}) custom-call(s32[16,16]{1,0:T(8,128)} %bitcast.32, bf16[32,1024]{1,0:T(8,128)(2,1)} %bitcast.29, bf16[32,1024]{1,0:T(8,128)(2,1)} %bitcast.30, bf16[32,1024]{1,0:T(8,128)(2,1)} %bitcast.31, bf16[32,2048]{1,0:T(8,128)(2,1)} %bitcast.22, s32[2,32]{1,0:T(2,128)} %bitcast.33), custom_call_target="tpu_custom_call" | custom-call | tf_op jit(solution)/shard_map/pallas_call | solution.py:308
  10.5 0.0 copy-start.6
  10.5 0.0 copy-start.5
  10.5 10.9 %all-to-all-start = ((bf16[8,176,128]{2,1,0:T(8,128)(2,1)}), bf16[8,176,128]{2,1,0:T(8,128)(2,1)S(1)}, u32[]{:S(2)}, u32[]{:S(2)}) async-start(bf16[8,176,128]{2,1,0:T(8,128)(2,1)} %get-tuple-element.13), calls=%async_computation | async-start | bytes 720896 | tf_op jit(solution)/shard_map/all_to_all | solution.py:298
  21.4 0.7 collective-permute-start
  22.1 12.2 %all-to-all-done.packed_ref = bf16[8,176,128]{2,1,0:T(8,128)(2,1)S(1)} async-done(((bf16[8,176,128]{2,1,0:T(8,128)(2,1)}), bf16[8,176,128]{2,1,0:T(8,128)(2,1)S(1)}, u32[]{:S(2)}, u32[]{:S(2)}) %all-to-all-start) | async-done | bytes 360480 | tf_op jit(solution)/shard_map/all_to_all | solution.py:298
  34.3 0.1 shard_map.132
  34.4 10.8 %all_to_all.35 = bf16[4,8,64,128]{3,2,1,0:T(8,128)(2,1)S(1)} all-to-all(bf16[4,8,64,128]{3,2,1,0:T(8,128)(2,1)S(1)} %shard_map.132), channel_id=1, replica_groups=mesh['x'=4,'z'=8,'c'=2,'y'=8] {'x'}, dimensions={0} | all-to-all | bytes 1048576 | tf_op jit(solution)/shard_map/all_to_all | solution.py:298
  45.2 5.3 %collective-permute-start.1 = (bf16[32,64,128]{2,1,0:T(8,128)(2,1)S(1)}, bf16[32,64,128]{2,1,0:T(8,128)(2,1)S(1)}, u32[]{:S(2)}, u32[]{:S(2)}) collective-permute-start(bf16[32,64,128]{2,1,0:T(8,128)(2,1)S(1)} %bitcast.20), channel_id=1, source_target_pairs={{0,8},{8,0},{1,9},{9,1},{2,10},{10,2},{3,11},{11,3},{4,12},{12,4},... | collective-permute-start | bytes 1572872 | tf_op jit(solution)/shard_map/ppermute | solution.py:325
  50.5 1.5 collective-permute-done.1.other_ref
  52.0 2.2 shard_map.133
  54.2 5.8 %all-to-all-start.2 = ((bf16[8,256,128]{2,1,0:T(8,128)(2,1)}), bf16[8,256,128]{2,1,0:T(8,128)(2,1)S(1)}, u32[]{:S(2)}, u32[]{:S(2)}) async-start(bf16[8,256,128]{2,1,0:T(8,128)(2,1)} %shard_map.133), calls=%async_computation.2 | async-start | bytes 1048576 | tf_op jit(solution)/shard_map/all_to_all | solution.py:298
  60.1 2.2 %collective-permute-start.3 = (bf16[256,256]{1,0:T(8,128)(2,1)S(1)}, bf16[256,256]{1,0:T(8,128)(2,1)S(1)}, u32[]{:S(2)}, u32[]{:S(2)}) collective-permute-start(bf16[256,256]{1,0:T(8,128)(2,1)S(1)} %collective-permute-done._.own_ref), channel_id=1, source_target_pairs={{0,128},{128,0},{256,384},{384,256},{1,129},{129,1},{257,385},{385... | collective-permute-start | bytes 393224 | tf_op jit(solution)/shard_map/ppermute | solution.py:327
  62.3 2.8 %collective-permute-start.2 = (bf16[256,256]{1,0:T(8,128)(2,1)S(1)}, bf16[256,256]{1,0:T(8,128)(2,1)S(1)}, u32[]{:S(2)}, u32[]{:S(2)}) collective-permute-start(bf16[256,256]{1,0:T(8,128)(2,1)S(1)} %collective-permute-done._.own_ref), channel_id=1, source_target_pairs={{0,8},{8,0},{1,9},{9,1},{2,10},{10,2},{3,11},{11,3},{4,12},{12,4},... | collective-permute-start | bytes 393224 | tf_op jit(solution)/shard_map/ppermute | solution.py:329
  65.1 1.3 collective-permute-done.3.x_ref
  66.4 3.3 %collective-permute-start.4 = (bf16[256,256]{1,0:T(8,128)(2,1)S(1)}, bf16[256,256]{1,0:T(8,128)(2,1)S(1)}, u32[]{:S(2)}, u32[]{:S(2)}) collective-permute-start(bf16[256,256]{1,0:T(8,128)(2,1)S(1)} %collective-permute-done.3.x_ref), channel_id=1, source_target_pairs={{0,8},{8,0},{1,9},{9,1},{2,10},{10,2},{3,11},{11,3},{4,12},{12,4},... | collective-permute-start | bytes 393224 | tf_op jit(solution)/shard_map/ppermute | solution.py:329
  69.8 0.3 shard_map.134.route_ref
  70.1 0.0 copy-start.7
  70.1 0.6 collective-permute-done.4.x_core_ref
  70.7 7.3 %all-to-all-done.2.att_ref = bf16[8,256,128]{2,1,0:T(8,128)(2,1)S(1)} async-done(((bf16[8,256,128]{2,1,0:T(8,128)(2,1)}), bf16[8,256,128]{2,1,0:T(8,128)(2,1)S(1)}, u32[]{:S(2)}, u32[]{:S(2)}) %all-to-all-start.2) | async-done | bytes 524320 | tf_op jit(solution)/shard_map/all_to_all | solution.py:298
  78.0 1.6 shard_map.135
  79.6 4.6 %all-to-all-start.4 = ((bf16[64,16,256]{2,1,0:T(8,128)(2,1)}), bf16[64,16,256]{2,1,0:T(8,128)(2,1)S(1)}, u32[]{:S(2)}, u32[]{:S(2)}) async-start(bf16[64,16,256]{2,1,0:T(8,128)(2,1)} %get-tuple-element.20), calls=%async_computation.4 | async-start | bytes 1048576 | tf_op jit(solution)/shard_map/all_to_all | solution.py:298
  84.2 0.0 copy-start.4
  84.2 0.0 all-gather.6.cloned.1.call-start
  84.3 4.2 %all-gather.4.cloned.1.call-done.down_hbm = bf16[8,176,2048]{2,1,0:T(8,128)(2,1)} async-done(((bf16[1,176,2048]{2,1,0:T(8,128)(2,1)}), bf16[8,176,2048]{2,1,0:T(8,128)(2,1)}) %all-gather.4.cloned.1.call-update) | async-done | bytes 5767184 | tf_op jit(solution)/shard_map/all_gather | solution.py:300
  88.5 1.2 slice.4
  90.3 11.2 %all-to-all-done.4 = bf16[64,16,256]{2,1,0:T(8,128)(2,1)S(1)} async-done(((bf16[64,16,256]{2,1,0:T(8,128)(2,1)}), bf16[64,16,256]{2,1,0:T(8,128)(2,1)S(1)}, u32[]{:S(2)}, u32[]{:S(2)}) %all-to-all-start.4) | async-done | bytes 524320 | tf_op jit(solution)/shard_map/all_to_all | solution.py:298
  101.6 0.9 broadcast_add_fusion
  102.4 0.0 all-gather.6.cloned.1.call-update
  102.5 0.3 copy.16.router_ref
  102.7 0.1 copy.17.ids_ref
  102.8 4.1 %all-to-all-start.3 = ((bf16[8,32,256]{2,1,0:T(8,128)(2,1)}), bf16[8,32,256]{2,1,0:T(8,128)(2,1)S(1)}, u32[]{:S(2)}, u32[]{:S(2)}) async-start(bf16[8,32,256]{2,1,0:T(8,128)(2,1)} %get-tuple-element.15), calls=%async_computation.3 | async-start | bytes 262144 | tf_op jit(solution)/shard_map/all_to_all | solution.py:298
  106.9 1.4 pad_maximum_fusion.weight_ref
  108.4 6.4 %all-to-all-done.3.projected_ref = bf16[8,32,256]{2,1,0:T(8,128)(2,1)S(1)} async-done(((bf16[8,32,256]{2,1,0:T(8,128)(2,1)}), bf16[8,32,256]{2,1,0:T(8,128)(2,1)S(1)}, u32[]{:S(2)}, u32[]{:S(2)}) %all-to-all-start.3) | async-done | bytes 131104 | tf_op jit(solution)/shard_map/all_to_all | solution.py:298
  114.8 2.6 %copy-done.1 = bf16[8,176,2048]{2,1,0:T(8,128)(2,1)S(1)} copy-done((bf16[8,176,2048]{2,1,0:T(8,128)(2,1)S(1)}, bf16[8,176,2048]{2,1,0:T(8,128)(2,1)}, u32[]{:S(2)}) %copy-start.1) | copy-done | bytes 5767192
  117.4 0.8 shard_map.136
  118.2 2.5 %copy-done.2 = bf16[8,176,2048]{2,1,0:T(8,128)(2,1)} copy-done((bf16[8,176,2048]{2,1,0:T(8,128)(2,1)}, bf16[8,176,2048]{2,1,0:T(8,128)(2,1)S(1)}, u32[]{:S(2)}) %copy-start.2) | copy-done | bytes 5767192
  120.7 36.6 %all-gather.6.cloned.1.call-done = bf16[512,16,256]{2,1,0:T(8,128)(2,1)} async-done(((bf16[64,16,256]{2,1,0:T(8,128)(2,1)}), bf16[512,16,256]{2,1,0:T(8,128)(2,1)}) %all-gather.6.cloned.1.call-update) | async-done | bytes 4194320 | tf_op jit(solution)/shard_map/all_gather | solution.py:340
  157.3 4.3 %shard_map.137 = bf16[8,176,128]{2,1,0:T(8,128)(2,1)S(1)} custom-call(bf16[8,4,8,2,16,256]{5,4,3,2,1,0:T(8,128)(2,1)} %bitcast.25, f32[8,256]{1,0:T(8,128)S(1)} %reshape.27.inverse_ref, bf16[352,2048]{1,0:T(8,128)(2,1)S(1)} %pad_maximum_fusion.weight_ref, f32[32,2]{1,0:T(8,128)S(1)} %get-tuple-element.17._.gates_ref), custom_call_target="tpu_custom_call" | custom-call | tf_op jit(solution)/shard_map/pallas_call | solution.py:240
  161.6 16.9 %all_to_all.36.active_ref = bf16[8,176,128]{2,1,0:T(8,128)(2,1)S(1)} all-to-all(bf16[8,176,128]{2,1,0:T(8,128)(2,1)S(1)} %shard_map.137), channel_id=1, replica_groups=mesh['x'=4,'z'=8,'c'=2,'y'=8] {'y'}, dimensions={0} | all-to-all | bytes 720896 | tf_op jit(solution)/shard_map/all_to_all | solution.py:298
  178.5 1.1 shard_map.138
  179.7 0.3 reshape.28
  180.0 29.5 %all_to_all.37 = bf16[64,2,2048]{2,1,0:T(2,128)(2,1)S(1)} all-to-all(bf16[64,2,2048]{2,1,0:T(2,128)(2,1)S(1)} %reshape.28), channel_id=1, replica_groups=mesh['x'=4,'z'=8,'c'=2,'y'=8] {'x','z','c'}, dimensions={0} | all-to-all | bytes 1048576 | tf_op jit(solution)/shard_map/all_to_all | solution.py:298
  209.5 0.2 reshape.29.rows_ref
  209.7 0.9 shard_map.139
  (17 shorter events, 0.1 us)
Async XLA Ops:
  7.2 14.2 %copy-start = (bf16[1024,256]{1,0:T(8,128)(2,1)S(1)}, bf16[1024,256]{1,0:T(8,128)(2,1)}, u32[]{:S(2)}) copy-start(bf16[1024,256]{1,0:T(8,128)(2,1)} %param.17) | copy-start | bytes 1572868
  7.2 81.3 %all-gather.4.cloned.1.call-start = ((), (), s32[]{:S(2)}) async-start(), calls=%async_computation.7 | async-start | bytes 6488064 | tf_op jit(solution)/shard_map/all_gather | solution.py:300
  10.5 41.6 %copy-start.6 = (s32[16,16]{1,0:T(8,128)S(1)}, s32[16,16]{1,0:T(8,128)}, u32[]{:S(2)}) copy-start(s32[16,16]{1,0:T(8,128)} %get-tuple-element.12.mask_ref) | copy-start | bytes 3076
  10.5 51.8 %copy-start.5 = (f32[2048]{0:T(1024)S(1)}, f32[2048]{0:T(1024)}, u32[]{:S(2)}) copy-start(f32[2048]{0:T(1024)} %param.18) | copy-start | bytes 24580
  10.5 23.8 %all-to-all-start = ((bf16[8,176,128]{2,1,0:T(8,128)(2,1)}), bf16[8,176,128]{2,1,0:T(8,128)(2,1)S(1)}, u32[]{:S(2)}, u32[]{:S(2)}) async-start(bf16[8,176,128]{2,1,0:T(8,128)(2,1)} %get-tuple-element.13), calls=%async_computation | async-start | bytes 720896 | tf_op jit(solution)/shard_map/all_to_all | solution.py:298
  21.4 0.7 collective-permute-start
  45.2 6.9 %collective-permute-start.1 = (bf16[32,64,128]{2,1,0:T(8,128)(2,1)S(1)}, bf16[32,64,128]{2,1,0:T(8,128)(2,1)S(1)}, u32[]{:S(2)}, u32[]{:S(2)}) collective-permute-start(bf16[32,64,128]{2,1,0:T(8,128)(2,1)S(1)} %bitcast.20), channel_id=1, source_target_pairs={{0,8},{8,0},{1,9},{9,1},{2,10},{10,2},{3,11},{11,3},{4,12},{12,4},... | collective-permute-start | bytes 1572872 | tf_op jit(solution)/shard_map/ppermute | solution.py:325
  54.2 23.8 %all-to-all-start.2 = ((bf16[8,256,128]{2,1,0:T(8,128)(2,1)}), bf16[8,256,128]{2,1,0:T(8,128)(2,1)S(1)}, u32[]{:S(2)}, u32[]{:S(2)}) async-start(bf16[8,256,128]{2,1,0:T(8,128)(2,1)} %shard_map.133), calls=%async_computation.2 | async-start | bytes 1048576 | tf_op jit(solution)/shard_map/all_to_all | solution.py:298
  60.1 6.4 %collective-permute-start.3 = (bf16[256,256]{1,0:T(8,128)(2,1)S(1)}, bf16[256,256]{1,0:T(8,128)(2,1)S(1)}, u32[]{:S(2)}, u32[]{:S(2)}) collective-permute-start(bf16[256,256]{1,0:T(8,128)(2,1)S(1)} %collective-permute-done._.own_ref), channel_id=1, source_target_pairs={{0,128},{128,0},{256,384},{384,256},{1,129},{129,1},{257,385},{385... | collective-permute-start | bytes 393224 | tf_op jit(solution)/shard_map/ppermute | solution.py:327
  62.3 7.8 %collective-permute-start.2 = (bf16[256,256]{1,0:T(8,128)(2,1)S(1)}, bf16[256,256]{1,0:T(8,128)(2,1)S(1)}, u32[]{:S(2)}, u32[]{:S(2)}) collective-permute-start(bf16[256,256]{1,0:T(8,128)(2,1)S(1)} %collective-permute-done._.own_ref), channel_id=1, source_target_pairs={{0,8},{8,0},{1,9},{9,1},{2,10},{10,2},{3,11},{11,3},{4,12},{12,4},... | collective-permute-start | bytes 393224 | tf_op jit(solution)/shard_map/ppermute | solution.py:329
  66.4 4.3 %collective-permute-start.4 = (bf16[256,256]{1,0:T(8,128)(2,1)S(1)}, bf16[256,256]{1,0:T(8,128)(2,1)S(1)}, u32[]{:S(2)}, u32[]{:S(2)}) collective-permute-start(bf16[256,256]{1,0:T(8,128)(2,1)S(1)} %collective-permute-done.3.x_ref), channel_id=1, source_target_pairs={{0,8},{8,0},{1,9},{9,1},{2,10},{10,2},{3,11},{11,3},{4,12},{12,4},... | collective-permute-start | bytes 393224 | tf_op jit(solution)/shard_map/ppermute | solution.py:329
  70.1 32.4 %copy-start.7 = (bf16[2048,64]{0,1:T(8,128)(2,1)S(1)}, bf16[2048,64]{0,1:T(8,128)(2,1)}, u32[]{:S(2)}) copy-start(bf16[2048,64]{0,1:T(8,128)(2,1)} %param.19) | copy-start | bytes 786436
  70.1 32.7 %copy-start.8 = (s32[1,32,2]{1,2,0:T(2,128)S(1)}, s32[1,32,2]{1,2,0:T(2,128)}, u32[]{:S(2)}) copy-start(s32[1,32,2]{1,2,0:T(2,128)} %param.20) | copy-start | bytes 772
  79.6 21.9 %all-to-all-start.4 = ((bf16[64,16,256]{2,1,0:T(8,128)(2,1)}), bf16[64,16,256]{2,1,0:T(8,128)(2,1)S(1)}, u32[]{:S(2)}, u32[]{:S(2)}) async-start(bf16[64,16,256]{2,1,0:T(8,128)(2,1)} %get-tuple-element.20), calls=%async_computation.4 | async-start | bytes 1048576 | tf_op jit(solution)/shard_map/all_to_all | solution.py:298
  84.2 30.6 %copy-start.4 = (bf16[1,32,2048]{2,1,0:T(8,128)(2,1)S(1)}, bf16[1,32,2048]{2,1,0:T(8,128)(2,1)}, u32[]{:S(2)}) copy-start(bf16[1,32,2048]{2,1,0:T(8,128)(2,1)} %param.12) | copy-start | bytes 393220
  84.2 73.1 %all-gather.6.cloned.1.call-start = ((), (), s32[]{:S(2)}) async-start(), calls=%async_computation.8 | async-start | bytes 4718592 | tf_op jit(solution)/shard_map/all_gather | solution.py:340
  102.8 11.9 %all-to-all-start.3 = ((bf16[8,32,256]{2,1,0:T(8,128)(2,1)}), bf16[8,32,256]{2,1,0:T(8,128)(2,1)S(1)}, u32[]{:S(2)}, u32[]{:S(2)}) async-start(bf16[8,32,256]{2,1,0:T(8,128)(2,1)} %get-tuple-element.15), calls=%async_computation.3 | async-start | bytes 262144 | tf_op jit(solution)/shard_map/all_to_all | solution.py:298
  114.8 2.6 %copy-start.1 = (bf16[8,176,2048]{2,1,0:T(8,128)(2,1)S(1)}, bf16[8,176,2048]{2,1,0:T(8,128)(2,1)}, u32[]{:S(2)}) copy-start(bf16[8,176,2048]{2,1,0:T(8,128)(2,1)} %all-gather.4.cloned.1.call-done.down_hbm) | copy-start | bytes 17301508
  118.2 2.5 %copy-start.2 = (bf16[8,176,2048]{2,1,0:T(8,128)(2,1)}, bf16[8,176,2048]{2,1,0:T(8,128)(2,1)S(1)}, u32[]{:S(2)}) copy-start(bf16[8,176,2048]{2,1,0:T(8,128)(2,1)S(1)} %get-tuple-element.21.down_ref) | copy-start | bytes 17301508
  157.3 21.2 %copy-start.3 = (bf16[8,176,2048]{2,1,0:T(8,128)(2,1)S(1)}, bf16[8,176,2048]{2,1,0:T(8,128)(2,1)}, u32[]{:S(2)}) copy-start(bf16[8,176,2048]{2,1,0:T(8,128)(2,1)} %copy-done.2) | copy-start | bytes 17301508
Sparse Core Ops, SparseCore 0:
  10.1 78.3 all-gather.3
  102.6 54.6 all-gather.5
